TPU v7x, 1024 devices: a whole 4x8x16 slice. The times are simulated.
1024 devices in a mesh: dp: 16 (over y, core), table: 64 (over x, z).
Axes of the slice: x: 4, y: 8, z: 16, core: 2. Of those that a mesh axis runs over, the one named last changes fastest.
Arguments:
- table: float32 [131072, 256], P(('dp', 'table')), may hold values from -6 to 6
- accum: float32 [131072], P(('dp', 'table')), may hold values from 0.05 to 2
- item_weight: bfloat16 [256, 256], replicated, may hold values from -0.375 to 0.375
- query_weight: bfloat16 [256, 256], replicated, may hold values from -0.375 to 0.375
- packed_rows: int32 [16, 64, 1536], P('dp', 'table'), may hold values from 0 to 127
- block_counts: int32 [16, 64, 1024], P('dp', 'table'), may hold values from 1 to 2, 1536 in all within a row
- item_refs: int32 [16, 64, 128, 4], P('dp', 'table'), may hold values from 0 to 1535
- query_refs: int32 [16, 64, 128, 4], P('dp', 'table'), may hold values from 0 to 1535
Outputs:
- new_table: float32 [131072, 256], P(('dp', 'table'))
- new_accum: float32 [131072], P(('dp', 'table'))
- pair_loss: float32 [16, 64, 128], P('dp', 'table')
Inputs may be any that keep to these rules, and one draw needn't show every extreme that they name: `block_counts`: each device's 1024 counts sum to 1536, every count is at least 1, and in every device's list some owner gets exactly 2 entries. `packed_rows`: a row number within the shard of the owner that its position belongs to; rows may repeat. `item_refs`: positions in the same device's packed list; they repeat. `query_refs`: positions in the same device's packed list; they repeat.
All inputs are finite; a program needn't handle non-finite values.
Results may differ from a plain program's by a relative error of at most 0.0026.
Values may be sent and summed in bfloat16 or wider, within the bound.
No kernel may reach another device: no remote copies, remote signals or barrier semaphores. Data moves between devices by JAX's collectives and lax.ppermute only.
A program may use at most 32 MiB of HBM per device.

v0:
```python
import jax
import jax.numpy as jnp
from jax import lax
from jax.sharding import PartitionSpec as P

CAP = 2


learn_rate = 0.3
epsilon = 1e-06
sharpness = 3.0


def project(pooled, weight):
    hidden = jnp.dot(pooled, weight, preferred_element_type=jnp.float32)
    factor = lax.rsqrt(jnp.mean(hidden * hidden, axis=1, keepdims=True) + epsilon)
    return (hidden * factor, factor)


def project_back(grad_out, normed, factor, weight):
    inner_mean = jnp.mean(grad_out * normed, axis=1, keepdims=True)
    grad_hidden = (factor * (grad_out - normed * inner_mean)).astype(jnp.bfloat16)
    return lax.dot_general(
        grad_hidden, weight, (((1,), (1,)), ((), ())), preferred_element_type=jnp.float32
    )


def slot_table(rows_list, counts, capacity):
    block_ends = jnp.cumsum(counts)
    block_starts = block_ends - counts
    positions = jnp.arange(rows_list.shape[0], dtype=jnp.int32)
    owners = jnp.searchsorted(block_ends, positions, side="right")
    starts = jnp.take(block_starts, owners)
    return owners * capacity + positions - starts


def slot_counts(slot_ids, slot_total):
    slot_range = jnp.arange(slot_total, dtype=jnp.int32)
    matches = (slot_range[:, None, None] == slot_ids[None, :, :]).astype(jnp.float32)
    return jnp.sum(matches, axis=2)


def adagrad(old_rows, old_state, row_grads):
    new_state = old_state + jnp.mean(row_grads * row_grads, axis=1)
    return (old_rows - learn_rate * row_grads / jnp.sqrt(new_state)[:, None], new_state)


def on_device(
    table, accum, item_weight, query_weight, packed_rows, block_counts, item_refs, query_refs
):
    rows_list = packed_rows[0, 0]
    counts = block_counts[0, 0]
    replica_count = lax.axis_size("dp")
    group_count = lax.axis_size("table")
    feature_width = table.shape[1]
    pair_count = item_refs.shape[2]
    score_scale = sharpness * feature_width ** (-0.5)
    block_starts = jnp.cumsum(counts) - counts
    offsets = jnp.arange(CAP, dtype=jnp.int32)
    positions = jnp.minimum(block_starts[:, None] + offsets[None, :], rows_list.shape[0] - 1)
    requests = jnp.where(offsets[None, :] < counts[:, None], jnp.take(rows_list, positions), 0)
    requests = requests.reshape(replica_count, group_count, CAP)
    received = lax.all_to_all(
        lax.all_to_all(requests, "dp", split_axis=0, concat_axis=0, tiled=True),
        "table",
        split_axis=1,
        concat_axis=1,
        tiled=True,
    )
    shard_bf = table.astype(jnp.bfloat16)
    picked = jnp.take(shard_bf, received.reshape(-1), axis=0).reshape(
        replica_count, group_count, CAP, feature_width
    )
    fetched = lax.all_to_all(
        lax.all_to_all(picked, "dp", split_axis=0, concat_axis=0, tiled=True),
        "table",
        split_axis=1,
        concat_axis=1,
        tiled=True,
    )
    fetched_rows = fetched.reshape(-1, feature_width)
    slot_total = fetched_rows.shape[0]
    slots = slot_table(rows_list, counts, CAP)
    item_slots = jnp.take(slots, item_refs[0, 0])
    query_slots = jnp.take(slots, query_refs[0, 0])
    item_pool = jnp.sum(fetched_rows[item_slots].astype(jnp.float32), axis=1).astype(jnp.bfloat16)
    query_pool = jnp.sum(fetched_rows[query_slots].astype(jnp.float32), axis=1).astype(jnp.bfloat16)
    item_normed, item_factor = project(item_pool, item_weight)
    query_normed, query_factor = project(query_pool, query_weight)
    item_out = item_normed.astype(jnp.bfloat16)
    query_out = query_normed.astype(jnp.bfloat16)
    all_items = lax.all_gather(item_out, "dp", axis=0, tiled=True)
    scores = (
        lax.dot_general(
            query_out, all_items, (((1,), (1,)), ((), ())), preferred_element_type=jnp.float32
        )
        * score_scale
    )
    totals = jnp.log(jnp.sum(jnp.exp(scores), axis=1))
    own_index = lax.axis_index("dp") * pair_count + jnp.arange(pair_count, dtype=jnp.int32)
    columns = jnp.arange(scores.shape[1], dtype=jnp.int32)
    own_hits = columns[None, :] == own_index[:, None]
    pair_loss = totals - jnp.sum(jnp.where(own_hits, scores, 0.0), axis=1)
    grad_scores = (jnp.exp(scores - totals[:, None]) - jnp.where(own_hits, 1.0, 0.0)).astype(
        jnp.bfloat16
    )
    grad_query = jnp.dot(grad_scores, all_items, preferred_element_type=jnp.float32) * score_scale
    grad_item = lax.psum_scatter(
        lax.dot_general(
            grad_scores, query_out, (((0,), (0,)), ((), ())), preferred_element_type=jnp.float32
        )
        * score_scale,
        "dp",
        scatter_dimension=0,
        tiled=True,
    )
    item_back = project_back(grad_item, item_normed, item_factor, item_weight)
    query_back = project_back(grad_query, query_normed, query_factor, query_weight)
    pair_weights = jnp.concatenate(
        [slot_counts(item_slots, slot_total), slot_counts(query_slots, slot_total)], axis=1
    )
    pair_backs = jnp.concatenate([item_back, query_back], axis=0)
    slot_grads = jnp.dot(
        pair_weights,
        pair_backs,
        precision=lax.Precision.HIGHEST,
        preferred_element_type=jnp.float32,
    )
    outgoing = slot_grads.reshape(replica_count, group_count, CAP, feature_width)
    returned = lax.all_to_all(
        lax.all_to_all(
            outgoing.astype(jnp.bfloat16), "dp", split_axis=0, concat_axis=0, tiled=True
        ),
        "table",
        split_axis=1,
        concat_axis=1,
        tiled=True,
    ).astype(outgoing.dtype)
    shard_range = jnp.arange(table.shape[0], dtype=jnp.int32)
    owner_hits = (shard_range[:, None] == received.reshape(-1)[None, :]).astype(jnp.float32)
    shard_grad = jnp.dot(
        owner_hits,
        returned.reshape(-1, feature_width),
        precision=lax.Precision.HIGHEST,
        preferred_element_type=jnp.float32,
    )
    new_table, new_accum = adagrad(table, accum, shard_grad)
    return (new_table, new_accum, pair_loss[None, None, :])


def solution(mesh):
    in_specs = (
        P(("dp", "table"), None),
        P(("dp", "table")),
        P(),
        P(),
        P("dp", "table", None),
        P("dp", "table", None),
        P("dp", "table", None, None),
        P("dp", "table", None, None),
    )
    out_specs = (P(("dp", "table"), None), P(("dp", "table")), P("dp", "table", None))
    return jax.shard_map(
        on_device, mesh=mesh, in_specs=in_specs, out_specs=out_specs, check_vma=False
    )
```

profile of v0, /device:TPU:1, one launch (start us, length us, event | category | flops | bytes accessed | tf_op | source)
XLA Modules:
  0.0 450.6 jit_solution(15495837189153253830)
XLA Ops:
  14.9 11.8 %gather_fusion.1 = s32[2048]{0:T(1024)S(1)} fusion(s32[1536]{0:T(1024)S(1)} %reduce.6, s32[2048]{0:T(1024)S(1)} %broadcast_clamp_fusion.1), kind=kCustom, calls=%fused_computation.3 | custom fusion | bytes 24576 | tf_op jit(solution)/shard_map/jit(_take)/gather | solution.py:61
  27.6 23.6 %all_to_all.30 = s32[16,1,128]{2,1,0:T(1,128)S(1)} all-to-all(s32[16,1,128]{2,1,0:T(1,128)S(1)} %reshape.334), channel_id=1, replica_groups=mesh['dp'=16,'table'=64] {'dp'}, dimensions={0} | all-to-all | bytes 16384 | tf_op jit(solution)/shard_map/all_to_all | solution.py:64
  53.1 13.8 %all-to-all-start.1 = ((s32[16,64,2]{0,2,1:T(2,128)}), s32[16,64,2]{0,2,1:T(2,128)S(1)}, u32[]{:S(2)}, u32[]{:S(2)}) async-start(s32[16,64,2]{0,2,1:T(2,128)} %copy.72), calls=%async_computation.1 | async-start | bytes 131072 | tf_op jit(solution)/shard_map/all_to_all | solution.py:63
  66.9 13.5 %all-to-all-done.1 = s32[16,64,2]{0,2,1:T(2,128)S(1)} async-done(((s32[16,64,2]{0,2,1:T(2,128)}), s32[16,64,2]{0,2,1:T(2,128)S(1)}, u32[]{:S(2)}, u32[]{:S(2)}) %all-to-all-start.1) | async-done | bytes 8224 | tf_op jit(solution)/shard_map/all_to_all | solution.py:63
  81.8 7.5 %gather_fusion.3 = bf16[2048,256]{1,0:T(8,128)(2,1)S(1)} fusion(bf16[128,256]{1,0:T(8,128)(2,1)S(1)} %convert_element_type.49, s32[2048]{0:T(1024)S(1)} %broadcast_clamp_fusion), kind=kCustom, calls=%fused_computation.5 | custom fusion | bytes 2105344 | tf_op jit(solution)/shard_map/jit(_take)/gather | solution.py:71
  89.8 2.7 broadcast_select_fusion
  92.4 5.5 %all-to-all-start.2 = ((bf16[16,64,2,256]{3,2,1,0:T(2,128)(2,1)}), bf16[16,64,2,256]{3,2,1,0:T(2,128)(2,1)S(1)}, u32[]{:S(2)}, u32[]{:S(2)}) async-start(bf16[16,64,2,256]{3,2,1,0:T(2,128)(2,1)} %broadcast_select_fusion), calls=%async_computation.2 | async-start | bytes 2097152 | tf_op jit(solution)/shard_map/all_to_all | solution.py:75
  98.0 28.0 %all-to-all-done.2 = bf16[16,64,2,256]{3,2,1,0:T(2,128)(2,1)S(1)} async-done(((bf16[16,64,2,256]{3,2,1,0:T(2,128)(2,1)}), bf16[16,64,2,256]{3,2,1,0:T(2,128)(2,1)S(1)}, u32[]{:S(2)}, u32[]{:S(2)}) %all-to-all-start.2) | async-done | bytes 1048608 | tf_op jit(solution)/shard_map/all_to_all | solution.py:75
  128.1 4.7 %all-to-all-start.3 = ((bf16[16,64,2,256]{3,2,0,1:T(2,128)(2,1)}), bf16[16,64,2,256]{3,2,0,1:T(2,128)(2,1)S(1)}, u32[]{:S(2)}, u32[]{:S(2)}) async-start(bf16[16,64,2,256]{3,2,0,1:T(2,128)(2,1)} %copy.83), calls=%async_computation.3 | async-start | bytes 2097152 | tf_op jit(solution)/shard_map/all_to_all | solution.py:74
  132.8 65.4 %while.24 = (s32[]{:T(128)}, u32[1536]{0:T(1024)S(1)}, u32[1536]{0:T(1024)S(1)}, s32[1024]{0:T(1024)S(1)}, s32[]{:T(128)}, /*index=5*/s32[]{:T(128)}, s32[]{}) while((s32[]{:T(128)}, u32[1536]{0:T(1024)S(1)}, u32[1536]{0:T(1024)S(1)}, s32[1024]{0:T(1024)S(1)}, s32[]{:T(128)}, /*index=5*/s32[]{:T(128)}, s32[]{}) %tuple.57), condition=%wide.region_3.4_spmd.clone, body=%wide.region_2.3_spmd.clone.sunk | while | flops 29700 | bytes 109669 | solution.py:32
  132.9 5.9 %gather_fusion = s32[1536]{0:T(1024)S(1)} fusion(s32[1024]{0:T(1024)S(1)} %get-tuple-element.166, u32[2048]{0:T(1024)S(1)} %pad_clamp_fusion.7), kind=kCustom, calls=%fused_computation.clone.clone.1 | custom fusion | bytes 18432 | tf_op jit(solution)/shard_map/jit(searchsorted)/jit(_searchsorted_scan_impl)/vmap(jit(_searchsorted_scan_impl))/while/body/eval_jaxpr/gather | solution.py:32
  138.8 5.9 %gather_fusion = s32[1536]{0:T(1024)S(1)} fusion(s32[1024]{0:T(1024)S(1)} %get-tuple-element.166, u32[2048]{0:T(1024)S(1)} %pad_clamp_fusion.7), kind=kCustom, calls=%fused_computation.clone.clone.1 | custom fusion | bytes 18432 | tf_op jit(solution)/shard_map/jit(searchsorted)/jit(_searchsorted_scan_impl)/vmap(jit(_searchsorted_scan_impl))/while/body/eval_jaxpr/gather | solution.py:32
  144.8 5.9 %gather_fusion = s32[1536]{0:T(1024)S(1)} fusion(s32[1024]{0:T(1024)S(1)} %get-tuple-element.166, u32[2048]{0:T(1024)S(1)} %pad_clamp_fusion.7), kind=kCustom, calls=%fused_computation.clone.clone.1 | custom fusion | bytes 18432 | tf_op jit(solution)/shard_map/jit(searchsorted)/jit(_searchsorted_scan_impl)/vmap(jit(_searchsorted_scan_impl))/while/body/eval_jaxpr/gather | solution.py:32
  150.7 5.9 %gather_fusion = s32[1536]{0:T(1024)S(1)} fusion(s32[1024]{0:T(1024)S(1)} %get-tuple-element.166, u32[2048]{0:T(1024)S(1)} %pad_clamp_fusion.7), kind=kCustom, calls=%fused_computation.clone.clone.1 | custom fusion | bytes 18432 | tf_op jit(solution)/shard_map/jit(searchsorted)/jit(_searchsorted_scan_impl)/vmap(jit(_searchsorted_scan_impl))/while/body/eval_jaxpr/gather | solution.py:32
  156.7 5.9 %gather_fusion = s32[1536]{0:T(1024)S(1)} fusion(s32[1024]{0:T(1024)S(1)} %get-tuple-element.166, u32[2048]{0:T(1024)S(1)} %pad_clamp_fusion.7), kind=kCustom, calls=%fused_computation.clone.clone.1 | custom fusion | bytes 18432 | tf_op jit(solution)/shard_map/jit(searchsorted)/jit(_searchsorted_scan_impl)/vmap(jit(_searchsorted_scan_impl))/while/body/eval_jaxpr/gather | solution.py:32
  162.6 5.9 %gather_fusion = s32[1536]{0:T(1024)S(1)} fusion(s32[1024]{0:T(1024)S(1)} %get-tuple-element.166, u32[2048]{0:T(1024)S(1)} %pad_clamp_fusion.7), kind=kCustom, calls=%fused_computation.clone.clone.1 | custom fusion | bytes 18432 | tf_op jit(solution)/shard_map/jit(searchsorted)/jit(_searchsorted_scan_impl)/vmap(jit(_searchsorted_scan_impl))/while/body/eval_jaxpr/gather | solution.py:32
  168.6 5.9 %gather_fusion = s32[1536]{0:T(1024)S(1)} fusion(s32[1024]{0:T(1024)S(1)} %get-tuple-element.166, u32[2048]{0:T(1024)S(1)} %pad_clamp_fusion.7), kind=kCustom, calls=%fused_computation.clone.clone.1 | custom fusion | bytes 18432 | tf_op jit(solution)/shard_map/jit(searchsorted)/jit(_searchsorted_scan_impl)/vmap(jit(_searchsorted_scan_impl))/while/body/eval_jaxpr/gather | solution.py:32
  174.5 5.9 %gather_fusion = s32[1536]{0:T(1024)S(1)} fusion(s32[1024]{0:T(1024)S(1)} %get-tuple-element.166, u32[2048]{0:T(1024)S(1)} %pad_clamp_fusion.7), kind=kCustom, calls=%fused_computation.clone.clone.1 | custom fusion | bytes 18432 | tf_op jit(solution)/shard_map/jit(searchsorted)/jit(_searchsorted_scan_impl)/vmap(jit(_searchsorted_scan_impl))/while/body/eval_jaxpr/gather | solution.py:32
  180.4 5.9 %gather_fusion = s32[1536]{0:T(1024)S(1)} fusion(s32[1024]{0:T(1024)S(1)} %get-tuple-element.166, u32[2048]{0:T(1024)S(1)} %pad_clamp_fusion.7), kind=kCustom, calls=%fused_computation.clone.clone.1 | custom fusion | bytes 18432 | tf_op jit(solution)/shard_map/jit(searchsorted)/jit(_searchsorted_scan_impl)/vmap(jit(_searchsorted_scan_impl))/while/body/eval_jaxpr/gather | solution.py:32
  186.4 5.9 %gather_fusion = s32[1536]{0:T(1024)S(1)} fusion(s32[1024]{0:T(1024)S(1)} %get-tuple-element.166, u32[2048]{0:T(1024)S(1)} %pad_clamp_fusion.7), kind=kCustom, calls=%fused_computation.clone.clone.1 | custom fusion | bytes 18432 | tf_op jit(solution)/shard_map/jit(searchsorted)/jit(_searchsorted_scan_impl)/vmap(jit(_searchsorted_scan_impl))/while/body/eval_jaxpr/gather | solution.py:32
  192.3 5.9 %gather_fusion = s32[1536]{0:T(1024)S(1)} fusion(s32[1024]{0:T(1024)S(1)} %get-tuple-element.166, u32[2048]{0:T(1024)S(1)} %pad_clamp_fusion.7), kind=kCustom, calls=%fused_computation.clone.clone.1 | custom fusion | bytes 18432 | tf_op jit(solution)/shard_map/jit(searchsorted)/jit(_searchsorted_scan_impl)/vmap(jit(_searchsorted_scan_impl))/while/body/eval_jaxpr/gather | solution.py:32
  198.9 5.8 %gather_fusion.2 = s32[1536]{0:T(1024)S(1)} fusion(s32[1024]{0:T(1024)S(1)} %copy-done.3, s32[2048]{0:T(1024)S(1)} %pad_clamp_fusion.1), kind=kCustom, calls=%fused_computation.4 | custom fusion | bytes 18432 | tf_op jit(solution)/shard_map/jit(_take)/gather | solution.py:33
  205.1 3.1 gather_fusion.6
  213.8 3.1 gather_fusion.7
  219.9 36.6 %all-gather.2.cloned.1.call-done = bf16[2048,256]{1,0:T(8,128)(2,1)} async-done(((bf16[128,256]{1,0:T(8,128)(2,1)}), bf16[2048,256]{1,0:T(8,128)(2,1)}) %all-gather.2.cloned.1.call-update) | async-done | bytes 1048592 | tf_op jit(solution)/shard_map/all_gather | solution.py:92
  256.5 2.7 select_reduce_fusion
  259.7 3.2 convolution_multiply_fusion
  266.5 62.1 %reduce-scatter.2.cloned.1.call-done = f32[128,256]{1,0:T(8,128)} async-done(((f32[2048,256]{1,0:T(8,128)}), f32[128,256]{1,0:T(8,128)}) %reduce-scatter.2.cloned.1.call-update) | async-done | bytes 131088 | tf_op jit(solution)/shard_map/reduce_scatter | solution.py:108
  330.7 2.8 convolution_convert_fusion
  335.0 33.8 %all_to_all.31 = bf16[16,64,2,256]{3,2,1,0:T(2,128)(2,1)S(1)} all-to-all(bf16[16,64,2,256]{3,2,1,0:T(2,128)(2,1)S(1)} %convert_element_type.56), channel_id=1, replica_groups=mesh['dp'=16,'table'=64] {'dp'}, dimensions={0} | all-to-all | bytes 2097152 | tf_op jit(solution)/shard_map/all_to_all | solution.py:131
  371.0 16.1 %all-to-all-start.5 = ((bf16[16,64,2,256]{3,2,0,1:T(2,128)(2,1)}), bf16[16,64,2,256]{3,2,0,1:T(2,128)(2,1)S(1)}, u32[]{:S(2)}, u32[]{:S(2)}) async-start(bf16[16,64,2,256]{3,2,0,1:T(2,128)(2,1)} %copy.85), calls=%async_computation.6 | async-start | bytes 2097152 | tf_op jit(solution)/shard_map/all_to_all | solution.py:130
  387.3 53.3 %all-to-all-done.5 = bf16[16,64,2,256]{3,2,0,1:T(2,128)(2,1)S(1)} async-done(((bf16[16,64,2,256]{3,2,0,1:T(2,128)(2,1)}), bf16[16,64,2,256]{3,2,0,1:T(2,128)(2,1)S(1)}, u32[]{:S(2)}, u32[]{:S(2)}) %all-to-all-start.5) | async-done | bytes 1048608 | tf_op jit(solution)/shard_map/all_to_all | solution.py:130
  (172 shorter events, 37.3 us)
Async XLA Ops:
  7.2 212.4 %copy-start = (bf16[256,256]{1,0:T(8,128)(2,1)S(1)}, bf16[256,256]{1,0:T(8,128)(2,1)}, u32[]{:S(2)}) copy-start(bf16[256,256]{1,0:T(8,128)(2,1)} %param.15) | copy-start | bytes 393220
  13.6 13.0 %copy-start.2 = (s32[1024]{0:T(1024)}, s32[1024]{0:T(1024)S(1)}, u32[]{:S(2)}) copy-start(s32[1024]{0:T(1024)S(1)} %get-tuple-element.105) | copy-start | bytes 12292
  14.8 12.5 %copy-start.6 = (s32[16,64]{1,0:T(8,128)S(1)}, s32[16,64]{1,0:T(8,128)}, u32[]{:S(2)}) copy-start(s32[16,64]{1,0:T(8,128)} %lt.88) | copy-start | bytes 12292
  14.8 12.5 %copy-start.7 = (s32[16,64]{1,0:T(8,128)S(1)}, s32[16,64]{1,0:T(8,128)}, u32[]{:S(2)}) copy-start(s32[16,64]{1,0:T(8,128)} %reshape.230) | copy-start | bytes 12292
  14.8 12.5 %copy-start.10 = (s32[16]{0:T(128)S(1)}, s32[16]{0:T(128)}, u32[]{:S(2)}) copy-start(s32[16]{0:T(128)} %reshape.232) | copy-start | bytes 196
  14.8 52.1 %copy-start.5 = (f32[128,256]{1,0:T(8,128)S(1)}, f32[128,256]{1,0:T(8,128)}, u32[]{:S(2)}) copy-start(f32[128,256]{1,0:T(8,128)} %param.12) | copy-start | bytes 393220
  53.1 27.3 %all-to-all-start.1 = ((s32[16,64,2]{0,2,1:T(2,128)}), s32[16,64,2]{0,2,1:T(2,128)S(1)}, u32[]{:S(2)}, u32[]{:S(2)}) async-start(s32[16,64,2]{0,2,1:T(2,128)} %copy.72), calls=%async_computation.1 | async-start | bytes 131072 | tf_op jit(solution)/shard_map/all_to_all | solution.py:63
  92.4 33.5 %all-to-all-start.2 = ((bf16[16,64,2,256]{3,2,1,0:T(2,128)(2,1)}), bf16[16,64,2,256]{3,2,1,0:T(2,128)(2,1)S(1)}, u32[]{:S(2)}, u32[]{:S(2)}) async-start(bf16[16,64,2,256]{3,2,1,0:T(2,128)(2,1)} %broadcast_select_fusion), calls=%async_computation.2 | async-start | bytes 2097152 | tf_op jit(solution)/shard_map/all_to_all | solution.py:75
  98.0 34.8 %copy-start.1 = (s32[1024]{0:T(1024)S(1)}, s32[1024]{0:T(1024)}, u32[]{:S(2)}) copy-start(s32[1024]{0:T(1024)} %get-tuple-element.152) | copy-start | bytes 12292
  128.1 80.4 %all-to-all-start.3 = ((bf16[16,64,2,256]{3,2,0,1:T(2,128)(2,1)}), bf16[16,64,2,256]{3,2,0,1:T(2,128)(2,1)S(1)}, u32[]{:S(2)}, u32[]{:S(2)}) async-start(bf16[16,64,2,256]{3,2,0,1:T(2,128)(2,1)} %copy.83), calls=%async_computation.3 | async-start | bytes 2097152 | tf_op jit(solution)/shard_map/all_to_all | solution.py:74
  132.8 123.7 %all-gather.2.cloned.1.call-start = ((), (), s32[]{:S(2)}) async-start(), calls=%async_computation.7 | async-start | bytes 1114112 | tf_op jit(solution)/shard_map/all_gather | solution.py:92
  198.2 0.7 copy-start.3
  198.9 5.9 %copy-start.8 = (s32[1,1,128,4]{2,3,1,0:T(4,128)S(1)}, s32[1,1,128,4]{2,3,1,0:T(4,128)}, u32[]{:S(2)}) copy-start(s32[1,1,128,4]{2,3,1,0:T(4,128)} %param.18) | copy-start | bytes 6148
  209.9 2.4 copy-start.4
  209.9 3.6 copy-start.9
  213.3 115.2 %reduce-scatter.2.cloned.1.call-start = ((), (), s32[]{:S(2)}) async-start(), calls=%async_computation.8 | async-start | bytes 2228224 | tf_op jit(solution)/shard_map/reduce_scatter | solution.py:108
  371.0 69.6 %all-to-all-start.5 = ((bf16[16,64,2,256]{3,2,0,1:T(2,128)(2,1)}), bf16[16,64,2,256]{3,2,0,1:T(2,128)(2,1)S(1)}, u32[]{:S(2)}, u32[]{:S(2)}) async-start(bf16[16,64,2,256]{3,2,0,1:T(2,128)(2,1)} %copy.85), calls=%async_computation.6 | async-start | bytes 2097152 | tf_op jit(solution)/shard_map/all_to_all | solution.py:130
  441.6 0.9 copy-start.11
Sparse Core Ops, SparseCore 0:
  213.4 42.9 all-gather.1
  263.0 65.4 reduce-scatter.1
where the time goes:
time: 451 us
  waiting for transfers between devices  193 us (43%)
  local copies, waits for them, and re-layouts  117 us (26%)
  blocking collectives  57.4 us (13%)
  starting transfers between devices  40.3 us (9%)
  between operations  14.6 us (3%)
  other arithmetic  14 us (3%)
  matrix products  13 us (3%)
    gather x11, local copies, waits for them, and re-layouts, slot_table(): owners = jnp.searchsorted(block_ends, positions, side='right')  64.4 us
    reduce_scatter x1, waiting for transfers between devices, on_device(): lax.psum_scatter(lax.dot_general(grad_scores, query_out, (((0,), (0,)), (...  62.1 us
    all_to_all x1, waiting for transfers between devices, on_device(): lax.all_to_all(lax.all_to_all(outgoing.astype(jnp.bfloat16), 'dp', split_...  53.3 us
    all_gather x1, waiting for transfers between devices, on_device(): all_items = lax.all_gather(item_out, 'dp', axis=0, tiled=True)  36.6 us
    all_to_all x1, blocking collectives, on_device(): lax.all_to_all(outgoing.astype(jnp.bfloat16), 'dp', split_axis=0, concat_...  33.8 us
    all_to_all x1, waiting for transfers between devices, on_device(): lax.all_to_all(picked, 'dp', split_axis=0, concat_axis=0, tiled=True)  28 us
    all_to_all x1, blocking collectives, on_device(): lax.all_to_all(requests, 'dp', split_axis=0, concat_axis=0, tiled=True)  23.6 us
    all_to_all x1, starting transfers between devices, on_device(): lax.all_to_all(lax.all_to_all(outgoing.astype(jnp.bfloat16), 'dp', split_...  16.1 us
  transfers between devices with their start and end apart: 6, of which 5 were waited for; matrix products, arithmetic and copies ran while one was open for 19% of the time, Pallas kernels for 0%

commit v1 on v0

v1 whole, which is shorter than its diff:
```python
import jax
import jax.numpy as jnp
from jax import lax
from jax.experimental import pallas as pl
from jax.experimental.pallas import tpu as pltpu
from jax.sharding import PartitionSpec as P

CAP = 2
LANES = 128
CORES = 2

learn_rate = 0.3
epsilon = 1e-06
sharpness = 3.0

VMEM = pl.BlockSpec(memory_space=pltpu.VMEM)
SMEM = pl.BlockSpec(memory_space=pltpu.SMEM)

NT = (((1,), (1,)), ((), ()))
TN = (((0,), (0,)), ((), ()))


def iota(shape, axis):
    return lax.broadcasted_iota(jnp.int32, shape, axis)


def dot(a, b, dims=(((1,), (0,)), ((), ()))):
    return lax.dot_general(a, b, dims, preferred_element_type=jnp.float32)


def hits(a, b):
    return jnp.where(a == b, 1.0, 0.0)


def call(body, out_shape, in_specs, scratch=()):
    return pl.pallas_call(
        body,
        out_shape=out_shape,
        in_specs=in_specs,
        out_specs=jax.tree.map(lambda _: VMEM, out_shape),
        scratch_shapes=list(scratch),
        compiler_params=pltpu.CompilerParams(vmem_limit_bytes=40 * 1024 * 1024),
    )


def request_body(core_ref, list_ref, counts_ref, req_ref, pos_ref, list2d, counts2d, square):
    length, owners = list_ref.shape[1], counts_ref.shape[1]
    list2d[...] = jnp.zeros_like(list2d)
    for b in range(length // LANES):
        list2d[b : b + 1, :] = list_ref[:, b * LANES : (b + 1) * LANES].astype(jnp.float32)
    for b in range(owners // LANES):
        counts2d[b : b + 1, :] = counts_ref[:, b * LANES : (b + 1) * LANES].astype(jnp.float32)
    rows = owners // LANES
    counts = counts2d[...]
    counts_bf = counts.astype(jnp.bfloat16)
    before = hits(iota((LANES, LANES), 0) < iota((LANES, LANES), 1), True).astype(jnp.bfloat16)
    within = dot(counts_bf, before)
    row_total = dot(counts_bf, jnp.ones((LANES, LANES), jnp.bfloat16))
    base = [jnp.zeros((1, LANES), jnp.float32)]
    for i in range(rows - 1):
        base.append(base[-1] + row_total[i : i + 1, :])
    starts = within + jnp.concatenate(base, axis=0)
    second = jnp.where(counts > 1.5, starts + 1.0, -1.0)
    positions = jnp.concatenate([starts, second], axis=0)
    pos_int = positions.astype(jnp.int32)
    list_bf = list2d[...].astype(jnp.bfloat16)
    down = iota((LANES, LANES), 0)
    block = iota((list2d.shape[0], LANES), 0)
    picked = []
    for r in range(CAP * rows):
        p = pos_int[r : r + 1, :]
        spread = dot(list_bf, hits(down, p & (LANES - 1)).astype(jnp.bfloat16))
        value = jnp.sum(jnp.where(block == (p >> 7), spread, 0.0), axis=0, keepdims=True)
        picked.append(jnp.where(p >= 0, value, -1.0))
    width = LANES // CORES
    mine = core_ref[0] == 0
    for out_ref, values in ((req_ref, jnp.concatenate(picked, axis=0)), (pos_ref, positions)):
        square[...] = jnp.zeros_like(square)
        square[0 : CAP * rows, :] = values
        turned = square[...].T
        first, other = turned[:width, : CAP * rows], turned[width:, : CAP * rows]
        swapped = jnp.concatenate(
            [jnp.where(mine, first, other), jnp.where(mine, other, first)], axis=1
        )
        out_ref[...] = swapped.astype(jnp.int32)


def pick_body(recv_ref, near_ref, far_ref, out_ref, *wide):
    groups, slots = recv_ref.shape
    chips, per = near_ref.shape[:2]
    recv = recv_ref[...]
    lane = iota((groups, per), 1)
    for side, rows_ref in enumerate((near_ref, far_ref)):
        for y in range(chips):
            ks = [side * CAP * chips + c * chips + y for c in range(CAP)]
            wanted = jnp.concatenate([hits(lane, recv[:, k : k + 1]) for k in ks], axis=0)
            got = dot(wanted.astype(jnp.bfloat16), rows_ref[y])
            for c, k in enumerate(ks):
                for b, half in enumerate(wide):
                    half[pl.ds(k, groups, stride=slots), :] = got[
                        c * groups : (c + 1) * groups, b * LANES : (b + 1) * LANES
                    ]
    for b, half in enumerate(wide):
        out_ref[:, b * LANES : (b + 1) * LANES] = half[...].astype(jnp.bfloat16)


def tower_body(
    pos_ref, item_refs, query_refs, fetched, item_w, query_w, hits_ref, normed_ref, factor_ref, out_ref
):
    pairs = item_refs.shape[0]
    fetched_rows = fetched[...]
    pos = pos_ref[...]
    outs = []
    for side, (refs_ref, w_ref) in enumerate(((item_refs, item_w), (query_refs, query_w))):
        span = pl.ds(side * pairs, pairs)
        refs = refs_ref[...]
        weight = hits(refs[:, 0:1], pos)
        for l in range(1, refs.shape[1]):
            weight = weight + hits(refs[:, l : l + 1], pos)
        weight = weight.astype(jnp.bfloat16)
        hits_ref[span, :] = weight
        pool = dot(weight, fetched_rows).astype(jnp.bfloat16)
        hidden = dot(pool, w_ref[...])
        factor = lax.rsqrt(jnp.mean(hidden * hidden, axis=1, keepdims=True) + epsilon)
        normed = hidden * factor
        normed_ref[span, :] = normed
        factor_ref[span, :] = jnp.broadcast_to(factor, (pairs, LANES))
        outs.append(normed.astype(jnp.bfloat16))
    for y in range(out_ref.shape[0]):
        out_ref[y, :pairs, :] = outs[0]
        out_ref[y, pairs:, :] = outs[1]


def loss_body(
    y_ref, near, far, normed_ref, factor_ref, item_w, query_w, hits_ref, loss_ref, grads_ref, inverse, own_exp
):
    chips, both, width = near.shape
    pairs = both // 2
    scale = sharpness * width ** (-0.5)
    own = y_ref[0]

    def items(y):
        return jnp.concatenate([near[y, :pairs, :], far[y, :pairs, :]], axis=0)

    def queries(y):
        return jnp.concatenate([near[y, pairs:, :], far[y, pairs:, :]], axis=0)

    def denominators(y, carry):
        q = queries(y)
        total = jnp.zeros((8, both), jnp.float32)
        for j in range(chips):
            e = jnp.exp(dot(items(j), q, NT) * scale)
            total = total + jnp.sum(e.reshape(both // 8, 8, both), axis=0)
        inverse[y] = jnp.sum(total, axis=0, keepdims=True)
        return carry

    lax.fori_loop(0, chips, denominators, 0)
    item_own, query_own = near[own, :pairs, :], near[own, pairs:, :]
    own_hits = iota((pairs, pairs), 0) == iota((pairs, pairs), 1)
    diagonal = jnp.sum(
        jnp.where(own_hits, dot(item_own, query_own, NT) * scale, 0.0), axis=0, keepdims=True
    )
    loss_ref[...] = jnp.log(inverse[own][:, :pairs]) - diagonal
    ones = hits(iota((pairs, both), 0), iota((pairs, both), 1))
    grad_item = jnp.zeros((pairs, width), jnp.float32)
    row_total = jnp.zeros((pairs, LANES), jnp.float32)
    for y in range(chips):
        q = queries(y)
        soft = jnp.exp(dot(item_own, q, NT) * scale) * (1.0 / inverse[y])
        soft = soft - jnp.where(own == y, ones, 0.0)
        grad_item = grad_item + dot(soft.astype(jnp.bfloat16), q)
        e = jnp.exp(dot(query_own, items(y), NT) * scale)
        own_exp[y] = e
        for b in range(both // LANES):
            row_total = row_total + e[:, b * LANES : (b + 1) * LANES]
    row_inverse = 1.0 / jnp.sum(row_total, axis=1, keepdims=True)
    grad_query = jnp.zeros((pairs, width), jnp.float32)
    for y in range(chips):
        soft = own_exp[y] * row_inverse - jnp.where(own == y, ones, 0.0)
        grad_query = grad_query + dot(soft.astype(jnp.bfloat16), items(y))
    backs = []
    for side, (grad, w_ref) in enumerate(((grad_item, item_w), (grad_query, query_w))):
        span = pl.ds(side * pairs, pairs)
        grad = grad * scale
        normed = normed_ref[span, :]
        factor = factor_ref[span, 0:1]
        inner_mean = jnp.mean(grad * normed, axis=1, keepdims=True)
        grad_hidden = (factor * (grad - normed * inner_mean)).astype(jnp.bfloat16)
        backs.append(dot(grad_hidden, w_ref[...], NT))
    back = jnp.concatenate(backs, axis=0)
    high = back.astype(jnp.bfloat16)
    low = (back - high.astype(jnp.float32)).astype(jnp.bfloat16)
    step = 256
    for s in range(hits_ref.shape[1] // step):
        weight = hits_ref[:, s * step : (s + 1) * step]
        grads_ref[s * step : (s + 1) * step, :] = (
            dot(weight, high, TN) + dot(weight, low, TN)
        ).astype(jnp.bfloat16)


def column_body(recv_ref, grads_ref, keep_ref, send_ref, square, *wide):
    groups, slots = recv_ref.shape
    chips = slots // (CAP * CORES)
    per = keep_ref.shape[1]
    square[...] = jnp.full_like(square, -1.0)
    square[0:groups, 0:slots] = recv_ref[...].astype(jnp.float32)
    turned = square[...].T.astype(jnp.int32)
    for b, half in enumerate(wide):
        half[...] = grads_ref[:, b * LANES : (b + 1) * LANES].astype(jnp.float32)
    down = iota((per, CAP * groups), 0)
    for side in (1, 0):
        for y in range(chips):
            ks = [side * CAP * chips + c * chips + y for c in range(CAP)]
            wanted = jnp.concatenate([turned[k : k + 1, :groups] for k in ks], axis=1)
            values = jnp.concatenate(
                [
                    jnp.concatenate([half[pl.ds(k, groups, stride=slots), :] for half in wide], axis=1)
                    for k in ks
                ],
                axis=0,
            ).astype(jnp.bfloat16)
            summed = dot(hits(down, wanted).astype(jnp.bfloat16), values)
            if side == 1:
                send_ref[y] = summed.astype(jnp.bfloat16)
            else:
                keep_ref[y] = summed


def add_body(a_ref, b_ref, out_ref):
    out_ref[...] = (a_ref[...] + b_ref[...].astype(jnp.float32)).astype(jnp.bfloat16)


def adagrad_body(parts_ref, table_ref, accum_ref, new_table_ref, new_accum_ref):
    grad = parts_ref[0].astype(jnp.float32)
    for y in range(1, parts_ref.shape[0]):
        grad = grad + parts_ref[y].astype(jnp.float32)
    rows, width = grad.shape
    mean = jnp.sum(grad * grad, axis=1, keepdims=True) * (1.0 / width)
    across = jnp.sum(
        jnp.where(iota((rows, rows), 0) == iota((rows, rows), 1), mean, 0.0), axis=0, keepdims=True
    )
    down = jnp.sum(
        jnp.where(iota((rows, rows), 0) == iota((rows, rows), 1), accum_ref[...], 0.0),
        axis=1,
        keepdims=True,
    )
    new_accum_ref[...] = accum_ref[...] + across
    new_table_ref[...] = table_ref[...] - learn_rate * grad / jnp.sqrt(down + mean)


def on_device(
    table, accum, item_weight, query_weight, packed_rows, block_counts, item_refs, query_refs
):
    bf16, f32, i32 = jnp.bfloat16, jnp.float32, jnp.int32
    shape = jax.ShapeDtypeStruct
    n_dp, n_table = lax.axis_size("dp"), lax.axis_size("table")
    chips = n_dp // CORES
    per, width = table.shape
    pairs = item_refs.shape[2]
    slots = CAP * n_dp
    total = slots * n_table
    replica = lax.axis_index("dp")
    core = (replica % CORES).reshape(1).astype(i32)
    chip = (replica // CORES).reshape(1).astype(i32)
    along_y = [[y * CORES + c for y in range(chips)] for c in range(CORES)]
    swap = [(r, r ^ 1) for r in range(n_dp)]

    near_rows = lax.all_to_all(
        jnp.broadcast_to(table.astype(bf16)[None], (chips, per, width)),
        "dp",
        split_axis=0,
        concat_axis=0,
        axis_index_groups=along_y,
        tiled=True,
    )
    far_rows = lax.ppermute(near_rows, "dp", swap)
    requests, positions = call(
        request_body,
        (shape((n_table, slots), i32), shape((n_table, slots), i32)),
        [SMEM, VMEM, VMEM],
        [
            pltpu.VMEM((16, LANES), f32),
            pltpu.VMEM((n_dp * n_table // LANES, LANES), f32),
            pltpu.VMEM((LANES, LANES), f32),
        ],
    )(core, packed_rows.reshape(1, -1), block_counts.reshape(1, -1))
    received = lax.all_to_all(requests, "table", split_axis=0, concat_axis=0, tiled=True)
    picked = call(
        pick_body,
        shape((total, width), bf16),
        [VMEM] * 3,
        [pltpu.VMEM((total, LANES), f32)] * (width // LANES),
    )(received, near_rows, far_rows)
    fetched = lax.all_to_all(
        picked.reshape(n_table, slots, width), "table", split_axis=0, concat_axis=0, tiled=True
    ).reshape(total, width)
    pair_hits, normed, factor, spread = call(
        tower_body,
        (
            shape((2 * pairs, total), bf16),
            shape((2 * pairs, width), f32),
            shape((2 * pairs, LANES), f32),
            shape((chips, 2 * pairs, width), bf16),
        ),
        [VMEM] * 6,
    )(positions.reshape(1, total), item_refs[0, 0], query_refs[0, 0], fetched, item_weight, query_weight)
    near = lax.all_to_all(
        spread, "dp", split_axis=0, concat_axis=0, axis_index_groups=along_y, tiled=True
    )
    far = lax.ppermute(near, "dp", swap)
    loss, slot_grads = call(
        loss_body,
        (shape((1, pairs), f32), shape((total, width), bf16)),
        [SMEM] + [VMEM] * 7,
        [pltpu.VMEM((chips, 1, 2 * pairs), f32), pltpu.VMEM((chips, pairs, 2 * pairs), f32)],
    )(chip, near, far, normed, factor, item_weight, query_weight, pair_hits)
    returned = lax.all_to_all(
        slot_grads.reshape(n_table, slots, width), "table", split_axis=0, concat_axis=0, tiled=True
    ).reshape(total, width)
    keep, send = call(
        column_body,
        (shape((chips, per, width), f32), shape((chips, per, width), bf16)),
        [VMEM] * 2,
        [pltpu.VMEM((LANES, LANES), f32)] + [pltpu.VMEM((total, LANES), f32)] * (width // LANES),
    )(received, returned)
    other = lax.ppermute(send, "dp", swap)
    both = call(add_body, shape((chips, per, width), bf16), [VMEM] * 2)(keep, other)
    parts = lax.all_to_all(
        both, "dp", split_axis=0, concat_axis=0, axis_index_groups=along_y, tiled=True
    )
    new_table, new_accum = call(
        adagrad_body, (shape((per, width), f32), shape((1, per), f32)), [VMEM] * 3
    )(parts, table, accum.reshape(1, per))
    return (new_table, new_accum.reshape(per), loss.reshape(1, 1, pairs))


def solution(mesh):
    in_specs = (
        P(("dp", "table"), None),
        P(("dp", "table")),
        P(),
        P(),
        P("dp", "table", None),
        P("dp", "table", None),
        P("dp", "table", None, None),
        P("dp", "table", None, None),
    )
    out_specs = (P(("dp", "table"), None), P(("dp", "table")), P("dp", "table", None))
    return jax.shard_map(
        on_device, mesh=mesh, in_specs=in_specs, out_specs=out_specs, check_vma=False
    )
```

time: 451 us -> 263 us (0.58)
  waiting for transfers between devices: 193 us -> 53.5 us
  local copies, waits for them, and re-layouts: 117 us -> 4.25 us
  blocking collectives: 57.4 us -> 157 us
  Pallas kernels: 0 us -> 14 us
  between operations: 14.6 us -> 0.78 us
  other arithmetic: 14 us -> 0.92 us
  matrix products: 13 us -> 0 us
  starting transfers between devices: 40.3 us -> 32 us
    gather x25 -> x0, local copies, waits for them, and re-layouts: 101 us -> none  [the longest x11 64.4 us: slot_table(): owners = jnp.searchsorted(block_ends, positions, side='right')]
    all_to_all x2 -> x5, blocking collectives: 57.4 us -> 157 us  [the longest x1 60.7 us: on_device(): lax.all_to_all(slot_grads.reshape(n_table, slots, width), 'table', split_...]
    reduce_scatter x1 -> x0, waiting for transfers between devices: 62.1 us -> none  [on_device(): lax.psum_scatter(lax.dot_general(grad_scores, query_out, (((0,), (0,)), (...]
    all_to_all x4 -> x1, waiting for transfers between devices: 94.7 us -> 49.7 us  [on_device(): lax.all_to_all(picked.reshape(n_table, slots, width), 'table', split_axis...]
    all_gather x1 -> x0, waiting for transfers between devices: 36.6 us -> none  [on_device(): all_items = lax.all_gather(item_out, 'dp', axis=0, tiled=True)]
    all_to_all x4 -> x1, starting transfers between devices: 40 us -> 4.78 us  [on_device(): lax.all_to_all(picked.reshape(n_table, slots, width), 'table', split_axis...]
    ppermute x0 -> x3, starting transfers between devices: none -> 27.2 us  [the longest x1 12.2 us: on_device(): far_rows = lax.ppermute(near_rows, 'dp', swap)]
    pallas_call x0 -> x7, Pallas kernels: none -> 14 us  [the longest x1 6.35 us: on_device(): call(loss_body, (shape((1, pairs), f32), shape((total, width), bf16)), [S...]
  transfers between devices with their start and end apart: 6 -> 4, of which waited for: 5 -> 3; matrix products, arithmetic and copies ran while one was open for 19% -> 0% of each run, Pallas kernels for 0% -> 0%
where the time goes in v1:
time: 263 us
  blocking collectives  157 us (60%)
  waiting for transfers between devices  53.5 us (20%)
  starting transfers between devices  32 us (12%)
  Pallas kernels  14 us (5%)
  local copies, waits for them, and re-layouts  4.25 us (2%)
    all_to_all x1, blocking collectives, on_device(): lax.all_to_all(slot_grads.reshape(n_table, slots, width), 'table', split_...  60.7 us
    all_to_all x1, waiting for transfers between devices, on_device(): lax.all_to_all(picked.reshape(n_table, slots, width), 'table', split_axis...  49.7 us
    all_to_all x1, blocking collectives, on_device(): lax.all_to_all(requests, 'table', split_axis=0, concat_axis=0, tiled=True)  31.1 us
    all_to_all x1, blocking collectives, on_device(): lax.all_to_all(spread, 'dp', split_axis=0, concat_axis=0, axis_index_grou...  25.4 us
    all_to_all x1, blocking collectives, on_device(): lax.all_to_all(both, 'dp', split_axis=0, concat_axis=0, axis_index_groups...  20.5 us
    all_to_all x1, blocking collectives, on_device(): lax.all_to_all(jnp.broadcast_to(table.astype(bf16)[None], (chips, per, wi...  19.6 us
    ppermute x1, starting transfers between devices, on_device(): far_rows = lax.ppermute(near_rows, 'dp', swap)  12.2 us
    ppermute x1, starting transfers between devices, on_device(): far = lax.ppermute(near, 'dp', swap)  8.55 us
  transfers between devices with their start and end apart: 4, of which 3 were waited for; matrix products, arithmetic and copies ran while one was open for 0% of the time, Pallas kernels for 0%

profile of v1, /device:TPU:1, one launch (start us, length us, event | category | flops | bytes accessed | tf_op | source)
XLA Modules:
  0.0 262.7 jit_solution(10105612870305384677)
XLA Ops:
  0.6 0.9 convert_element_type.3
  1.6 19.6 %all_to_all.36.near_ref = bf16[8,128,256]{2,1,0:T(8,128)(2,1)S(1)} all-to-all(bf16[8,128,256]{2,1,0:T(8,128)(2,1)S(1)} %broadcast_in_dim.2), channel_id=1, replica_groups={{0,128,256,384,512,640,768,896},{64,192,320,448,576,704,832,960},{1,129..., dimensions={0} | all-to-all | bytes 1048576 | tf_op jit(solution)/shard_map/all_to_all | solution.py:268
  21.2 12.2 %collective-permute-start = (bf16[8,128,256]{2,1,0:T(8,128)(2,1)S(1)}, bf16[8,128,256]{2,1,0:T(8,128)(2,1)S(1)}, u32[]{:S(2)}, u32[]{:S(2)}) collective-permute-start(bf16[8,128,256]{2,1,0:T(8,128)(2,1)S(1)} %all_to_all.36.near_ref), channel_id=1, source_target_pairs={{0,64},{64,0},{128,192},{192,128},{256,320},{320,256},{384,448},{4... | collective-permute-start | bytes 1572872 | tf_op jit(solution)/shard_map/ppermute | solution.py:276
  33.3 0.0 copy-start.7
  33.4 0.0 copy-start.8
  33.4 0.7 copy-done.7
  34.0 0.0 copy-done.8
  34.1 0.6 shard_map.103
  34.6 31.1 %all_to_all.37 = s32[64,1,32]{2,1,0:T(1,128)S(1)} all-to-all(s32[64,1,32]{2,1,0:T(1,128)S(1)} %bitcast.24), channel_id=1, replica_groups=mesh['dp'=16,'table'=64] {'table'}, dimensions={0} | all-to-all | bytes 16384 | tf_op jit(solution)/shard_map/all_to_all | solution.py:287
  65.7 3.2 %shard_map.104 = bf16[2048,256]{1,0:T(8,128)(2,1)} custom-call(s32[64,32]{1,0:T(8,128)S(1)} %bitcast.20, bf16[8,128,256]{2,1,0:T(8,128)(2,1)S(1)} %all_to_all.36.near_ref, bf16[8,128,256]{2,1,0:T(8,128)(2,1)S(1)} %collective-permute-done.far_ref), custom_call_target="tpu_custom_call" | custom-call | tf_op jit(solution)/shard_map/pallas_call | solution.py:288
  68.9 4.8 %all-to-all-start.2 = ((bf16[64,32,256]{2,1,0:T(8,128)(2,1)}), bf16[64,32,256]{2,1,0:T(8,128)(2,1)S(1)}, u32[]{:S(2)}, u32[]{:S(2)}) async-start(bf16[64,32,256]{2,1,0:T(8,128)(2,1)} %bitcast.9), calls=%async_computation.2 | async-start | bytes 2097152 | tf_op jit(solution)/shard_map/all_to_all | solution.py:294
  73.7 0.0 copy-start.1
  73.7 0.1 reshape.49.pos_ref
  73.8 0.1 copy.16
  73.9 0.1 copy.17
  74.0 49.7 %all-to-all-done.2 = bf16[64,32,256]{2,1,0:T(8,128)(2,1)S(1)} async-done(((bf16[64,32,256]{2,1,0:T(8,128)(2,1)}), bf16[64,32,256]{2,1,0:T(8,128)(2,1)S(1)}, u32[]{:S(2)}, u32[]{:S(2)}) %all-to-all-start.2) | async-done | bytes 1048608 | tf_op jit(solution)/shard_map/all_to_all | solution.py:294
  123.7 1.3 shard_map.105
  125.0 0.7 copy-done.3
  125.7 25.4 %all_to_all.38.near = bf16[8,256,256]{2,1,0:T(8,128)(2,1)S(1)} all-to-all(bf16[8,256,256]{2,1,0:T(8,128)(2,1)S(1)} %get-tuple-element.17), channel_id=1, replica_groups={{0,128,256,384,512,640,768,896},{64,192,320,448,576,704,832,960},{1,129..., dimensions={0} | all-to-all | bytes 2097152 | tf_op jit(solution)/shard_map/all_to_all | solution.py:307
  151.2 8.6 %collective-permute-start.1 = (bf16[8,256,256]{2,1,0:T(8,128)(2,1)S(1)}, bf16[8,256,256]{2,1,0:T(8,128)(2,1)S(1)}, u32[]{:S(2)}, u32[]{:S(2)}) collective-permute-start(bf16[8,256,256]{2,1,0:T(8,128)(2,1)S(1)} %all_to_all.38.near), channel_id=1, source_target_pairs={{0,64},{64,0},{128,192},{192,128},{256,320},{320,256},{384,448},{4... | collective-permute-start | bytes 3145736 | tf_op jit(solution)/shard_map/ppermute | solution.py:310
  159.7 2.3 collective-permute-done.1.far
  162.0 0.9 copy-done.4
  162.9 0.9 copy-done.6
  163.8 6.4 %shard_map.106 = (f32[1,128]{1,0:T(1,128)}, bf16[2048,256]{1,0:T(8,128)(2,1)S(1)}) custom-call(s32[1]{0:T(128)} %bitcast.6.y_ref, bf16[8,256,256]{2,1,0:T(8,128)(2,1)S(1)} %all_to_all.38.near, bf16[8,256,256]{2,1,0:T(8,128)(2,1)S(1)} %collective-permute-done.1.far, f32[256,256]{1,0:T(8,128)S(1)} %copy-done.4, f32[256,128]{1,0:T(8,128)S(1)} %copy-done.6, ...), custom_call_target="tpu_custom_call" | custom-call | tf_op jit(solution)/shard_map/pallas_call | solution.py:311
  170.2 60.7 %all_to_all.39 = bf16[64,32,256]{2,1,0:T(8,128)(2,1)S(1)} all-to-all(bf16[64,32,256]{2,1,0:T(8,128)(2,1)S(1)} %bitcast.19), channel_id=1, replica_groups=mesh['dp'=16,'table'=64] {'table'}, dimensions={0} | all-to-all | bytes 2097152 | tf_op jit(solution)/shard_map/all_to_all | solution.py:317
  230.9 1.7 shard_map.107
  232.5 6.5 %collective-permute-start.2 = (bf16[8,128,256]{2,1,0:T(8,128)(2,1)S(1)}, bf16[8,128,256]{2,1,0:T(8,128)(2,1)S(1)}, u32[]{:S(2)}, u32[]{:S(2)}) collective-permute-start(bf16[8,128,256]{2,1,0:T(8,128)(2,1)S(1)} %get-tuple-element.23), channel_id=1, source_target_pairs={{0,64},{64,0},{128,192},{192,128},{256,320},{320,256},{384,448},{4... | collective-permute-start | bytes 1572872 | tf_op jit(solution)/shard_map/ppermute | solution.py:326
  239.1 1.5 collective-permute-done.2.b_ref
  240.6 0.1 shard_map.108
  240.7 20.5 %all_to_all.40.parts_ref = bf16[8,128,256]{2,1,0:T(8,128)(2,1)S(1)} all-to-all(bf16[8,128,256]{2,1,0:T(8,128)(2,1)S(1)} %shard_map.108), channel_id=1, replica_groups={{0,128,256,384,512,640,768,896},{64,192,320,448,576,704,832,960},{1,129..., dimensions={0} | all-to-all | bytes 1048576 | tf_op jit(solution)/shard_map/all_to_all | solution.py:328
  261.2 0.7 copy-done.9
  261.8 0.9 shard_map.109
  (17 shorter events, 0.1 us)
Async XLA Ops:
  21.2 44.5 %collective-permute-start = (bf16[8,128,256]{2,1,0:T(8,128)(2,1)S(1)}, bf16[8,128,256]{2,1,0:T(8,128)(2,1)S(1)}, u32[]{:S(2)}, u32[]{:S(2)}) collective-permute-start(bf16[8,128,256]{2,1,0:T(8,128)(2,1)S(1)} %all_to_all.36.near_ref), channel_id=1, source_target_pairs={{0,64},{64,0},{128,192},{192,128},{256,320},{320,256},{384,448},{4... | collective-permute-start | bytes 1572872 | tf_op jit(solution)/shard_map/ppermute | solution.py:276
  33.3 0.7 copy-start.7
  33.4 0.7 copy-start.8
  68.9 4.9 %copy-start.10 = (s32[1,1,128,4]{2,3,1,0:T(4,128)S(1)}, s32[1,1,128,4]{2,3,1,0:T(4,128)}, u32[]{:S(2)}) copy-start(s32[1,1,128,4]{2,3,1,0:T(4,128)} %param.14) | copy-start | bytes 6148
  68.9 5.0 %copy-start.11 = (s32[1,1,128,4]{2,3,1,0:T(4,128)S(1)}, s32[1,1,128,4]{2,3,1,0:T(4,128)}, u32[]{:S(2)}) copy-start(s32[1,1,128,4]{2,3,1,0:T(4,128)} %param.15) | copy-start | bytes 6148
  68.9 54.8 %copy-start.2 = (bf16[256,256]{1,0:T(8,128)(2,1)S(1)}, bf16[256,256]{1,0:T(8,128)(2,1)}, u32[]{:S(2)}) copy-start(bf16[256,256]{1,0:T(8,128)(2,1)} %query_w.3) | copy-start | bytes 393220
  68.9 54.8 %all-to-all-start.2 = ((bf16[64,32,256]{2,1,0:T(8,128)(2,1)}), bf16[64,32,256]{2,1,0:T(8,128)(2,1)S(1)}, u32[]{:S(2)}, u32[]{:S(2)}) async-start(bf16[64,32,256]{2,1,0:T(8,128)(2,1)} %bitcast.9), calls=%async_computation.2 | async-start | bytes 2097152 | tf_op jit(solution)/shard_map/all_to_all | solution.py:294
  73.7 50.0 %copy-start.1 = (bf16[256,256]{1,0:T(8,128)(2,1)S(1)}, bf16[256,256]{1,0:T(8,128)(2,1)}, u32[]{:S(2)}) copy-start(bf16[256,256]{1,0:T(8,128)(2,1)} %item_w.3) | copy-start | bytes 393220
  125.0 0.7 copy-start.3
  125.7 25.4 %copy-start.5 = (f32[256,128]{1,0:T(8,128)}, f32[256,128]{1,0:T(8,128)S(1)}, u32[]{:S(2)}) copy-start(f32[256,128]{1,0:T(8,128)S(1)} %get-tuple-element.19.factor_ref) | copy-start | bytes 393220
  151.2 10.8 %collective-permute-start.1 = (bf16[8,256,256]{2,1,0:T(8,128)(2,1)S(1)}, bf16[8,256,256]{2,1,0:T(8,128)(2,1)S(1)}, u32[]{:S(2)}, u32[]{:S(2)}) collective-permute-start(bf16[8,256,256]{2,1,0:T(8,128)(2,1)S(1)} %all_to_all.38.near), channel_id=1, source_target_pairs={{0,64},{64,0},{128,192},{192,128},{256,320},{320,256},{384,448},{4... | collective-permute-start | bytes 3145736 | tf_op jit(solution)/shard_map/ppermute | solution.py:310
  162.0 0.9 copy-start.4
  162.9 0.9 copy-start.6
  232.5 8.0 %collective-permute-start.2 = (bf16[8,128,256]{2,1,0:T(8,128)(2,1)S(1)}, bf16[8,128,256]{2,1,0:T(8,128)(2,1)S(1)}, u32[]{:S(2)}, u32[]{:S(2)}) collective-permute-start(bf16[8,128,256]{2,1,0:T(8,128)(2,1)S(1)} %get-tuple-element.23), channel_id=1, source_target_pairs={{0,64},{64,0},{128,192},{192,128},{256,320},{320,256},{384,448},{4... | collective-permute-start | bytes 1572872 | tf_op jit(solution)/shard_map/ppermute | solution.py:326
  240.7 20.5 %copy-start = (f32[128,256]{1,0:T(8,128)S(1)}, f32[128,256]{1,0:T(8,128)}, u32[]{:S(2)}) copy-start(f32[128,256]{1,0:T(8,128)} %table_ref.1) | copy-start | bytes 393220
  261.2 0.7 copy-start.9

commit v2 on v1

v2 whole, which is shorter than its diff:
```python
import functools

import jax
import jax.numpy as jnp
from jax import lax
from jax.experimental import pallas as pl
from jax.experimental.pallas import tpu as pltpu
from jax.sharding import PartitionSpec as P

CAP = 2
LANES = 128
CORES = 2

learn_rate = 0.3
epsilon = 1e-06
sharpness = 3.0

VMEM = pl.BlockSpec(memory_space=pltpu.VMEM)
SMEM = pl.BlockSpec(memory_space=pltpu.SMEM)

NT = (((1,), (1,)), ((), ()))
TN = (((0,), (0,)), ((), ()))


def iota(shape, axis):
    return lax.broadcasted_iota(jnp.int32, shape, axis)


def dot(a, b, dims=(((1,), (0,)), ((), ()))):
    return lax.dot_general(a, b, dims, preferred_element_type=jnp.float32)


def hits(a, b):
    return jnp.where(a == b, 1.0, 0.0)


def call(body, out_shape, in_specs, scratch=(), out_specs=None):
    return pl.pallas_call(
        body,
        out_shape=out_shape,
        in_specs=in_specs,
        out_specs=jax.tree.map(lambda _: VMEM, out_shape) if out_specs is None else out_specs,
        scratch_shapes=list(scratch),
        compiler_params=pltpu.CompilerParams(vmem_limit_bytes=24 * 1024 * 1024),
    )


def request_body(
    core_ref, list_ref, counts_ref, item_refs, query_refs, req_ref, pos_ref, looked, counts2d, square, *, base
):
    length, owners = list_ref.shape[1], counts_ref.shape[1]
    rows = owners // LANES
    depth = looked.shape[0] // 2
    groups, slots = pos_ref.shape
    looked[...] = jnp.zeros_like(looked)
    for b in range(length // LANES):
        looked[b : b + 1, :] = list_ref[:, b * LANES : (b + 1) * LANES].astype(jnp.float32)
    for b in range(rows):
        counts2d[b : b + 1, :] = counts_ref[:, b * LANES : (b + 1) * LANES].astype(jnp.float32)
    down = iota((LANES, LANES), 0)
    block = iota((depth, LANES), 0)
    wanted = jnp.zeros((depth, LANES), jnp.float32)
    for refs_ref in (item_refs, query_refs):
        for l in range(refs_ref.shape[0]):
            ref = refs_ref[l : l + 1, :]
            high = hits(block, ref >> 7).astype(jnp.bfloat16)
            low = hits(down, ref & (LANES - 1)).astype(jnp.bfloat16)
            wanted = wanted + dot(high, low, NT)
    looked[depth:, :] = jnp.where(wanted > 0.5, 1.0, 0.0)
    looked_bf = looked[...].astype(jnp.bfloat16)

    counts = counts2d[...]
    counts_bf = counts.astype(jnp.bfloat16)
    before = hits(down < iota((LANES, LANES), 1), True).astype(jnp.bfloat16)
    within = dot(counts_bf, before)
    row_total = dot(counts_bf, jnp.ones((LANES, LANES), jnp.bfloat16))
    offsets = [jnp.zeros((1, LANES), jnp.float32)]
    for i in range(rows - 1):
        offsets.append(offsets[-1] + row_total[i : i + 1, :])
    starts = within + jnp.concatenate(offsets, axis=0)
    second = jnp.where(counts > 1.5, starts + 1.0, -1.0)
    positions = jnp.concatenate([starts, second], axis=0)
    pos_int = positions.astype(jnp.int32)
    entries = CAP * rows
    width = LANES // CORES
    owner_core = jnp.where(iota((1, LANES), 1) < width, 0, 1)
    side = jnp.where(owner_core == core_ref[0], 0.0, 1.0)
    square[...] = jnp.zeros_like(square)
    square[entries : 2 * entries, :] = positions
    for r in range(entries):
        p = pos_int[r : r + 1, :]
        spread = dot(looked_bf, hits(down, p & (LANES - 1)).astype(jnp.bfloat16))
        here = block == (p >> 7)
        value = jnp.sum(jnp.where(here, spread[:depth], 0.0), axis=0, keepdims=True)
        used = jnp.sum(jnp.where(here, spread[depth:], 0.0), axis=0, keepdims=True)
        square[r : r + 1, :] = value + (side * rows + (r % rows)) * LANES
        square[2 * entries + r : 2 * entries + r + 1, :] = used
    turned = square[...].T

    def column(n):
        part = slice(n * entries, (n + 1) * entries)
        return jnp.concatenate([turned[:width, part], turned[width:, part]], axis=1)

    codes, places, used = column(0), column(1), column(2)
    before = hits(iota((slots, slots), 0) < iota((slots, slots), 1), True).astype(jnp.bfloat16)
    rank = dot(used.astype(jnp.bfloat16), before)
    rank = jnp.where(used > 0.5, rank, -1.0).astype(jnp.int32)
    slot = iota((groups, slots), 1)
    packed_codes = jnp.full((groups, slots), -1.0, jnp.float32)
    packed_places = packed_codes
    for k in range(slots):
        here = slot == rank[:, k : k + 1]
        packed_codes = jnp.where(here, codes[:, k : k + 1], packed_codes)
        packed_places = jnp.where(here, places[:, k : k + 1], packed_places)
    over = jnp.max(rank, axis=1, keepdims=True)
    over = jnp.max(over, axis=0, keepdims=True)
    over = jnp.where(over >= base, 1, 0)
    pos_ref[...] = packed_places.astype(jnp.int32)
    req_ref[:, :slots] = packed_codes.astype(jnp.int32)
    req_ref[:, slots:] = jnp.broadcast_to(over, (groups, req_ref.shape[1] - slots))


def pick_body(recv_ref, near_ref, far_ref, out_ref, over_ref, square, *, first, count, slots):
    groups = recv_ref.shape[0]
    chips, per, width = near_ref.shape
    square[...] = jnp.zeros_like(square)
    square[:groups, : recv_ref.shape[1]] = recv_ref[...].astype(jnp.float32)
    turned = square[...].T.astype(jnp.int32)
    over_ref[0] = jnp.max(turned[slots : slots + 1, :groups])
    lane = iota((count, LANES), 1)
    rows = jnp.concatenate(
        [near_ref[...].reshape(chips * per, width), far_ref[...].reshape(chips * per, width)], axis=0
    )
    step = 8
    for t in range(0, groups, step):
        hot = []
        for u in range(t, t + step):
            code = jnp.broadcast_to(turned[first : first + count, u : u + 1], (count, LANES))
            hot.append(
                jnp.concatenate(
                    [hits(lane + b * LANES, code) for b in range(rows.shape[0] // LANES)], axis=1
                )
            )
        hot = jnp.concatenate(hot, axis=0).astype(jnp.bfloat16)
        out_ref[t * count : (t + step) * count, :] = dot(hot, rows).astype(jnp.bfloat16)


def pair_weight(refs, pos):
    weight = hits(refs[:, 0:1], pos)
    for l in range(1, refs.shape[1]):
        weight = weight + hits(refs[:, l : l + 1], pos)
    return weight.astype(jnp.bfloat16)


def tower_body(
    pos_ref, more_pos_ref, item_refs, query_refs, fetched, more_fetched, item_w, query_w,
    hits_ref, more_hits_ref, normed_ref, factor_ref, out_ref, square,
):
    pairs = item_refs.shape[1]
    square[...] = jnp.zeros_like(square)
    square[0 : item_refs.shape[0], :] = item_refs[...].astype(jnp.float32)
    square[8 : 8 + query_refs.shape[0], :] = query_refs[...].astype(jnp.float32)
    turned = square[...].T.astype(jnp.int32)
    item_columns = turned[:, 0 : item_refs.shape[0]]
    query_columns = turned[:, 8 : 8 + query_refs.shape[0]]
    outs = []
    for side, (refs, w_ref) in enumerate(((item_columns, item_w), (query_columns, query_w))):
        span = pl.ds(side * pairs, pairs)
        weight = pair_weight(refs, pos_ref[...])
        more_weight = pair_weight(refs, more_pos_ref[...])
        hits_ref[span, :] = weight
        more_hits_ref[span, :] = more_weight
        pool = (dot(weight, fetched[...]) + dot(more_weight, more_fetched[...])).astype(jnp.bfloat16)
        hidden = dot(pool, w_ref[...])
        factor = lax.rsqrt(jnp.mean(hidden * hidden, axis=1, keepdims=True) + epsilon)
        normed = hidden * factor
        normed_ref[span, :] = normed
        factor_ref[span, :] = jnp.broadcast_to(factor, (pairs, LANES))
        outs.append(normed.astype(jnp.bfloat16))
    for y in range(out_ref.shape[0]):
        out_ref[y, :pairs, :] = outs[0]
        out_ref[y, pairs:, :] = outs[1]


def scale_of(width):
    return sharpness * width ** (-0.5)


def near_body(near, sums_ref):
    chips, both, width = near.shape
    pairs = both // 2
    for y in range(0, chips, 2):
        q = jnp.concatenate([near[y, pairs:, :], near[y + 1, pairs:, :]], axis=0)
        total = jnp.zeros((8, both), jnp.float32)
        for j in range(0, chips, 2):
            items = jnp.concatenate([near[j, :pairs, :], near[j + 1, :pairs, :]], axis=0)
            e = jnp.exp(dot(items, q, NT) * scale_of(width))
            total = total + jnp.sum(e.reshape(both // 8, 8, both), axis=0)
        total = jnp.sum(total, axis=0, keepdims=True)
        sums_ref[y] = total[:, :pairs]
        sums_ref[y + 1] = total[:, pairs:]


def loss_body(
    y_ref, near, far, near_sums, normed_ref, factor_ref, item_w, query_w, hits_ref, more_hits_ref,
    loss_ref, grads_ref, more_grads_ref, inverse, own_exp,
):
    chips, both, width = near.shape
    pairs = both // 2
    scale = scale_of(width)
    own = y_ref[0]

    def items(y):
        return jnp.concatenate([near[y, :pairs, :], far[y, :pairs, :]], axis=0)

    def queries(y):
        return jnp.concatenate([near[y, pairs:, :], far[y, pairs:, :]], axis=0)

    def denominators(h, carry):
        y = 2 * h
        q = jnp.concatenate([queries(y), queries(y + 1)], axis=0)
        far_q = jnp.concatenate([far[y, pairs:, :], far[y + 1, pairs:, :]], axis=0)
        total = jnp.zeros((8, 2 * both), jnp.float32)
        far_total = jnp.zeros((8, both), jnp.float32)
        for j in range(0, chips, 2):
            far_items = jnp.concatenate([far[j, :pairs, :], far[j + 1, :pairs, :]], axis=0)
            near_items = jnp.concatenate([near[j, :pairs, :], near[j + 1, :pairs, :]], axis=0)
            e = jnp.exp(dot(far_items, q, NT) * scale)
            total = total + jnp.sum(e.reshape(both // 8, 8, 2 * both), axis=0)
            e = jnp.exp(dot(near_items, far_q, NT) * scale)
            far_total = far_total + jnp.sum(e.reshape(both // 8, 8, both), axis=0)
        total = jnp.sum(total, axis=0, keepdims=True)
        far_total = jnp.sum(far_total, axis=0, keepdims=True)
        for u in range(2):
            inverse[y + u] = jnp.concatenate(
                [
                    total[:, u * both : u * both + pairs] + near_sums[y + u],
                    total[:, u * both + pairs : (u + 1) * both] + far_total[:, u * pairs : (u + 1) * pairs],
                ],
                axis=1,
            )
        return carry

    lax.fori_loop(0, chips // 2, denominators, 0)
    item_own, query_own = near[own, :pairs, :], near[own, pairs:, :]
    own_hits = iota((pairs, pairs), 0) == iota((pairs, pairs), 1)
    diagonal = jnp.sum(
        jnp.where(own_hits, dot(item_own, query_own, NT) * scale, 0.0), axis=0, keepdims=True
    )
    loss_ref[...] = jnp.log(inverse[own][:, :pairs]) - diagonal
    ones = hits(iota((pairs, both), 0), iota((pairs, both), 1))
    grad_item = jnp.zeros((pairs, width), jnp.float32)
    row_total = jnp.zeros((pairs, LANES), jnp.float32)
    for y in range(chips):
        q = queries(y)
        soft = jnp.exp(dot(item_own, q, NT) * scale) * (1.0 / inverse[y])
        soft = soft - jnp.where(own == y, ones, 0.0)
        grad_item = grad_item + dot(soft.astype(jnp.bfloat16), q)
        e = jnp.exp(dot(query_own, items(y), NT) * scale)
        own_exp[y] = e
        for b in range(both // LANES):
            row_total = row_total + e[:, b * LANES : (b + 1) * LANES]
    row_inverse = 1.0 / jnp.sum(row_total, axis=1, keepdims=True)
    grad_query = jnp.zeros((pairs, width), jnp.float32)
    for y in range(chips):
        soft = own_exp[y] * row_inverse - jnp.where(own == y, ones, 0.0)
        grad_query = grad_query + dot(soft.astype(jnp.bfloat16), items(y))
    backs = []
    for side, (grad, w_ref) in enumerate(((grad_item, item_w), (grad_query, query_w))):
        span = pl.ds(side * pairs, pairs)
        grad = grad * scale
        normed = normed_ref[span, :]
        factor = factor_ref[span, 0:1]
        inner_mean = jnp.mean(grad * normed, axis=1, keepdims=True)
        grad_hidden = (factor * (grad - normed * inner_mean)).astype(jnp.bfloat16)
        backs.append(dot(grad_hidden, w_ref[...], NT))
    back = jnp.concatenate(backs, axis=0)
    high = back.astype(jnp.bfloat16)
    low = (back - high.astype(jnp.float32)).astype(jnp.bfloat16)
    step = 256
    for weights, out in ((hits_ref, grads_ref), (more_hits_ref, more_grads_ref)):
        for s in range(weights.shape[1] // step):
            weight = weights[:, s * step : (s + 1) * step]
            out[s * step : (s + 1) * step, :] = (
                dot(weight, high, TN) + dot(weight, low, TN)
            ).astype(jnp.bfloat16)


def column_body(codes_ref, more_codes_ref, grads_ref, more_grads_ref, out_ref, *, side):
    chips, per = out_ref.shape[:2]
    for y in range(0, chips, 2):
        begin = (side * chips + y) * per
        total = None
        for codes, grads in ((codes_ref, grads_ref), (more_codes_ref, more_grads_ref)):
            down = iota((2 * per, codes.shape[1]), 0)
            hot = hits(down, codes[...] - begin).astype(jnp.bfloat16)
            part = dot(hot, grads[...])
            total = part if total is None else total + part
        out_ref[y] = total[:per].astype(out_ref.dtype)
        out_ref[y + 1] = total[per:].astype(out_ref.dtype)


def add_body(a_ref, b_ref, out_ref):
    out_ref[...] = (a_ref[...] + b_ref[...].astype(jnp.float32)).astype(jnp.bfloat16)


def adagrad_body(parts_ref, table_ref, accum_ref, new_table_ref, new_accum_ref):
    grad = parts_ref[0].astype(jnp.float32)
    for y in range(1, parts_ref.shape[0]):
        grad = grad + parts_ref[y].astype(jnp.float32)
    rows, width = grad.shape
    mean = jnp.sum(grad * grad, axis=1, keepdims=True) * (1.0 / width)
    across = jnp.sum(
        jnp.where(iota((rows, rows), 0) == iota((rows, rows), 1), mean, 0.0), axis=0, keepdims=True
    )
    down = jnp.sum(
        jnp.where(iota((rows, rows), 0) == iota((rows, rows), 1), accum_ref[...], 0.0),
        axis=1,
        keepdims=True,
    )
    new_accum_ref[...] = accum_ref[...] + across
    new_table_ref[...] = table_ref[...] - learn_rate * grad / jnp.sqrt(down + mean)


def on_device(
    table, accum, item_weight, query_weight, packed_rows, block_counts, item_refs, query_refs
):
    bf16, f32, i32 = jnp.bfloat16, jnp.float32, jnp.int32
    shape = jax.ShapeDtypeStruct
    n_dp, n_table = lax.axis_size("dp"), lax.axis_size("table")
    chips = n_dp // CORES
    per, width = table.shape
    pairs = item_refs.shape[2]
    slots = CAP * n_dp
    base = slots * 3 // 4
    more = slots - base
    replica = lax.axis_index("dp")
    core = (replica % CORES).reshape(1).astype(i32)
    chip = (replica // CORES).reshape(1).astype(i32)
    along_y = [[y * CORES + c for y in range(chips)] for c in range(CORES)]
    swap = [(r, r ^ 1) for r in range(n_dp)]

    def over_y(x):
        return lax.all_to_all(
            x, "dp", split_axis=0, concat_axis=0, axis_index_groups=along_y, tiled=True
        )

    def over_table(x):
        parts = x.reshape(n_table, -1, x.shape[-1])
        return lax.all_to_all(parts, "table", split_axis=0, concat_axis=0, tiled=True).reshape(x.shape)

    near_rows = over_y(jnp.broadcast_to(table.astype(bf16)[None], (chips, per, width)))
    far_rows = lax.ppermute(near_rows, "dp", swap)
    items, queries = item_refs[0, 0].T, query_refs[0, 0].T
    requests, places = call(
        functools.partial(request_body, base=base),
        (shape((n_table, slots + 8), i32), shape((n_table, slots), i32)),
        [SMEM] + [VMEM] * 4,
        [
            pltpu.VMEM((32, LANES), f32),
            pltpu.VMEM((n_dp * n_table // LANES, LANES), f32),
            pltpu.VMEM((LANES, LANES), f32),
        ],
    )(core, packed_rows.reshape(1, -1), block_counts.reshape(1, -1), items, queries)
    received = over_table(requests)

    def pick(first, count):
        return call(
            functools.partial(pick_body, first=first, count=count, slots=slots),
            (shape((n_table * count, width), bf16), shape((1,), i32)),
            [VMEM] * 3,
            [pltpu.VMEM((LANES, LANES), f32)],
            out_specs=(VMEM, SMEM),
        )(received, near_rows, far_rows)

    picked, over = pick(0, base)
    fetched = over_table(picked)
    crowded = over[0] > 0
    nothing = jnp.zeros((n_table * more, width), bf16)
    more_fetched = lax.cond(
        crowded, lambda: over_table(pick(base, more)[0]), lambda: nothing
    )
    pair_hits, more_hits, normed, factor, spread = call(
        tower_body,
        (
            shape((2 * pairs, n_table * base), bf16),
            shape((2 * pairs, n_table * more), bf16),
            shape((2 * pairs, width), f32),
            shape((2 * pairs, LANES), f32),
            shape((chips, 2 * pairs, width), bf16),
        ),
        [VMEM] * 8,
        [pltpu.VMEM((LANES, LANES), f32)],
    )(
        places[:, :base].reshape(1, -1),
        places[:, base:].reshape(1, -1),
        items,
        queries,
        fetched,
        more_fetched,
        item_weight,
        query_weight,
    )
    near = over_y(spread)
    far = lax.ppermute(near, "dp", swap)
    near_sums = call(near_body, shape((chips, 1, pairs), f32), [VMEM])(near)
    loss, grads, more_grads = call(
        loss_body,
        (
            shape((1, pairs), f32),
            shape((n_table * base, width), bf16),
            shape((n_table * more, width), bf16),
        ),
        [SMEM] + [VMEM] * 9,
        [pltpu.VMEM((chips, 1, 2 * pairs), f32), pltpu.VMEM((chips, pairs, 2 * pairs), f32)],
    )(chip, near, far, near_sums, normed, factor, item_weight, query_weight, pair_hits, more_hits)
    returned = over_table(grads)
    more_returned = lax.cond(crowded, lambda: over_table(more_grads), lambda: nothing)
    codes = received[:, :base].reshape(1, -1)
    more_codes = received[:, base:slots].reshape(1, -1)

    def column(side, dtype):
        return call(
            functools.partial(column_body, side=side), shape((chips, per, width), dtype), [VMEM] * 4
        )(codes, more_codes, returned, more_returned)

    other = lax.ppermute(column(1, bf16), "dp", swap)
    both = call(add_body, shape((chips, per, width), bf16), [VMEM] * 2)(column(0, f32), other)
    new_table, new_accum = call(
        adagrad_body, (shape((per, width), f32), shape((1, per), f32)), [VMEM] * 3
    )(over_y(both), table, accum.reshape(1, per))
    return (new_table, new_accum.reshape(per), loss.reshape(1, 1, pairs))


def solution(mesh):
    in_specs = (
        P(("dp", "table"), None),
        P(("dp", "table")),
        P(),
        P(),
        P("dp", "table", None),
        P("dp", "table", None),
        P("dp", "table", None, None),
        P("dp", "table", None, None),
    )
    out_specs = (P(("dp", "table"), None), P(("dp", "table")), P("dp", "table", None))
    return jax.shard_map(
        on_device, mesh=mesh, in_specs=in_specs, out_specs=out_specs, check_vma=False
    )
```

time: 263 us -> 241 us (0.916)
  blocking collectives: 157 us -> 65.5 us
  waiting for transfers between devices: 53.5 us -> 93.2 us
  starting transfers between devices: 32 us -> 59.8 us
  Pallas kernels: 14 us -> 16.9 us
    all_to_all x5 -> x3, blocking collectives: 157 us -> 65.5 us  [over_y(): lax.all_to_all(x, 'dp', split_axis=0, concat_axis=0, axis_index_groups=al...]
    all_to_all x1 -> x3, waiting for transfers between devices: 49.7 us -> 91.7 us  [over_table(): lax.all_to_all(parts, 'table', split_axis=0, concat_axis=0, tiled=True)]
    all_to_all x1 -> x3, starting transfers between devices: 4.78 us -> 33.3 us  [over_table(): lax.all_to_all(parts, 'table', split_axis=0, concat_axis=0, tiled=True)]
    pallas_call x6 -> x8, Pallas kernels: 13.2 us -> 16.1 us  [the longest x1 5.76 us: on_device(): call(loss_body, (shape((1, pairs), f32), shape((n_table * base, width), b...]
  transfers between devices with their start and end apart: 4 -> 6, of which waited for: 3 -> 5; matrix products, arithmetic and copies ran while one was open for 0% -> 0% of each run, Pallas kernels for 0% -> 2%
where the time goes in v2:
time: 241 us
  waiting for transfers between devices  93.2 us (39%)
  blocking collectives  65.5 us (27%)
  starting transfers between devices  59.8 us (25%)
  Pallas kernels  16.9 us (7%)
  local copies, waits for them, and re-layouts  2.66 us (1%)
    all_to_all x3, waiting for transfers between devices, over_table(): lax.all_to_all(parts, 'table', split_axis=0, concat_axis=0, tiled=True)  91.7 us
    all_to_all x3, blocking collectives, over_y(): lax.all_to_all(x, 'dp', split_axis=0, concat_axis=0, axis_index_groups=al...  65.5 us
    all_to_all x3, starting transfers between devices, over_table(): lax.all_to_all(parts, 'table', split_axis=0, concat_axis=0, tiled=True)  33.3 us
    ppermute x1, starting transfers between devices, on_device(): far_rows = lax.ppermute(near_rows, 'dp', swap)  12.2 us
    ppermute x1, starting transfers between devices, on_device(): far = lax.ppermute(near, 'dp', swap)  8.81 us
    pallas_call x1, Pallas kernels, on_device(): call(loss_body, (shape((1, pairs), f32), shape((n_table * base, width), b...  5.76 us
    ppermute x1, starting transfers between devices, on_device(): other = lax.ppermute(column(1, bf16), 'dp', swap)  5.53 us
  transfers between devices with their start and end apart: 6, of which 5 were waited for; matrix products, arithmetic and copies ran while one was open for 0% of the time, Pallas kernels for 2%

profile of v2, /device:TPU:1, one launch (start us, length us, event | category | flops | bytes accessed | tf_op | source)
XLA Modules:
  0.0 240.5 jit_solution(7753157180423257747)
XLA Ops:
  0.6 0.9 convert_element_type.10
  1.6 19.6 %all_to_all.40.near_ref = bf16[8,128,256]{2,1,0:T(8,128)(2,1)S(1)} all-to-all(bf16[8,128,256]{2,1,0:T(8,128)(2,1)S(1)} %broadcast_in_dim.12), channel_id=1, replica_groups={{0,128,256,384,512,640,768,896},{64,192,320,448,576,704,832,960},{1,129..., dimensions={0} | all-to-all | bytes 1048576 | tf_op jit(solution)/shard_map/all_to_all | solution.py:344
  21.2 12.2 %collective-permute-start = (bf16[8,128,256]{2,1,0:T(8,128)(2,1)S(1)}, bf16[8,128,256]{2,1,0:T(8,128)(2,1)S(1)}, u32[]{:S(2)}, u32[]{:S(2)}) collective-permute-start(bf16[8,128,256]{2,1,0:T(8,128)(2,1)S(1)} %all_to_all.40.near_ref), channel_id=1, source_target_pairs={{0,64},{64,0},{128,192},{192,128},{256,320},{320,256},{384,448},{4... | collective-permute-start | bytes 1572872 | tf_op jit(solution)/shard_map/ppermute | solution.py:353
  33.4 0.6 copy-done.8
  34.1 2.8 %shard_map.103 = (s32[64,40]{1,0:T(8,128)}, s32[64,32]{1,0:T(8,128)S(1)}) custom-call(s32[1]{0:T(128)} %bitcast.4.core_ref, s32[1,1536]{1,0:T(1,128)S(1)} %bitcast.37, s32[1,1024]{1,0:T(1,128)S(1)} %bitcast.38, s32[4,128]{1,0:T(4,128)S(1)} %bitcast.33, s32[4,128]{1,0:T(4,128)S(1)} %bitcast.35), custom_call_target="tpu_custom_call" | custom-call | tf_op jit(solution)/shard_map/pallas_call | solution.py:355
  36.9 18.0 %all-to-all-start.2 = ((s32[64,1,40]{2,1,0:T(1,128)}), s32[64,1,40]{2,1,0:T(1,128)S(1)}, u32[]{:S(2)}, u32[]{:S(2)}) async-start(s32[64,1,40]{2,1,0:T(1,128)} %bitcast.12), calls=%async_computation.2 | async-start | bytes 65536 | tf_op jit(solution)/shard_map/all_to_all | solution.py:350
  54.9 13.2 %all-to-all-done.2 = s32[64,1,40]{2,1,0:T(1,128)S(1)} async-done(((s32[64,1,40]{2,1,0:T(1,128)}), s32[64,1,40]{2,1,0:T(1,128)S(1)}, u32[]{:S(2)}, u32[]{:S(2)}) %all-to-all-start.2) | async-done | bytes 10272 | tf_op jit(solution)/shard_map/all_to_all | solution.py:350
  68.1 2.9 %shard_map.104 = (bf16[1536,256]{1,0:T(8,128)(2,1)}, s32[1]{0:T(128)}) custom-call(s32[64,40]{1,0:T(8,128)S(1)} %bitcast.42, bf16[8,128,256]{2,1,0:T(8,128)(2,1)S(1)} %all_to_all.40.near_ref, bf16[8,128,256]{2,1,0:T(8,128)(2,1)S(1)} %collective-permute-done.far_ref), custom_call_target="tpu_custom_call" | custom-call | tf_op jit(solution)/shard_map/pallas_call | solution.py:368
  71.7 4.8 %all-to-all-start.4 = ((bf16[64,24,256]{2,1,0:T(8,128)(2,1)}), bf16[64,24,256]{2,1,0:T(8,128)(2,1)S(1)}, u32[]{:S(2)}, u32[]{:S(2)}) async-start(bf16[64,24,256]{2,1,0:T(8,128)(2,1)} %bitcast.17), calls=%async_computation.4 | async-start | bytes 1572864 | tf_op jit(solution)/shard_map/all_to_all | solution.py:350
  76.5 0.1 slice.15
  76.6 0.1 reshape.82.pos_ref
  76.7 0.1 reshape.83.more_pos_ref
  76.7 38.5 %all-to-all-done.4 = bf16[64,24,256]{2,1,0:T(8,128)(2,1)S(1)} async-done(((bf16[64,24,256]{2,1,0:T(8,128)(2,1)}), bf16[64,24,256]{2,1,0:T(8,128)(2,1)S(1)}, u32[]{:S(2)}, u32[]{:S(2)}) %all-to-all-start.4) | async-done | bytes 786464 | tf_op jit(solution)/shard_map/all_to_all | solution.py:350
  115.2 1.3 shard_map.105
  116.6 0.7 copy-done.3
  117.3 25.4 %all_to_all.41.near = bf16[8,256,256]{2,1,0:T(8,128)(2,1)S(1)} all-to-all(bf16[8,256,256]{2,1,0:T(8,128)(2,1)S(1)} %get-tuple-element.38), channel_id=1, replica_groups={{0,128,256,384,512,640,768,896},{64,192,320,448,576,704,832,960},{1,129..., dimensions={0} | all-to-all | bytes 2097152 | tf_op jit(solution)/shard_map/all_to_all | solution.py:344
  142.6 8.8 %collective-permute-start.1 = (bf16[8,256,256]{2,1,0:T(8,128)(2,1)S(1)}, bf16[8,256,256]{2,1,0:T(8,128)(2,1)S(1)}, u32[]{:S(2)}, u32[]{:S(2)}) collective-permute-start(bf16[8,256,256]{2,1,0:T(8,128)(2,1)S(1)} %all_to_all.41.near), channel_id=1, source_target_pairs={{0,64},{64,0},{128,192},{192,128},{256,320},{320,256},{384,448},{4... | collective-permute-start | bytes 3145736 | tf_op jit(solution)/shard_map/ppermute | solution.py:405
  151.5 0.8 shard_map.106.near_sums
  152.2 1.3 collective-permute-done.1.far
  153.5 5.8 %shard_map.107 = (f32[1,128]{1,0:T(1,128)}, bf16[1536,256]{1,0:T(8,128)(2,1)}, bf16[512,256]{1,0:T(8,128)(2,1)}) custom-call(s32[1]{0:T(128)} %bitcast.14.y_ref, bf16[8,256,256]{2,1,0:T(8,128)(2,1)S(1)} %all_to_all.41.near, bf16[8,256,256]{2,1,0:T(8,128)(2,1)S(1)} %collective-permute-done.1.far, f32[8,1,128]{2,1,0:T(1,128)S(1)} %shard_map.106.near_sums, ...), custom_call_target="tpu_custom_call" | custom-call | tf_op jit(solution)/shard_map/pallas_call | solution.py:407
  159.3 10.5 %all-to-all-start.6 = ((bf16[64,24,256]{2,1,0:T(8,128)(2,1)}), bf16[64,24,256]{2,1,0:T(8,128)(2,1)S(1)}, u32[]{:S(2)}, u32[]{:S(2)}) async-start(bf16[64,24,256]{2,1,0:T(8,128)(2,1)} %bitcast.20), calls=%async_computation.6 | async-start | bytes 1572864 | tf_op jit(solution)/shard_map/all_to_all | solution.py:350
  169.9 0.1 reshape.79.codes_ref
  170.0 0.1 reshape.80.more_codes_ref
  170.1 40.0 %all-to-all-done.6 = bf16[64,24,256]{2,1,0:T(8,128)(2,1)S(1)} async-done(((bf16[64,24,256]{2,1,0:T(8,128)(2,1)}), bf16[64,24,256]{2,1,0:T(8,128)(2,1)S(1)}, u32[]{:S(2)}, u32[]{:S(2)}) %all-to-all-start.6) | async-done | bytes 786464 | tf_op jit(solution)/shard_map/all_to_all | solution.py:350
  210.1 1.2 shard_map.109
  211.3 5.5 %collective-permute-start.2 = (bf16[8,128,256]{2,1,0:T(8,128)(2,1)S(1)}, bf16[8,128,256]{2,1,0:T(8,128)(2,1)S(1)}, u32[]{:S(2)}, u32[]{:S(2)}) collective-permute-start(bf16[8,128,256]{2,1,0:T(8,128)(2,1)S(1)} %shard_map.109), channel_id=1, source_target_pairs={{0,64},{64,0},{128,192},{192,128},{256,320},{320,256},{384,448},{4... | collective-permute-start | bytes 1572872 | tf_op jit(solution)/shard_map/ppermute | solution.py:427
  216.9 1.2 shard_map.108.a_ref
  218.1 0.3 collective-permute-done.2.b_ref
  218.4 0.1 shard_map.110
  218.5 20.5 %all_to_all.42.parts_ref = bf16[8,128,256]{2,1,0:T(8,128)(2,1)S(1)} all-to-all(bf16[8,128,256]{2,1,0:T(8,128)(2,1)S(1)} %shard_map.110), channel_id=1, replica_groups={{0,128,256,384,512,640,768,896},{64,192,320,448,576,704,832,960},{1,129..., dimensions={0} | all-to-all | bytes 1048576 | tf_op jit(solution)/shard_map/all_to_all | solution.py:344
  239.0 0.7 copy-done.9
  239.7 0.9 shard_map.111
  (28 shorter events, 0.3 us)
Async XLA Ops:
  21.2 46.9 %collective-permute-start = (bf16[8,128,256]{2,1,0:T(8,128)(2,1)S(1)}, bf16[8,128,256]{2,1,0:T(8,128)(2,1)S(1)}, u32[]{:S(2)}, u32[]{:S(2)}) collective-permute-start(bf16[8,128,256]{2,1,0:T(8,128)(2,1)S(1)} %all_to_all.40.near_ref), channel_id=1, source_target_pairs={{0,64},{64,0},{128,192},{192,128},{256,320},{320,256},{384,448},{4... | collective-permute-start | bytes 1572872 | tf_op jit(solution)/shard_map/ppermute | solution.py:353
  33.3 0.7 copy-start.8
  33.4 0.7 copy-start.7
  33.4 0.7 copy-start.6
  33.4 0.7 copy-start.5
  36.9 31.2 %all-to-all-start.2 = ((s32[64,1,40]{2,1,0:T(1,128)}), s32[64,1,40]{2,1,0:T(1,128)S(1)}, u32[]{:S(2)}, u32[]{:S(2)}) async-start(s32[64,1,40]{2,1,0:T(1,128)} %bitcast.12), calls=%async_computation.2 | async-start | bytes 65536 | tf_op jit(solution)/shard_map/all_to_all | solution.py:350
  68.1 3.5 %copy-start.10 = (s32[64,1,40]{2,1,0:T(1,128)}, s32[64,1,40]{2,1,0:T(1,128)S(1)}, u32[]{:S(2)}) copy-start(s32[64,1,40]{2,1,0:T(1,128)S(1)} %all-to-all-done.2) | copy-start | bytes 30724
  71.7 43.5 %copy-start.1 = (bf16[256,256]{1,0:T(8,128)(2,1)S(1)}, bf16[256,256]{1,0:T(8,128)(2,1)}, u32[]{:S(2)}) copy-start(bf16[256,256]{1,0:T(8,128)(2,1)} %query_w.3) | copy-start | bytes 393220
  71.7 43.5 %all-to-all-start.4 = ((bf16[64,24,256]{2,1,0:T(8,128)(2,1)}), bf16[64,24,256]{2,1,0:T(8,128)(2,1)S(1)}, u32[]{:S(2)}, u32[]{:S(2)}) async-start(bf16[64,24,256]{2,1,0:T(8,128)(2,1)} %bitcast.17), calls=%async_computation.4 | async-start | bytes 1572864 | tf_op jit(solution)/shard_map/all_to_all | solution.py:350
  76.5 38.7 %copy-start = (bf16[256,256]{1,0:T(8,128)(2,1)S(1)}, bf16[256,256]{1,0:T(8,128)(2,1)}, u32[]{:S(2)}) copy-start(bf16[256,256]{1,0:T(8,128)(2,1)} %item_w.3) | copy-start | bytes 393220
  116.6 0.7 copy-start.3
  142.6 10.9 %collective-permute-start.1 = (bf16[8,256,256]{2,1,0:T(8,128)(2,1)S(1)}, bf16[8,256,256]{2,1,0:T(8,128)(2,1)S(1)}, u32[]{:S(2)}, u32[]{:S(2)}) collective-permute-start(bf16[8,256,256]{2,1,0:T(8,128)(2,1)S(1)} %all_to_all.41.near), channel_id=1, source_target_pairs={{0,64},{64,0},{128,192},{192,128},{256,320},{320,256},{384,448},{4... | collective-permute-start | bytes 3145736 | tf_op jit(solution)/shard_map/ppermute | solution.py:405
  151.4 2.1 copy-start.4
  159.3 10.5 %copy-start.11 = (s32[64,1,40]{2,1,0:T(1,128)S(1)}, s32[64,1,40]{2,1,0:T(1,128)}, u32[]{:S(2)}) copy-start(s32[64,1,40]{2,1,0:T(1,128)} %copy-done.10) | copy-start | bytes 30724
  159.3 50.8 %all-to-all-start.6 = ((bf16[64,24,256]{2,1,0:T(8,128)(2,1)}), bf16[64,24,256]{2,1,0:T(8,128)(2,1)S(1)}, u32[]{:S(2)}, u32[]{:S(2)}) async-start(bf16[64,24,256]{2,1,0:T(8,128)(2,1)} %bitcast.20), calls=%async_computation.6 | async-start | bytes 1572864 | tf_op jit(solution)/shard_map/all_to_all | solution.py:350
  211.3 7.0 %collective-permute-start.2 = (bf16[8,128,256]{2,1,0:T(8,128)(2,1)S(1)}, bf16[8,128,256]{2,1,0:T(8,128)(2,1)S(1)}, u32[]{:S(2)}, u32[]{:S(2)}) collective-permute-start(bf16[8,128,256]{2,1,0:T(8,128)(2,1)S(1)} %shard_map.109), channel_id=1, source_target_pairs={{0,64},{64,0},{128,192},{192,128},{256,320},{320,256},{384,448},{4... | collective-permute-start | bytes 1572872 | tf_op jit(solution)/shard_map/ppermute | solution.py:427
  218.5 20.5 %copy-start.2 = (f32[128,256]{1,0:T(8,128)S(1)}, f32[128,256]{1,0:T(8,128)}, u32[]{:S(2)}) copy-start(f32[128,256]{1,0:T(8,128)} %table_ref.1) | copy-start | bytes 393220
  239.0 0.7 copy-start.9

commit v3 on v2

--- a/solution.py
+++ b/solution.py
@@ -1,4 +1,5 @@
 import functools
+import math
 
 import jax
 import jax.numpy as jnp
@@ -19,7 +20,6 @@
 SMEM = pl.BlockSpec(memory_space=pltpu.SMEM)
 
 NT = (((1,), (1,)), ((), ()))
-TN = (((0,), (0,)), ((), ()))
 
 
 def iota(shape, axis):
@@ -41,17 +41,19 @@
         in_specs=in_specs,
         out_specs=jax.tree.map(lambda _: VMEM, out_shape) if out_specs is None else out_specs,
         scratch_shapes=list(scratch),
-        compiler_params=pltpu.CompilerParams(vmem_limit_bytes=24 * 1024 * 1024),
+        compiler_params=pltpu.CompilerParams(vmem_limit_bytes=12 * 1024 * 1024),
     )
 
 
 def request_body(
-    core_ref, list_ref, counts_ref, item_refs, query_refs, req_ref, pos_ref, looked, counts2d, square, *, base
+    core_ref, list_ref, counts_ref, item_refs, query_refs, accum_ref,
+    req_ref, pos_ref, accum_out, looked, counts2d, square, *, base,
 ):
     length, owners = list_ref.shape[1], counts_ref.shape[1]
     rows = owners // LANES
     depth = looked.shape[0] // 2
     groups, slots = pos_ref.shape
+    accum_out[...] = accum_ref[...]
     looked[...] = jnp.zeros_like(looked)
     for b in range(length // LANES):
         looked[b : b + 1, :] = list_ref[:, b * LANES : (b + 1) * LANES].astype(jnp.float32)
@@ -145,6 +147,12 @@
         out_ref[t * count : (t + step) * count, :] = dot(hot, rows).astype(jnp.bfloat16)
 
 
+def project(pool, weight):
+    hidden = dot(pool, weight)
+    factor = lax.rsqrt(jnp.mean(hidden * hidden, axis=1, keepdims=True) + epsilon)
+    return hidden * factor, factor
+
+
 def pair_weight(refs, pos):
     weight = hits(refs[:, 0:1], pos)
     for l in range(1, refs.shape[1]):
@@ -153,8 +161,8 @@
 
 
 def tower_body(
-    pos_ref, more_pos_ref, item_refs, query_refs, fetched, more_fetched, item_w, query_w,
-    hits_ref, more_hits_ref, normed_ref, factor_ref, out_ref, square,
+    pos_ref, more_pos_ref, item_refs, query_refs, fetched, more_fetched, weights,
+    hits_ref, more_hits_ref, pool_ref, out_ref, square,
 ):
     pairs = item_refs.shape[1]
     square[...] = jnp.zeros_like(square)
@@ -164,19 +172,15 @@
     item_columns = turned[:, 0 : item_refs.shape[0]]
     query_columns = turned[:, 8 : 8 + query_refs.shape[0]]
     outs = []
-    for side, (refs, w_ref) in enumerate(((item_columns, item_w), (query_columns, query_w))):
+    for side, refs in enumerate((item_columns, query_columns)):
         span = pl.ds(side * pairs, pairs)
         weight = pair_weight(refs, pos_ref[...])
         more_weight = pair_weight(refs, more_pos_ref[...])
         hits_ref[span, :] = weight
         more_hits_ref[span, :] = more_weight
         pool = (dot(weight, fetched[...]) + dot(more_weight, more_fetched[...])).astype(jnp.bfloat16)
-        hidden = dot(pool, w_ref[...])
-        factor = lax.rsqrt(jnp.mean(hidden * hidden, axis=1, keepdims=True) + epsilon)
-        normed = hidden * factor
-        normed_ref[span, :] = normed
-        factor_ref[span, :] = jnp.broadcast_to(factor, (pairs, LANES))
-        outs.append(normed.astype(jnp.bfloat16))
+        pool_ref[span, :] = pool
+        outs.append(project(pool, weights[side])[0].astype(jnp.bfloat16))
     for y in range(out_ref.shape[0]):
         out_ref[y, :pairs, :] = outs[0]
         out_ref[y, pairs:, :] = outs[1]
@@ -186,15 +190,23 @@
     return sharpness * width ** (-0.5)
 
 
-def near_body(near, sums_ref):
+def exp_of(products, width):
+    return jnp.exp2(products * (scale_of(width) * math.log2(math.e)))
+
+
+def near_body(near, hits_ref, more_hits_ref, sums_ref, turned_ref, more_turned_ref):
     chips, both, width = near.shape
     pairs = both // 2
+    step = 256
+    for weights, out in ((hits_ref, turned_ref), (more_hits_ref, more_turned_ref)):
+        for s in range(0, weights.shape[1], step):
+            out[s : s + step, :] = weights[:, s : s + step].T
     for y in range(0, chips, 2):
         q = jnp.concatenate([near[y, pairs:, :], near[y + 1, pairs:, :]], axis=0)
         total = jnp.zeros((8, both), jnp.float32)
         for j in range(0, chips, 2):
             items = jnp.concatenate([near[j, :pairs, :], near[j + 1, :pairs, :]], axis=0)
-            e = jnp.exp(dot(items, q, NT) * scale_of(width))
+            e = exp_of(dot(items, q, NT), width)
             total = total + jnp.sum(e.reshape(both // 8, 8, both), axis=0)
         total = jnp.sum(total, axis=0, keepdims=True)
         sums_ref[y] = total[:, :pairs]
@@ -202,7 +214,7 @@
 
 
 def loss_body(
-    y_ref, near, far, near_sums, normed_ref, factor_ref, item_w, query_w, hits_ref, more_hits_ref,
+    y_ref, near, far, near_sums, pool_ref, weights_ref, turned_ref, more_turned_ref,
     loss_ref, grads_ref, more_grads_ref, inverse, own_exp,
 ):
     chips, both, width = near.shape
@@ -225,9 +237,9 @@
         for j in range(0, chips, 2):
             far_items = jnp.concatenate([far[j, :pairs, :], far[j + 1, :pairs, :]], axis=0)
             near_items = jnp.concatenate([near[j, :pairs, :], near[j + 1, :pairs, :]], axis=0)
-            e = jnp.exp(dot(far_items, q, NT) * scale)
+            e = exp_of(dot(far_items, q, NT), width)
             total = total + jnp.sum(e.reshape(both // 8, 8, 2 * both), axis=0)
-            e = jnp.exp(dot(near_items, far_q, NT) * scale)
+            e = exp_of(dot(near_items, far_q, NT), width)
             far_total = far_total + jnp.sum(e.reshape(both // 8, 8, both), axis=0)
         total = jnp.sum(total, axis=0, keepdims=True)
         far_total = jnp.sum(far_total, axis=0, keepdims=True)
@@ -241,7 +253,8 @@
             )
         return carry
 
-    lax.fori_loop(0, chips // 2, denominators, 0)
+    for h in range(chips // 2):
+        denominators(h, 0)
     item_own, query_own = near[own, :pairs, :], near[own, pairs:, :]
     own_hits = iota((pairs, pairs), 0) == iota((pairs, pairs), 1)
     diagonal = jnp.sum(
@@ -253,10 +266,10 @@
     row_total = jnp.zeros((pairs, LANES), jnp.float32)
     for y in range(chips):
         q = queries(y)
-        soft = jnp.exp(dot(item_own, q, NT) * scale) * (1.0 / inverse[y])
+        soft = exp_of(dot(item_own, q, NT), width) * (1.0 / inverse[y])
         soft = soft - jnp.where(own == y, ones, 0.0)
         grad_item = grad_item + dot(soft.astype(jnp.bfloat16), q)
-        e = jnp.exp(dot(query_own, items(y), NT) * scale)
+        e = exp_of(dot(query_own, items(y), NT), width)
         own_exp[y] = e
         for b in range(both // LANES):
             row_total = row_total + e[:, b * LANES : (b + 1) * LANES]
@@ -266,24 +279,22 @@
         soft = own_exp[y] * row_inverse - jnp.where(own == y, ones, 0.0)
         grad_query = grad_query + dot(soft.astype(jnp.bfloat16), items(y))
     backs = []
-    for side, (grad, w_ref) in enumerate(((grad_item, item_w), (grad_query, query_w))):
+    for side, grad in enumerate((grad_item, grad_query)):
         span = pl.ds(side * pairs, pairs)
         grad = grad * scale
-        normed = normed_ref[span, :]
-        factor = factor_ref[span, 0:1]
+        normed, factor = project(pool_ref[span, :], weights_ref[side])
         inner_mean = jnp.mean(grad * normed, axis=1, keepdims=True)
         grad_hidden = (factor * (grad - normed * inner_mean)).astype(jnp.bfloat16)
-        backs.append(dot(grad_hidden, w_ref[...], NT))
+        backs.append(dot(grad_hidden, weights_ref[side], NT))
     back = jnp.concatenate(backs, axis=0)
     high = back.astype(jnp.bfloat16)
     low = (back - high.astype(jnp.float32)).astype(jnp.bfloat16)
+    split = jnp.concatenate([high, low], axis=1)
     step = 256
-    for weights, out in ((hits_ref, grads_ref), (more_hits_ref, more_grads_ref)):
-        for s in range(weights.shape[1] // step):
-            weight = weights[:, s * step : (s + 1) * step]
-            out[s * step : (s + 1) * step, :] = (
-                dot(weight, high, TN) + dot(weight, low, TN)
-            ).astype(jnp.bfloat16)
+    for weights, out in ((turned_ref, grads_ref), (more_turned_ref, more_grads_ref)):
+        for s in range(0, weights.shape[0], step):
+            parts = dot(weights[s : s + step, :], split)
+            out[s : s + step, :] = (parts[:, :width] + parts[:, width:]).astype(jnp.bfloat16)
 
 
 def column_body(codes_ref, more_codes_ref, grads_ref, more_grads_ref, out_ref, *, side):
@@ -350,21 +361,23 @@
         return lax.all_to_all(parts, "table", split_axis=0, concat_axis=0, tiled=True).reshape(x.shape)
 
     near_rows = over_y(jnp.broadcast_to(table.astype(bf16)[None], (chips, per, width)))
-    far_rows = lax.ppermute(near_rows, "dp", swap)
+    tower_weights = jnp.stack([item_weight, query_weight])
     items, queries = item_refs[0, 0].T, query_refs[0, 0].T
-    requests, places = call(
+    requests, places, old_accum = call(
         functools.partial(request_body, base=base),
-        (shape((n_table, slots + 8), i32), shape((n_table, slots), i32)),
-        [SMEM] + [VMEM] * 4,
+        (shape((n_table, slots + 8), i32), shape((n_table, slots), i32), shape((1, per), f32)),
+        [SMEM] + [VMEM] * 5,
         [
             pltpu.VMEM((32, LANES), f32),
             pltpu.VMEM((n_dp * n_table // LANES, LANES), f32),
             pltpu.VMEM((LANES, LANES), f32),
         ],
-    )(core, packed_rows.reshape(1, -1), block_counts.reshape(1, -1), items, queries)
+    )(core, packed_rows.reshape(1, -1), block_counts.reshape(1, -1), items, queries, accum.reshape(1, per))
+    near_rows, requests = lax.optimization_barrier((near_rows, requests))
+    far_rows = lax.ppermute(near_rows, "dp", swap)
     received = over_table(requests)
 
-    def pick(first, count):
+    def pick(first, count, received):
         return call(
             functools.partial(pick_body, first=first, count=count, slots=slots),
             (shape((n_table * count, width), bf16), shape((1,), i32)),
@@ -373,23 +386,23 @@
             out_specs=(VMEM, SMEM),
         )(received, near_rows, far_rows)
 
-    picked, over = pick(0, base)
+    picked, over = pick(0, base, received)
     fetched = over_table(picked)
     crowded = over[0] > 0
     nothing = jnp.zeros((n_table * more, width), bf16)
+    late, fetched = lax.optimization_barrier((received, fetched))
     more_fetched = lax.cond(
-        crowded, lambda: over_table(pick(base, more)[0]), lambda: nothing
-    )
-    pair_hits, more_hits, normed, factor, spread = call(
+        crowded, lambda: over_table(pick(base, more, late)[0]), lambda: nothing
+    )
+    pair_hits, more_hits, pool, spread = call(
         tower_body,
         (
             shape((2 * pairs, n_table * base), bf16),
             shape((2 * pairs, n_table * more), bf16),
-            shape((2 * pairs, width), f32),
-            shape((2 * pairs, LANES), f32),
+            shape((2 * pairs, width), bf16),
             shape((chips, 2 * pairs, width), bf16),
         ),
-        [VMEM] * 8,
+        [VMEM] * 7,
         [pltpu.VMEM((LANES, LANES), f32)],
     )(
         places[:, :base].reshape(1, -1),
@@ -398,12 +411,19 @@
         queries,
         fetched,
         more_fetched,
-        item_weight,
-        query_weight,
+        tower_weights,
     )
     near = over_y(spread)
     far = lax.ppermute(near, "dp", swap)
-    near_sums = call(near_body, shape((chips, 1, pairs), f32), [VMEM])(near)
+    near_sums, turned_hits, more_turned_hits = call(
+        near_body,
+        (
+            shape((chips, 1, pairs), f32),
+            shape((n_table * base, 2 * pairs), bf16),
+            shape((n_table * more, 2 * pairs), bf16),
+        ),
+        [VMEM] * 3,
+    )(near, pair_hits, more_hits)
     loss, grads, more_grads = call(
         loss_body,
         (
@@ -411,9 +431,9 @@
             shape((n_table * base, width), bf16),
             shape((n_table * more, width), bf16),
         ),
-        [SMEM] + [VMEM] * 9,
+        [SMEM] + [VMEM] * 7,
         [pltpu.VMEM((chips, 1, 2 * pairs), f32), pltpu.VMEM((chips, pairs, 2 * pairs), f32)],
-    )(chip, near, far, near_sums, normed, factor, item_weight, query_weight, pair_hits, more_hits)
+    )(chip, near, far, near_sums, pool, tower_weights, turned_hits, more_turned_hits)
     returned = over_table(grads)
     more_returned = lax.cond(crowded, lambda: over_table(more_grads), lambda: nothing)
     codes = received[:, :base].reshape(1, -1)
@@ -428,7 +448,7 @@
     both = call(add_body, shape((chips, per, width), bf16), [VMEM] * 2)(column(0, f32), other)
     new_table, new_accum = call(
         adagrad_body, (shape((per, width), f32), shape((1, per), f32)), [VMEM] * 3
-    )(over_y(both), table, accum.reshape(1, per))
+    )(over_y(both), table, old_accum)
     return (new_table, new_accum.reshape(per), loss.reshape(1, 1, pairs))
 
 

time: 241 us -> 238 us (0.988)
  blocking collectives: 65.5 us -> 76.2 us
  starting transfers between devices: 59.8 us -> 50.2 us
  waiting for transfers between devices: 93.2 us -> 87.9 us
    all_to_all x0 -> x1, blocking collectives: none -> 30.3 us  [over_table(): lax.all_to_all(parts, 'table', split_axis=0, concat_axis=0, tiled=True)]
    all_to_all x3 -> x2, blocking collectives: 65.5 us -> 45.9 us  [over_y(): lax.all_to_all(x, 'dp', split_axis=0, concat_axis=0, axis_index_groups=al...]
    all_to_all x3 -> x2, starting transfers between devices: 33.3 us -> 15.3 us  [over_table(): lax.all_to_all(parts, 'table', split_axis=0, concat_axis=0, tiled=True)]
    all_to_all x3 -> x2, waiting for transfers between devices: 91.7 us -> 77.1 us  [over_table(): lax.all_to_all(parts, 'table', split_axis=0, concat_axis=0, tiled=True)]
    all_to_all x0 -> x1, waiting for transfers between devices: none -> 9.24 us  [over_y(): lax.all_to_all(x, 'dp', split_axis=0, concat_axis=0, axis_index_groups=al...]
    all_to_all x0 -> x1, starting transfers between devices: none -> 7.65 us  [over_y(): lax.all_to_all(x, 'dp', split_axis=0, concat_axis=0, axis_index_groups=al...]
where the time goes in v3:
time: 238 us; the launch traced here: 237 us
  waiting for transfers between devices  87.9 us (37%)
  blocking collectives  76.2 us (32%)
  starting transfers between devices  50.2 us (21%)
  Pallas kernels  16.6 us (7%)
  local copies, waits for them, and re-layouts  3.45 us (1%)
    all_to_all x2, waiting for transfers between devices, over_table(): lax.all_to_all(parts, 'table', split_axis=0, concat_axis=0, tiled=True)  77.1 us
    all_to_all x2, blocking collectives, over_y(): lax.all_to_all(x, 'dp', split_axis=0, concat_axis=0, axis_index_groups=al...  45.9 us
    all_to_all x1, blocking collectives, over_table(): lax.all_to_all(parts, 'table', split_axis=0, concat_axis=0, tiled=True)  30.3 us
    all_to_all x2, starting transfers between devices, over_table(): lax.all_to_all(parts, 'table', split_axis=0, concat_axis=0, tiled=True)  15.3 us
    ppermute x1, starting transfers between devices, on_device(): far_rows = lax.ppermute(near_rows, 'dp', swap)  13 us
    all_to_all x1, waiting for transfers between devices, over_y(): lax.all_to_all(x, 'dp', split_axis=0, concat_axis=0, axis_index_groups=al...  9.24 us
    ppermute x1, starting transfers between devices, on_device(): far = lax.ppermute(near, 'dp', swap)  8.81 us
    all_to_all x1, starting transfers between devices, over_y(): lax.all_to_all(x, 'dp', split_axis=0, concat_axis=0, axis_index_groups=al...  7.65 us
  transfers between devices with their start and end apart: 6, of which 5 were waited for; matrix products, arithmetic and copies ran while one was open for 0% of the time, Pallas kernels for 2%

profile of v3, /device:TPU:1, one launch (start us, length us, event | category | flops | bytes accessed | tf_op | source)
XLA Modules:
  0.0 236.8 jit_solution(1751251221566574187)
XLA Ops:
  0.6 0.9 convert_element_type.10
  1.5 0.8 broadcast_in_dim.12
  2.4 7.7 %all-to-all-start.2 = ((bf16[8,128,256]{2,1,0:T(8,128)(2,1)}), bf16[8,128,256]{2,1,0:T(8,128)(2,1)S(1)}, u32[]{:S(2)}, u32[]{:S(2)}) async-start(bf16[8,128,256]{2,1,0:T(8,128)(2,1)} %broadcast_in_dim.12), calls=%async_computation.2 | async-start | bytes 1048576 | tf_op jit(solution)/shard_map/all_to_all | solution.py:355
  10.1 0.6 copy-done.4
  10.8 2.2 shard_map.103
  12.9 9.2 %all-to-all-done.2.near_ref = bf16[8,128,256]{2,1,0:T(8,128)(2,1)S(1)} async-done(((bf16[8,128,256]{2,1,0:T(8,128)(2,1)}), bf16[8,128,256]{2,1,0:T(8,128)(2,1)S(1)}, u32[]{:S(2)}, u32[]{:S(2)}) %all-to-all-start.2) | async-done | bytes 524320 | tf_op jit(solution)/shard_map/all_to_all | solution.py:355
  22.2 13.0 %collective-permute-start = (bf16[8,128,256]{2,1,0:T(8,128)(2,1)S(1)}, bf16[8,128,256]{2,1,0:T(8,128)(2,1)S(1)}, u32[]{:S(2)}, u32[]{:S(2)}) collective-permute-start(bf16[8,128,256]{2,1,0:T(8,128)(2,1)S(1)} %all-to-all-done.2.near_ref), channel_id=1, source_target_pairs={{0,64},{64,0},{128,192},{192,128},{256,320},{320,256},{384,448},{4... | collective-permute-start | bytes 1572872 | tf_op jit(solution)/shard_map/ppermute | solution.py:377
  35.2 30.3 %all_to_all.40 = s32[64,1,40]{2,1,0:T(1,128)S(1)} all-to-all(s32[64,1,40]{2,1,0:T(1,128)S(1)} %bitcast.35), channel_id=1, replica_groups=mesh['dp'=16,'table'=64] {'table'}, dimensions={0} | all-to-all | bytes 20480 | tf_op jit(solution)/shard_map/all_to_all | solution.py:361
  65.4 2.9 %shard_map.104 = (bf16[1536,256]{1,0:T(8,128)(2,1)}, s32[1]{0:T(128)}) custom-call(s32[64,40]{1,0:T(8,128)S(1)} %bitcast.44, bf16[8,128,256]{2,1,0:T(8,128)(2,1)S(1)} %all-to-all-done.2.near_ref, bf16[8,128,256]{2,1,0:T(8,128)(2,1)S(1)} %collective-permute-done.far_ref), custom_call_target="tpu_custom_call" | custom-call | tf_op jit(solution)/shard_map/pallas_call | solution.py:381
  68.3 4.8 %all-to-all-start.4 = ((bf16[64,24,256]{2,1,0:T(8,128)(2,1)}), bf16[64,24,256]{2,1,0:T(8,128)(2,1)S(1)}, u32[]{:S(2)}, u32[]{:S(2)}) async-start(bf16[64,24,256]{2,1,0:T(8,128)(2,1)} %bitcast.18), calls=%async_computation.4 | async-start | bytes 1572864 | tf_op jit(solution)/shard_map/all_to_all | solution.py:361
  73.2 0.1 reshape.83.pos_ref
  73.3 0.1 reshape.84.more_pos_ref
  73.4 0.6 copy-done.8
  74.7 37.1 %all-to-all-done.4 = bf16[64,24,256]{2,1,0:T(8,128)(2,1)S(1)} async-done(((bf16[64,24,256]{2,1,0:T(8,128)(2,1)}), bf16[64,24,256]{2,1,0:T(8,128)(2,1)S(1)}, u32[]{:S(2)}, u32[]{:S(2)}) %all-to-all-start.4) | async-done | bytes 786464 | tf_op jit(solution)/shard_map/all_to_all | solution.py:361
  111.8 0.7 conditional.2
  111.8 0.7 broadcast_in_dim.1
  112.6 2.3 shard_map.105
  114.9 25.4 %all_to_all.41.near = bf16[8,256,256]{2,1,0:T(8,128)(2,1)S(1)} all-to-all(bf16[8,256,256]{2,1,0:T(8,128)(2,1)S(1)} %get-tuple-element.49), channel_id=1, replica_groups={{0,128,256,384,512,640,768,896},{64,192,320,448,576,704,832,960},{1,129..., dimensions={0} | all-to-all | bytes 2097152 | tf_op jit(solution)/shard_map/all_to_all | solution.py:355
  140.2 8.8 %collective-permute-start.1 = (bf16[8,256,256]{2,1,0:T(8,128)(2,1)S(1)}, bf16[8,256,256]{2,1,0:T(8,128)(2,1)S(1)}, u32[]{:S(2)}, u32[]{:S(2)}) collective-permute-start(bf16[8,256,256]{2,1,0:T(8,128)(2,1)S(1)} %all_to_all.41.near), channel_id=1, source_target_pairs={{0,64},{64,0},{128,192},{192,128},{256,320},{320,256},{384,448},{4... | collective-permute-start | bytes 3145736 | tf_op jit(solution)/shard_map/ppermute | solution.py:417
  149.1 0.8 shard_map.106
  149.9 1.2 collective-permute-done.1.far
  151.1 5.1 %shard_map.107 = (f32[1,128]{1,0:T(1,128)}, bf16[1536,256]{1,0:T(8,128)(2,1)}, bf16[512,256]{1,0:T(8,128)(2,1)S(1)}) custom-call(s32[1]{0:T(128)} %bitcast.15.y_ref, bf16[8,256,256]{2,1,0:T(8,128)(2,1)S(1)} %all_to_all.41.near, bf16[8,256,256]{2,1,0:T(8,128)(2,1)S(1)} %collective-permute-done.1.far, f32[8,1,128]{2,1,0:T(1,128)S(1)} %get-tuple-element.52.near_sums, ...), custom_call_target="tpu_custom_call" | custom-call | tf_op jit(solution)/shard_map/pallas_call | solution.py:427
  156.3 10.5 %all-to-all-start.6 = ((bf16[64,24,256]{2,1,0:T(8,128)(2,1)}), bf16[64,24,256]{2,1,0:T(8,128)(2,1)S(1)}, u32[]{:S(2)}, u32[]{:S(2)}) async-start(bf16[64,24,256]{2,1,0:T(8,128)(2,1)} %bitcast.23), calls=%async_computation.6 | async-start | bytes 1572864 | tf_op jit(solution)/shard_map/all_to_all | solution.py:361
  166.9 0.1 reshape.80.codes_ref
  167.0 0.1 reshape.81.more_codes_ref
  167.0 40.0 %all-to-all-done.6 = bf16[64,24,256]{2,1,0:T(8,128)(2,1)S(1)} async-done(((bf16[64,24,256]{2,1,0:T(8,128)(2,1)}), bf16[64,24,256]{2,1,0:T(8,128)(2,1)S(1)}, u32[]{:S(2)}, u32[]{:S(2)}) %all-to-all-start.6) | async-done | bytes 786464 | tf_op jit(solution)/shard_map/all_to_all | solution.py:361
  207.0 1.2 shard_map.109
  208.3 5.5 %collective-permute-start.2 = (bf16[8,128,256]{2,1,0:T(8,128)(2,1)S(1)}, bf16[8,128,256]{2,1,0:T(8,128)(2,1)S(1)}, u32[]{:S(2)}, u32[]{:S(2)}) collective-permute-start(bf16[8,128,256]{2,1,0:T(8,128)(2,1)S(1)} %shard_map.109), channel_id=1, source_target_pairs={{0,64},{64,0},{128,192},{192,128},{256,320},{320,256},{384,448},{4... | collective-permute-start | bytes 1572872 | tf_op jit(solution)/shard_map/ppermute | solution.py:447
  213.8 1.2 shard_map.108.a_ref
  215.1 0.3 collective-permute-done.2.b_ref
  215.4 20.5 %all_to_all.42.parts_ref = bf16[8,128,256]{2,1,0:T(8,128)(2,1)S(1)} all-to-all(bf16[8,128,256]{2,1,0:T(8,128)(2,1)S(1)} %shard_map.110), channel_id=1, replica_groups={{0,128,256,384,512,640,768,896},{64,192,320,448,576,704,832,960},{1,129..., dimensions={0} | all-to-all | bytes 1048576 | tf_op jit(solution)/shard_map/all_to_all | solution.py:355
  235.9 0.9 shard_map.111
  (25 shorter events, 0.4 us)
Async XLA Ops:
  2.4 19.8 %all-to-all-start.2 = ((bf16[8,128,256]{2,1,0:T(8,128)(2,1)}), bf16[8,128,256]{2,1,0:T(8,128)(2,1)S(1)}, u32[]{:S(2)}, u32[]{:S(2)}) async-start(bf16[8,128,256]{2,1,0:T(8,128)(2,1)} %broadcast_in_dim.12), calls=%async_computation.2 | async-start | bytes 1048576 | tf_op jit(solution)/shard_map/all_to_all | solution.py:355
  10.0 0.7 copy-start.4
  10.1 0.7 copy-start.3
  10.1 0.7 copy-start.2
  10.1 0.7 copy-start.1
  10.1 0.7 copy-start.5
  22.2 43.3 %collective-permute-start = (bf16[8,128,256]{2,1,0:T(8,128)(2,1)S(1)}, bf16[8,128,256]{2,1,0:T(8,128)(2,1)S(1)}, u32[]{:S(2)}, u32[]{:S(2)}) collective-permute-start(bf16[8,128,256]{2,1,0:T(8,128)(2,1)S(1)} %all-to-all-done.2.near_ref), channel_id=1, source_target_pairs={{0,64},{64,0},{128,192},{192,128},{256,320},{320,256},{384,448},{4... | collective-permute-start | bytes 1572872 | tf_op jit(solution)/shard_map/ppermute | solution.py:377
  65.4 46.4 %copy-start.6 = (s32[64,1,40]{2,1,0:T(1,128)}, s32[64,1,40]{2,1,0:T(1,128)S(1)}, u32[]{:S(2)}) copy-start(s32[64,1,40]{2,1,0:T(1,128)S(1)} %all_to_all.40) | copy-start | bytes 30724
  68.3 5.1 %copy-start.9 = (bf16[256,256]{1,0:T(8,128)(2,1)S(1)}, bf16[256,256]{1,0:T(8,128)(2,1)}, u32[]{:S(2)}) copy-start(bf16[256,256]{1,0:T(8,128)(2,1)} %param.14) | copy-start | bytes 393220
  68.3 43.5 %all-to-all-start.4 = ((bf16[64,24,256]{2,1,0:T(8,128)(2,1)}), bf16[64,24,256]{2,1,0:T(8,128)(2,1)S(1)}, u32[]{:S(2)}, u32[]{:S(2)}) async-start(bf16[64,24,256]{2,1,0:T(8,128)(2,1)} %bitcast.18), calls=%async_computation.4 | async-start | bytes 1572864 | tf_op jit(solution)/shard_map/all_to_all | solution.py:361
  73.1 0.9 copy-start.8
  140.2 10.9 %collective-permute-start.1 = (bf16[8,256,256]{2,1,0:T(8,128)(2,1)S(1)}, bf16[8,256,256]{2,1,0:T(8,128)(2,1)S(1)}, u32[]{:S(2)}, u32[]{:S(2)}) collective-permute-start(bf16[8,256,256]{2,1,0:T(8,128)(2,1)S(1)} %all_to_all.41.near), channel_id=1, source_target_pairs={{0,64},{64,0},{128,192},{192,128},{256,320},{320,256},{384,448},{4... | collective-permute-start | bytes 3145736 | tf_op jit(solution)/shard_map/ppermute | solution.py:417
  156.3 10.5 %copy-start.7 = (s32[64,1,40]{2,1,0:T(1,128)S(1)}, s32[64,1,40]{2,1,0:T(1,128)}, u32[]{:S(2)}) copy-start(s32[64,1,40]{2,1,0:T(1,128)} %copy-done.6) | copy-start | bytes 30724
  156.3 50.8 %all-to-all-start.6 = ((bf16[64,24,256]{2,1,0:T(8,128)(2,1)}), bf16[64,24,256]{2,1,0:T(8,128)(2,1)S(1)}, u32[]{:S(2)}, u32[]{:S(2)}) async-start(bf16[64,24,256]{2,1,0:T(8,128)(2,1)} %bitcast.23), calls=%async_computation.6 | async-start | bytes 1572864 | tf_op jit(solution)/shard_map/all_to_all | solution.py:361
  208.3 7.0 %collective-permute-start.2 = (bf16[8,128,256]{2,1,0:T(8,128)(2,1)S(1)}, bf16[8,128,256]{2,1,0:T(8,128)(2,1)S(1)}, u32[]{:S(2)}, u32[]{:S(2)}) collective-permute-start(bf16[8,128,256]{2,1,0:T(8,128)(2,1)S(1)} %shard_map.109), channel_id=1, source_target_pairs={{0,64},{64,0},{128,192},{192,128},{256,320},{320,256},{384,448},{4... | collective-permute-start | bytes 1572872 | tf_op jit(solution)/shard_map/ppermute | solution.py:447
  215.4 20.5 %copy-start = (f32[128,256]{1,0:T(8,128)S(1)}, f32[128,256]{1,0:T(8,128)}, u32[]{:S(2)}) copy-start(f32[128,256]{1,0:T(8,128)} %table_ref.1) | copy-start | bytes 393220

commit v4 on v3

--- a/solution.py
+++ b/solution.py
@@ -46,7 +46,7 @@
 
 
 def request_body(
-    core_ref, list_ref, counts_ref, item_refs, query_refs, accum_ref,
+    place_ref, list_ref, counts_ref, item_refs, query_refs, accum_ref,
     req_ref, pos_ref, accum_out, looked, counts2d, square, *, base,
 ):
     length, owners = list_ref.shape[1], counts_ref.shape[1]
@@ -86,7 +86,8 @@
     entries = CAP * rows
     width = LANES // CORES
     owner_core = jnp.where(iota((1, LANES), 1) < width, 0, 1)
-    side = jnp.where(owner_core == core_ref[0], 0.0, 1.0)
+    side = jnp.where(owner_core == place_ref[1], 0.0, 1.0)
+    parity = place_ref[0] % 2
     square[...] = jnp.zeros_like(square)
     square[entries : 2 * entries, :] = positions
     for r in range(entries):
@@ -95,7 +96,9 @@
         here = block == (p >> 7)
         value = jnp.sum(jnp.where(here, spread[:depth], 0.0), axis=0, keepdims=True)
         used = jnp.sum(jnp.where(here, spread[depth:], 0.0), axis=0, keepdims=True)
-        square[r : r + 1, :] = value + (side * rows + (r % rows)) * LANES
+        y = r % rows
+        apart = jnp.where(parity == y % 2, 0, rows // 2).astype(jnp.float32)
+        square[r : r + 1, :] = value + (side * rows + apart + y // 2) * LANES
         square[2 * entries + r : 2 * entries + r + 1, :] = used
     turned = square[...].T
 
@@ -122,17 +125,13 @@
     req_ref[:, slots:] = jnp.broadcast_to(over, (groups, req_ref.shape[1] - slots))
 
 
-def pick_body(recv_ref, near_ref, far_ref, out_ref, over_ref, square, *, first, count, slots):
+def pick_rows(recv_ref, row_refs, square, first, count, begin):
     groups = recv_ref.shape[0]
-    chips, per, width = near_ref.shape
     square[...] = jnp.zeros_like(square)
     square[:groups, : recv_ref.shape[1]] = recv_ref[...].astype(jnp.float32)
     turned = square[...].T.astype(jnp.int32)
-    over_ref[0] = jnp.max(turned[slots : slots + 1, :groups])
+    rows = jnp.concatenate([ref[...].reshape(-1, ref.shape[-1]) for ref in row_refs], axis=0)
     lane = iota((count, LANES), 1)
-    rows = jnp.concatenate(
-        [near_ref[...].reshape(chips * per, width), far_ref[...].reshape(chips * per, width)], axis=0
-    )
     step = 8
     for t in range(0, groups, step):
         hot = []
@@ -140,11 +139,24 @@
             code = jnp.broadcast_to(turned[first : first + count, u : u + 1], (count, LANES))
             hot.append(
                 jnp.concatenate(
-                    [hits(lane + b * LANES, code) for b in range(rows.shape[0] // LANES)], axis=1
+                    [hits(lane + (begin + b * LANES), code) for b in range(rows.shape[0] // LANES)],
+                    axis=1,
                 )
             )
         hot = jnp.concatenate(hot, axis=0).astype(jnp.bfloat16)
-        out_ref[t * count : (t + step) * count, :] = dot(hot, rows).astype(jnp.bfloat16)
+        yield pl.ds(t * count, step * count), dot(hot, rows)
+
+
+def pick_near_body(recv_ref, near_ref, next_ref, out_ref, square, *, first, count):
+    for span, got in pick_rows(recv_ref, (near_ref, next_ref), square, first, count, 0):
+        out_ref[span, :] = got.astype(jnp.bfloat16)
+
+
+def pick_far_body(recv_ref, far_ref, near_got, out_ref, over_ref, square, *, first, count, slots):
+    begin = far_ref.shape[0] * far_ref.shape[1]
+    for span, got in pick_rows(recv_ref, (far_ref,), square, first, count, begin):
+        out_ref[span, :] = (got + near_got[span, :].astype(jnp.float32)).astype(jnp.bfloat16)
+    over_ref[0] = jnp.max(recv_ref[:, slots : slots + 1])
 
 
 def project(pool, weight):
@@ -161,8 +173,8 @@
 
 
 def tower_body(
-    pos_ref, more_pos_ref, item_refs, query_refs, fetched, more_fetched, weights,
-    hits_ref, more_hits_ref, pool_ref, out_ref, square,
+    recv_ref, pos_ref, more_pos_ref, item_refs, query_refs, fetched, more_fetched, weights,
+    hits_ref, more_hits_ref, pool_ref, out_ref, square, pool_sum, more_rows, sem,
 ):
     pairs = item_refs.shape[1]
     square[...] = jnp.zeros_like(square)
@@ -171,14 +183,28 @@
     turned = square[...].T.astype(jnp.int32)
     item_columns = turned[:, 0 : item_refs.shape[0]]
     query_columns = turned[:, 8 : 8 + query_refs.shape[0]]
+    slots = (pos_ref.shape[1] + more_pos_ref.shape[1]) // recv_ref.shape[0]
+    crowded = jnp.max(recv_ref[:, slots : slots + 1]) > 0
+    spans = [pl.ds(side * pairs, pairs) for side in range(2)]
+    for span, refs in zip(spans, (item_columns, query_columns)):
+        weight = pair_weight(refs, pos_ref[...])
+        hits_ref[span, :] = weight
+        pool_sum[span, :] = dot(weight, fetched[...])
+    more_hits_ref[...] = jnp.zeros_like(more_hits_ref)
+
+    @pl.when(crowded)
+    def _():
+        copy = pltpu.make_async_copy(more_fetched, more_rows, sem)
+        copy.start()
+        copy.wait()
+        for span, refs in zip(spans, (item_columns, query_columns)):
+            weight = pair_weight(refs, more_pos_ref[...])
+            more_hits_ref[span, :] = weight
+            pool_sum[span, :] = pool_sum[span, :] + dot(weight, more_rows[...])
+
     outs = []
-    for side, refs in enumerate((item_columns, query_columns)):
-        span = pl.ds(side * pairs, pairs)
-        weight = pair_weight(refs, pos_ref[...])
-        more_weight = pair_weight(refs, more_pos_ref[...])
-        hits_ref[span, :] = weight
-        more_hits_ref[span, :] = more_weight
-        pool = (dot(weight, fetched[...]) + dot(more_weight, more_fetched[...])).astype(jnp.bfloat16)
+    for side, span in enumerate(spans):
+        pool = pool_sum[span, :].astype(jnp.bfloat16)
         pool_ref[span, :] = pool
         outs.append(project(pool, weights[side])[0].astype(jnp.bfloat16))
     for y in range(out_ref.shape[0]):
@@ -297,18 +323,34 @@
             out[s : s + step, :] = (parts[:, :width] + parts[:, width:]).astype(jnp.bfloat16)
 
 
-def column_body(codes_ref, more_codes_ref, grads_ref, more_grads_ref, out_ref, *, side):
+def column_body(
+    place_ref, recv_ref, codes_ref, more_codes_ref, grads_ref, more_grads_ref, out_ref, sums, more_rows, sem, *, side
+):
     chips, per = out_ref.shape[:2]
+    slots = (codes_ref.shape[1] + more_codes_ref.shape[1]) // recv_ref.shape[0]
+    crowded = jnp.max(recv_ref[:, slots : slots + 1]) > 0
+
+    def sum_of(codes, grads, y):
+        hot = hits(iota((2 * per, codes.shape[1]), 0), codes - (side * chips + y) * per)
+        return dot(hot.astype(jnp.bfloat16), grads)
+
     for y in range(0, chips, 2):
-        begin = (side * chips + y) * per
-        total = None
-        for codes, grads in ((codes_ref, grads_ref), (more_codes_ref, more_grads_ref)):
-            down = iota((2 * per, codes.shape[1]), 0)
-            hot = hits(down, codes[...] - begin).astype(jnp.bfloat16)
-            part = dot(hot, grads[...])
-            total = part if total is None else total + part
-        out_ref[y] = total[:per].astype(out_ref.dtype)
-        out_ref[y + 1] = total[per:].astype(out_ref.dtype)
+        sums[y * per : (y + 2) * per, :] = sum_of(codes_ref[...], grads_ref[...], y)
+
+    @pl.when(crowded)
+    def _():
+        copy = pltpu.make_async_copy(more_grads_ref, more_rows, sem)
+        copy.start()
+        copy.wait()
+        for y in range(0, chips, 2):
+            span = pl.ds(y * per, 2 * per)
+            sums[span, :] = sums[span, :] + sum_of(more_codes_ref[...], more_rows[...], y)
+
+    parity = place_ref[0] % 2
+    for y in range(chips):
+        half, k = divmod(y, chips // 2)
+        owner_y = 2 * k + (parity if half == 0 else 1 - parity)
+        out_ref[owner_y] = sums[y * per : (y + 1) * per, :].astype(out_ref.dtype)
 
 
 def add_body(a_ref, b_ref, out_ref):
@@ -346,10 +388,17 @@
     base = slots * 3 // 4
     more = slots - base
     replica = lax.axis_index("dp")
-    core = (replica % CORES).reshape(1).astype(i32)
-    chip = (replica // CORES).reshape(1).astype(i32)
+    place = jnp.stack([replica // CORES, replica % CORES]).astype(i32)
     along_y = [[y * CORES + c for y in range(chips)] for c in range(CORES)]
+    along_parity = [
+        [(2 * k + p) * CORES + c for k in range(chips // 2)] for p in range(2) for c in range(CORES)
+    ]
     swap = [(r, r ^ 1) for r in range(n_dp)]
+    beside = [
+        (y * CORES + c, (y + (chips - 1 if c == 0 else 1)) % chips * CORES + c)
+        for y in range(chips)
+        for c in range(CORES)
+    ]
 
     def over_y(x):
         return lax.all_to_all(
@@ -360,7 +409,14 @@
         parts = x.reshape(n_table, -1, x.shape[-1])
         return lax.all_to_all(parts, "table", split_axis=0, concat_axis=0, tiled=True).reshape(x.shape)
 
-    near_rows = over_y(jnp.broadcast_to(table.astype(bf16)[None], (chips, per, width)))
+    near_rows = lax.all_to_all(
+        jnp.broadcast_to(table.astype(bf16)[None], (chips // 2, per, width)),
+        "dp",
+        split_axis=0,
+        concat_axis=0,
+        axis_index_groups=along_parity,
+        tiled=True,
+    )
     tower_weights = jnp.stack([item_weight, query_weight])
     items, queries = item_refs[0, 0].T, query_refs[0, 0].T
     requests, places, old_accum = call(
@@ -372,19 +428,26 @@
             pltpu.VMEM((n_dp * n_table // LANES, LANES), f32),
             pltpu.VMEM((LANES, LANES), f32),
         ],
-    )(core, packed_rows.reshape(1, -1), block_counts.reshape(1, -1), items, queries, accum.reshape(1, per))
+    )(place, packed_rows.reshape(1, -1), block_counts.reshape(1, -1), items, queries, accum.reshape(1, per))
     near_rows, requests = lax.optimization_barrier((near_rows, requests))
-    far_rows = lax.ppermute(near_rows, "dp", swap)
+    next_rows = lax.ppermute(near_rows, "dp", beside)
     received = over_table(requests)
+    received, near_rows, next_rows = lax.optimization_barrier((received, near_rows, next_rows))
+    far_rows = lax.ppermute(jnp.concatenate([near_rows, next_rows]), "dp", swap)
 
     def pick(first, count, received):
+        picked = shape((n_table * count, width), bf16)
+        square = [pltpu.VMEM((LANES, LANES), f32)]
+        near_got = call(
+            functools.partial(pick_near_body, first=first, count=count), picked, [VMEM] * 3, square
+        )(received, near_rows, next_rows)
         return call(
-            functools.partial(pick_body, first=first, count=count, slots=slots),
-            (shape((n_table * count, width), bf16), shape((1,), i32)),
+            functools.partial(pick_far_body, first=first, count=count, slots=slots),
+            (picked, shape((1,), i32)),
             [VMEM] * 3,
-            [pltpu.VMEM((LANES, LANES), f32)],
+            square,
             out_specs=(VMEM, SMEM),
-        )(received, near_rows, far_rows)
+        )(received, far_rows, near_got)
 
     picked, over = pick(0, base, received)
     fetched = over_table(picked)
@@ -402,9 +465,15 @@
             shape((2 * pairs, width), bf16),
             shape((chips, 2 * pairs, width), bf16),
         ),
-        [VMEM] * 7,
-        [pltpu.VMEM((LANES, LANES), f32)],
+        [VMEM] * 6 + [pl.BlockSpec(memory_space=pl.ANY), VMEM],
+        [
+            pltpu.VMEM((LANES, LANES), f32),
+            pltpu.VMEM((2 * pairs, width), f32),
+            pltpu.VMEM((n_table * more, width), bf16),
+            pltpu.SemaphoreType.DMA,
+        ],
     )(
+        received,
         places[:, :base].reshape(1, -1),
         places[:, base:].reshape(1, -1),
         items,
@@ -433,7 +502,7 @@
         ),
         [SMEM] + [VMEM] * 7,
         [pltpu.VMEM((chips, 1, 2 * pairs), f32), pltpu.VMEM((chips, pairs, 2 * pairs), f32)],
-    )(chip, near, far, near_sums, pool, tower_weights, turned_hits, more_turned_hits)
+    )(place, near, far, near_sums, pool, tower_weights, turned_hits, more_turned_hits)
     returned = over_table(grads)
     more_returned = lax.cond(crowded, lambda: over_table(more_grads), lambda: nothing)
     codes = received[:, :base].reshape(1, -1)
@@ -441,8 +510,15 @@
 
     def column(side, dtype):
         return call(
-            functools.partial(column_body, side=side), shape((chips, per, width), dtype), [VMEM] * 4
-        )(codes, more_codes, returned, more_returned)
+            functools.partial(column_body, side=side),
+            shape((chips, per, width), dtype),
+            [SMEM] + [VMEM] * 4 + [pl.BlockSpec(memory_space=pl.ANY)],
+            [
+                pltpu.VMEM((chips * per, width), f32),
+                pltpu.VMEM((n_table * more, width), bf16),
+                pltpu.SemaphoreType.DMA,
+            ],
+        )(place, received, codes, more_codes, returned, more_returned)
 
     other = lax.ppermute(column(1, bf16), "dp", swap)
     both = call(add_body, shape((chips, per, width), bf16), [VMEM] * 2)(column(0, f32), other)

time: 238 us -> 237 us (level)
  blocking collectives: 76.2 us -> 85.3 us
  starting transfers between devices: 50.2 us -> 42.3 us
    ppermute x1 -> x2, starting transfers between devices: 13 us -> 8.06 us  [the longest x1 6.16 us: on_device(): far_rows = lax.ppermute(jnp.concatenate([near_rows, next_rows]), 'dp', swap)]
    all_to_all x1, blocking collectives: 30.3 us -> 35 us  [over_table(): lax.all_to_all(parts, 'table', split_axis=0, concat_axis=0, tiled=True)]
    all_to_all x2, blocking collectives: 45.9 us -> 50.3 us  [over_y(): lax.all_to_all(x, 'dp', split_axis=0, concat_axis=0, axis_index_groups=al...]
    all_to_all x1, waiting for transfers between devices: 9.24 us -> 5.14 us  [on_device(): lax.all_to_all(jnp.broadcast_to(table.astype(bf16)[None], (chips // 2, pe...]
  transfers between devices with their start and end apart: 6 -> 7, of which waited for: 5 -> 5; matrix products, arithmetic and copies ran while one was open for 0% -> 0% of each run, Pallas kernels for 2% -> 3%
where the time goes in v4:
time: 237 us; the launch traced here: 236 us
  waiting for transfers between devices  85.8 us (36%)
  blocking collectives  85.3 us (36%)
  starting transfers between devices  42.3 us (18%)
  Pallas kernels  17.8 us (8%)
  local copies, waits for them, and re-layouts  2.61 us (1%)
    all_to_all x2, waiting for transfers between devices, over_table(): lax.all_to_all(parts, 'table', split_axis=0, concat_axis=0, tiled=True)  79 us
    all_to_all x2, blocking collectives, over_y(): lax.all_to_all(x, 'dp', split_axis=0, concat_axis=0, axis_index_groups=al...  50.3 us
    all_to_all x1, blocking collectives, over_table(): lax.all_to_all(parts, 'table', split_axis=0, concat_axis=0, tiled=True)  35 us
    all_to_all x2, starting transfers between devices, over_table(): lax.all_to_all(parts, 'table', split_axis=0, concat_axis=0, tiled=True)  13.6 us
    all_to_all x1, starting transfers between devices, on_device(): lax.all_to_all(jnp.broadcast_to(table.astype(bf16)[None], (chips // 2, pe...  7.64 us
    ppermute x1, starting transfers between devices, on_device(): far = lax.ppermute(near, 'dp', swap)  7.41 us
    ppermute x1, starting transfers between devices, on_device(): far_rows = lax.ppermute(jnp.concatenate([near_rows, next_rows]), 'dp', swap)  6.16 us
    pallas_call x1, Pallas kernels, on_device(): call(loss_body, (shape((1, pairs), f32), shape((n_table * base, width), b...  5.68 us
  transfers between devices with their start and end apart: 7, of which 5 were waited for; matrix products, arithmetic and copies ran while one was open for 0% of the time, Pallas kernels for 3%

profile of v4, /device:TPU:1, one launch (start us, length us, event | category | flops | bytes accessed | tf_op | source)
XLA Modules:
  0.0 236.4 jit_solution(16710769091114655001)
XLA Ops:
  0.6 0.9 convert_element_type.10
  1.5 0.7 broadcast_in_dim.12
  2.3 7.6 %all-to-all-start.2 = ((bf16[4,128,256]{2,1,0:T(8,128)(2,1)}), bf16[4,128,256]{2,1,0:T(8,128)(2,1)S(1)}, u32[]{:S(2)}, u32[]{:S(2)}) async-start(bf16[4,128,256]{2,1,0:T(8,128)(2,1)} %broadcast_in_dim.12), calls=%async_computation.2 | async-start | bytes 524288 | tf_op jit(solution)/shard_map/all_to_all | solution.py:412
  10.0 0.6 copy-done.4
  10.7 2.7 %shard_map.103 = (s32[64,40]{1,0:T(8,128)S(1)}, s32[64,32]{1,0:T(8,128)S(1)}, f32[1,128]{1,0:T(1,128)S(1)}) custom-call(s32[2]{0:T(128)S(1)} %pad_add_fusion.place_ref.y_ref, s32[1,1536]{1,0:T(1,128)S(1)} %bitcast.40, s32[1,1024]{1,0:T(1,128)S(1)} %bitcast.41, s32[4,128]{1,0:T(4,128)S(1)} %bitcast.36, s32[4,128]{1,0:T(4,128)S(1)} %bitcast.38, ...), custom_call_target="tpu_custom_call" | custom-call | tf_op jit(solution)/shard_map/pallas_call | solution.py:422
  13.4 5.1 %all-to-all-done.2.near_ref = bf16[4,128,256]{2,1,0:T(8,128)(2,1)S(1)} async-done(((bf16[4,128,256]{2,1,0:T(8,128)(2,1)}), bf16[4,128,256]{2,1,0:T(8,128)(2,1)S(1)}, u32[]{:S(2)}, u32[]{:S(2)}) %all-to-all-start.2) | async-done | bytes 262176 | tf_op jit(solution)/shard_map/all_to_all | solution.py:412
  18.5 1.9 collective-permute-start
  20.5 35.0 %all_to_all.40 = s32[64,1,40]{2,1,0:T(1,128)S(1)} all-to-all(s32[64,1,40]{2,1,0:T(1,128)S(1)} %bitcast.35), channel_id=1, replica_groups=mesh['dp'=16,'table'=64] {'table'}, dimensions={0} | all-to-all | bytes 20480 | tf_op jit(solution)/shard_map/all_to_all | solution.py:410
  55.5 6.2 %collective-permute-start.1 = (bf16[8,128,256]{2,1,0:T(8,128)(2,1)S(1)}, bf16[8,128,256]{2,1,0:T(8,128)(2,1)S(1)}, u32[]{:S(2)}, u32[]{:S(2)}) collective-permute-start(bf16[8,128,256]{2,1,0:T(8,128)(2,1)S(1)} %pad_maximum_fusion), channel_id=1, source_target_pairs={{0,64},{64,0},{128,192},{192,128},{256,320},{320,256},{384,448},{4... | collective-permute-start | bytes 1572872 | tf_op jit(solution)/shard_map/ppermute | solution.py:436
  61.6 1.1 shard_map.104.near_got
  62.8 0.4 collective-permute-done.1.far_ref
  63.2 2.1 shard_map.105
  65.2 4.8 %all-to-all-start.4 = ((bf16[64,24,256]{2,1,0:T(8,128)(2,1)}), bf16[64,24,256]{2,1,0:T(8,128)(2,1)S(1)}, u32[]{:S(2)}, u32[]{:S(2)}) async-start(bf16[64,24,256]{2,1,0:T(8,128)(2,1)} %bitcast.18), calls=%async_computation.4 | async-start | bytes 1572864 | tf_op jit(solution)/shard_map/all_to_all | solution.py:410
  70.1 0.1 reshape.76.more_pos_ref
  70.2 0.1 reshape.75.pos_ref
  70.3 0.6 copy-done.6
  71.6 39.0 %all-to-all-done.4 = bf16[64,24,256]{2,1,0:T(8,128)(2,1)S(1)} async-done(((bf16[64,24,256]{2,1,0:T(8,128)(2,1)}), bf16[64,24,256]{2,1,0:T(8,128)(2,1)S(1)}, u32[]{:S(2)}, u32[]{:S(2)}) %all-to-all-start.4) | async-done | bytes 786464 | tf_op jit(solution)/shard_map/all_to_all | solution.py:410
  110.7 1.3 shard_map.106
  112.0 29.8 %all_to_all.41.near = bf16[8,256,256]{2,1,0:T(8,128)(2,1)S(1)} all-to-all(bf16[8,256,256]{2,1,0:T(8,128)(2,1)S(1)} %get-tuple-element.58), channel_id=1, replica_groups={{0,128,256,384,512,640,768,896},{64,192,320,448,576,704,832,960},{1,129..., dimensions={0} | all-to-all | bytes 2097152 | tf_op jit(solution)/shard_map/all_to_all | solution.py:404
  141.8 7.4 %collective-permute-start.2 = (bf16[8,256,256]{2,1,0:T(8,128)(2,1)S(1)}, bf16[8,256,256]{2,1,0:T(8,128)(2,1)S(1)}, u32[]{:S(2)}, u32[]{:S(2)}) collective-permute-start(bf16[8,256,256]{2,1,0:T(8,128)(2,1)S(1)} %all_to_all.41.near), channel_id=1, source_target_pairs={{0,64},{64,0},{128,192},{192,128},{256,320},{320,256},{384,448},{4... | collective-permute-start | bytes 3145736 | tf_op jit(solution)/shard_map/ppermute | solution.py:486
  149.2 0.8 shard_map.107
  150.0 1.3 collective-permute-done.2.far
  151.3 5.7 %shard_map.108 = (f32[1,128]{1,0:T(1,128)}, bf16[1536,256]{1,0:T(8,128)(2,1)}, bf16[512,256]{1,0:T(8,128)(2,1)S(1)}) custom-call(s32[2]{0:T(128)S(1)} %pad_add_fusion.place_ref.y_ref, bf16[8,256,256]{2,1,0:T(8,128)(2,1)S(1)} %all_to_all.41.near, bf16[8,256,256]{2,1,0:T(8,128)(2,1)S(1)} %collective-permute-done.2.far, ...), custom_call_target="tpu_custom_call" | custom-call | tf_op jit(solution)/shard_map/pallas_call | solution.py:496
  157.0 8.9 %all-to-all-start.6 = ((bf16[64,24,256]{2,1,0:T(8,128)(2,1)}), bf16[64,24,256]{2,1,0:T(8,128)(2,1)S(1)}, u32[]{:S(2)}, u32[]{:S(2)}) async-start(bf16[64,24,256]{2,1,0:T(8,128)(2,1)} %bitcast.23), calls=%async_computation.6 | async-start | bytes 1572864 | tf_op jit(solution)/shard_map/all_to_all | solution.py:410
  165.9 0.1 reshape.74.more_codes_ref
  166.0 0.1 reshape.73.codes_ref
  166.1 40.0 %all-to-all-done.6 = bf16[64,24,256]{2,1,0:T(8,128)(2,1)S(1)} async-done(((bf16[64,24,256]{2,1,0:T(8,128)(2,1)}), bf16[64,24,256]{2,1,0:T(8,128)(2,1)S(1)}, u32[]{:S(2)}, u32[]{:S(2)}) %all-to-all-start.6) | async-done | bytes 786464 | tf_op jit(solution)/shard_map/all_to_all | solution.py:410
  206.1 1.6 shard_map.110
  207.7 5.5 %collective-permute-start.3 = (bf16[8,128,256]{2,1,0:T(8,128)(2,1)S(1)}, bf16[8,128,256]{2,1,0:T(8,128)(2,1)S(1)}, u32[]{:S(2)}, u32[]{:S(2)}) collective-permute-start(bf16[8,128,256]{2,1,0:T(8,128)(2,1)S(1)} %shard_map.110), channel_id=1, source_target_pairs={{0,64},{64,0},{128,192},{192,128},{256,320},{320,256},{384,448},{4... | collective-permute-start | bytes 1572872 | tf_op jit(solution)/shard_map/ppermute | solution.py:523
  213.3 1.6 shard_map.109.a_ref
  215.0 20.5 %all_to_all.42.parts_ref = bf16[8,128,256]{2,1,0:T(8,128)(2,1)S(1)} all-to-all(bf16[8,128,256]{2,1,0:T(8,128)(2,1)S(1)} %shard_map.111), channel_id=1, replica_groups={{0,128,256,384,512,640,768,896},{64,192,320,448,576,704,832,960},{1,129..., dimensions={0} | all-to-all | bytes 1048576 | tf_op jit(solution)/shard_map/all_to_all | solution.py:404
  235.5 0.9 shard_map.112
  (26 shorter events, 0.6 us)
Async XLA Ops:
  2.3 16.3 %all-to-all-start.2 = ((bf16[4,128,256]{2,1,0:T(8,128)(2,1)}), bf16[4,128,256]{2,1,0:T(8,128)(2,1)S(1)}, u32[]{:S(2)}, u32[]{:S(2)}) async-start(bf16[4,128,256]{2,1,0:T(8,128)(2,1)} %broadcast_in_dim.12), calls=%async_computation.2 | async-start | bytes 524288 | tf_op jit(solution)/shard_map/all_to_all | solution.py:412
  9.9 0.7 copy-start.4
  9.9 0.7 copy-start.3
  10.0 0.7 copy-start.2
  10.0 0.7 copy-start.1
  10.0 0.7 copy-start.5
  18.5 36.9 %collective-permute-start = (bf16[4,128,256]{2,1,0:T(8,128)(2,1)S(1)}, bf16[4,128,256]{2,1,0:T(8,128)(2,1)S(1)}, u32[]{:S(2)}, u32[]{:S(2)}) collective-permute-start(bf16[4,128,256]{2,1,0:T(8,128)(2,1)S(1)} %all-to-all-done.2.near_ref), channel_id=1, source_target_pairs={{0,896},{64,192},{128,0},{192,320},{256,128},{320,448},{384,256},{... | collective-permute-start | bytes 786440 | tf_op jit(solution)/shard_map/ppermute | solution.py:433
  55.5 7.7 %collective-permute-start.1 = (bf16[8,128,256]{2,1,0:T(8,128)(2,1)S(1)}, bf16[8,128,256]{2,1,0:T(8,128)(2,1)S(1)}, u32[]{:S(2)}, u32[]{:S(2)}) collective-permute-start(bf16[8,128,256]{2,1,0:T(8,128)(2,1)S(1)} %pad_maximum_fusion), channel_id=1, source_target_pairs={{0,64},{64,0},{128,192},{192,128},{256,320},{320,256},{384,448},{4... | collective-permute-start | bytes 1572872 | tf_op jit(solution)/shard_map/ppermute | solution.py:436
  65.2 5.1 %copy-start.7 = (bf16[256,256]{1,0:T(8,128)(2,1)S(1)}, bf16[256,256]{1,0:T(8,128)(2,1)}, u32[]{:S(2)}) copy-start(bf16[256,256]{1,0:T(8,128)(2,1)} %param.14) | copy-start | bytes 393220
  65.2 45.4 %all-to-all-start.4 = ((bf16[64,24,256]{2,1,0:T(8,128)(2,1)}), bf16[64,24,256]{2,1,0:T(8,128)(2,1)S(1)}, u32[]{:S(2)}, u32[]{:S(2)}) async-start(bf16[64,24,256]{2,1,0:T(8,128)(2,1)} %bitcast.18), calls=%async_computation.4 | async-start | bytes 1572864 | tf_op jit(solution)/shard_map/all_to_all | solution.py:410
  70.0 0.9 copy-start.6
  141.8 9.5 %collective-permute-start.2 = (bf16[8,256,256]{2,1,0:T(8,128)(2,1)S(1)}, bf16[8,256,256]{2,1,0:T(8,128)(2,1)S(1)}, u32[]{:S(2)}, u32[]{:S(2)}) collective-permute-start(bf16[8,256,256]{2,1,0:T(8,128)(2,1)S(1)} %all_to_all.41.near), channel_id=1, source_target_pairs={{0,64},{64,0},{128,192},{192,128},{256,320},{320,256},{384,448},{4... | collective-permute-start | bytes 3145736 | tf_op jit(solution)/shard_map/ppermute | solution.py:486
  157.0 49.1 %all-to-all-start.6 = ((bf16[64,24,256]{2,1,0:T(8,128)(2,1)}), bf16[64,24,256]{2,1,0:T(8,128)(2,1)S(1)}, u32[]{:S(2)}, u32[]{:S(2)}) async-start(bf16[64,24,256]{2,1,0:T(8,128)(2,1)} %bitcast.23), calls=%async_computation.6 | async-start | bytes 1572864 | tf_op jit(solution)/shard_map/all_to_all | solution.py:410
  207.7 7.2 %collective-permute-start.3 = (bf16[8,128,256]{2,1,0:T(8,128)(2,1)S(1)}, bf16[8,128,256]{2,1,0:T(8,128)(2,1)S(1)}, u32[]{:S(2)}, u32[]{:S(2)}) collective-permute-start(bf16[8,128,256]{2,1,0:T(8,128)(2,1)S(1)} %shard_map.110), channel_id=1, source_target_pairs={{0,64},{64,0},{128,192},{192,128},{256,320},{320,256},{384,448},{4... | collective-permute-start | bytes 1572872 | tf_op jit(solution)/shard_map/ppermute | solution.py:523
  215.0 20.5 %copy-start = (f32[128,256]{1,0:T(8,128)S(1)}, f32[128,256]{1,0:T(8,128)}, u32[]{:S(2)}) copy-start(f32[128,256]{1,0:T(8,128)} %table_ref.1) | copy-start | bytes 393220

commit v5 on v4

--- a/solution.py
+++ b/solution.py
@@ -46,7 +46,7 @@
 
 
 def request_body(
-    place_ref, list_ref, counts_ref, item_refs, query_refs, accum_ref,
+    y_ref, core_ref, list_ref, counts_ref, item_refs, query_refs, accum_ref,
     req_ref, pos_ref, accum_out, looked, counts2d, square, *, base,
 ):
     length, owners = list_ref.shape[1], counts_ref.shape[1]
@@ -86,8 +86,8 @@
     entries = CAP * rows
     width = LANES // CORES
     owner_core = jnp.where(iota((1, LANES), 1) < width, 0, 1)
-    side = jnp.where(owner_core == place_ref[1], 0.0, 1.0)
-    parity = place_ref[0] % 2
+    side = jnp.where(owner_core == core_ref[0], 0.0, 1.0)
+    parity = y_ref[0] % 2
     square[...] = jnp.zeros_like(square)
     square[entries : 2 * entries, :] = positions
     for r in range(entries):
@@ -98,7 +98,7 @@
         used = jnp.sum(jnp.where(here, spread[depth:], 0.0), axis=0, keepdims=True)
         y = r % rows
         apart = jnp.where(parity == y % 2, 0, rows // 2).astype(jnp.float32)
-        square[r : r + 1, :] = value + (side * rows + apart + y // 2) * LANES
+        square[r : r + 1, :] = value + ((apart + y // 2) * CORES + side) * LANES
         square[2 * entries + r : 2 * entries + r + 1, :] = used
     turned = square[...].T
 
@@ -125,12 +125,13 @@
     req_ref[:, slots:] = jnp.broadcast_to(over, (groups, req_ref.shape[1] - slots))
 
 
-def pick_rows(recv_ref, row_refs, square, first, count, begin):
+def pick_body(recv_ref, near_ref, next_ref, out_ref, over_ref, square, *, first, count, slots):
     groups = recv_ref.shape[0]
     square[...] = jnp.zeros_like(square)
     square[:groups, : recv_ref.shape[1]] = recv_ref[...].astype(jnp.float32)
     turned = square[...].T.astype(jnp.int32)
-    rows = jnp.concatenate([ref[...].reshape(-1, ref.shape[-1]) for ref in row_refs], axis=0)
+    over_ref[0] = jnp.max(turned[slots : slots + 1, :groups])
+    rows = jnp.concatenate([ref[...].reshape(-1, ref.shape[-1]) for ref in (near_ref, next_ref)], axis=0)
     lane = iota((count, LANES), 1)
     step = 8
     for t in range(0, groups, step):
@@ -139,24 +140,11 @@
             code = jnp.broadcast_to(turned[first : first + count, u : u + 1], (count, LANES))
             hot.append(
                 jnp.concatenate(
-                    [hits(lane + (begin + b * LANES), code) for b in range(rows.shape[0] // LANES)],
-                    axis=1,
+                    [hits(lane + b * LANES, code) for b in range(rows.shape[0] // LANES)], axis=1
                 )
             )
         hot = jnp.concatenate(hot, axis=0).astype(jnp.bfloat16)
-        yield pl.ds(t * count, step * count), dot(hot, rows)
-
-
-def pick_near_body(recv_ref, near_ref, next_ref, out_ref, square, *, first, count):
-    for span, got in pick_rows(recv_ref, (near_ref, next_ref), square, first, count, 0):
-        out_ref[span, :] = got.astype(jnp.bfloat16)
-
-
-def pick_far_body(recv_ref, far_ref, near_got, out_ref, over_ref, square, *, first, count, slots):
-    begin = far_ref.shape[0] * far_ref.shape[1]
-    for span, got in pick_rows(recv_ref, (far_ref,), square, first, count, begin):
-        out_ref[span, :] = (got + near_got[span, :].astype(jnp.float32)).astype(jnp.bfloat16)
-    over_ref[0] = jnp.max(recv_ref[:, slots : slots + 1])
+        out_ref[t * count : (t + step) * count, :] = dot(hot, rows).astype(jnp.bfloat16)
 
 
 def project(pool, weight):
@@ -323,34 +311,22 @@
             out[s : s + step, :] = (parts[:, :width] + parts[:, width:]).astype(jnp.bfloat16)
 
 
-def column_body(
-    place_ref, recv_ref, codes_ref, more_codes_ref, grads_ref, more_grads_ref, out_ref, sums, more_rows, sem, *, side
-):
+def column_body(y_ref, codes_ref, more_codes_ref, grads_ref, more_grads_ref, out_ref, *, side):
     chips, per = out_ref.shape[:2]
-    slots = (codes_ref.shape[1] + more_codes_ref.shape[1]) // recv_ref.shape[0]
-    crowded = jnp.max(recv_ref[:, slots : slots + 1]) > 0
-
-    def sum_of(codes, grads, y):
-        hot = hits(iota((2 * per, codes.shape[1]), 0), codes - (side * chips + y) * per)
-        return dot(hot.astype(jnp.bfloat16), grads)
-
-    for y in range(0, chips, 2):
-        sums[y * per : (y + 2) * per, :] = sum_of(codes_ref[...], grads_ref[...], y)
-
-    @pl.when(crowded)
-    def _():
-        copy = pltpu.make_async_copy(more_grads_ref, more_rows, sem)
-        copy.start()
-        copy.wait()
-        for y in range(0, chips, 2):
-            span = pl.ds(y * per, 2 * per)
-            sums[span, :] = sums[span, :] + sum_of(more_codes_ref[...], more_rows[...], y)
-
-    parity = place_ref[0] % 2
-    for y in range(chips):
-        half, k = divmod(y, chips // 2)
-        owner_y = 2 * k + (parity if half == 0 else 1 - parity)
-        out_ref[owner_y] = sums[y * per : (y + 1) * per, :].astype(out_ref.dtype)
+    parity = y_ref[0] % 2
+    for n in range(0, chips, 2):
+        total = None
+        for codes, grads in ((codes_ref, grads_ref), (more_codes_ref, more_grads_ref)):
+            hot = [
+                hits(iota((per, codes.shape[1]), 0), codes[...] - ((n + u) * CORES + side) * per)
+                for u in range(2)
+            ]
+            part = dot(jnp.concatenate(hot, axis=0).astype(jnp.bfloat16), grads[...])
+            total = part if total is None else total + part
+        for u in range(2):
+            half, k = divmod(n + u, chips // 2)
+            owner_y = 2 * k + (parity if half == 0 else 1 - parity)
+            out_ref[owner_y] = total[u * per : (u + 1) * per].astype(out_ref.dtype)
 
 
 def add_body(a_ref, b_ref, out_ref):
@@ -388,7 +364,8 @@
     base = slots * 3 // 4
     more = slots - base
     replica = lax.axis_index("dp")
-    place = jnp.stack([replica // CORES, replica % CORES]).astype(i32)
+    core = (replica % CORES).reshape(1).astype(i32)
+    chip = (replica // CORES).reshape(1).astype(i32)
     along_y = [[y * CORES + c for y in range(chips)] for c in range(CORES)]
     along_parity = [
         [(2 * k + p) * CORES + c for k in range(chips // 2)] for p in range(2) for c in range(CORES)
@@ -409,8 +386,10 @@
         parts = x.reshape(n_table, -1, x.shape[-1])
         return lax.all_to_all(parts, "table", split_axis=0, concat_axis=0, tiled=True).reshape(x.shape)
 
+    own_rows = table.astype(bf16)
+    chip_rows = jnp.concatenate([own_rows, lax.ppermute(own_rows, "dp", swap)])
     near_rows = lax.all_to_all(
-        jnp.broadcast_to(table.astype(bf16)[None], (chips // 2, per, width)),
+        jnp.broadcast_to(chip_rows[None], (chips // 2, CORES * per, width)),
         "dp",
         split_axis=0,
         concat_axis=0,
@@ -422,32 +401,25 @@
     requests, places, old_accum = call(
         functools.partial(request_body, base=base),
         (shape((n_table, slots + 8), i32), shape((n_table, slots), i32), shape((1, per), f32)),
-        [SMEM] + [VMEM] * 5,
+        [SMEM] * 2 + [VMEM] * 5,
         [
             pltpu.VMEM((32, LANES), f32),
             pltpu.VMEM((n_dp * n_table // LANES, LANES), f32),
             pltpu.VMEM((LANES, LANES), f32),
         ],
-    )(place, packed_rows.reshape(1, -1), block_counts.reshape(1, -1), items, queries, accum.reshape(1, per))
+    )(chip, core, packed_rows.reshape(1, -1), block_counts.reshape(1, -1), items, queries, accum.reshape(1, per))
     near_rows, requests = lax.optimization_barrier((near_rows, requests))
     next_rows = lax.ppermute(near_rows, "dp", beside)
     received = over_table(requests)
-    received, near_rows, next_rows = lax.optimization_barrier((received, near_rows, next_rows))
-    far_rows = lax.ppermute(jnp.concatenate([near_rows, next_rows]), "dp", swap)
 
     def pick(first, count, received):
-        picked = shape((n_table * count, width), bf16)
-        square = [pltpu.VMEM((LANES, LANES), f32)]
-        near_got = call(
-            functools.partial(pick_near_body, first=first, count=count), picked, [VMEM] * 3, square
+        return call(
+            functools.partial(pick_body, first=first, count=count, slots=slots),
+            (shape((n_table * count, width), bf16), shape((1,), i32)),
+            [VMEM] * 3,
+            [pltpu.VMEM((LANES, LANES), f32)],
+            out_specs=(VMEM, SMEM),
         )(received, near_rows, next_rows)
-        return call(
-            functools.partial(pick_far_body, first=first, count=count, slots=slots),
-            (picked, shape((1,), i32)),
-            [VMEM] * 3,
-            square,
-            out_specs=(VMEM, SMEM),
-        )(received, far_rows, near_got)
 
     picked, over = pick(0, base, received)
     fetched = over_table(picked)
@@ -502,7 +474,7 @@
         ),
         [SMEM] + [VMEM] * 7,
         [pltpu.VMEM((chips, 1, 2 * pairs), f32), pltpu.VMEM((chips, pairs, 2 * pairs), f32)],
-    )(place, near, far, near_sums, pool, tower_weights, turned_hits, more_turned_hits)
+    )(chip, near, far, near_sums, pool, tower_weights, turned_hits, more_turned_hits)
     returned = over_table(grads)
     more_returned = lax.cond(crowded, lambda: over_table(more_grads), lambda: nothing)
     codes = received[:, :base].reshape(1, -1)
@@ -512,13 +484,8 @@
         return call(
             functools.partial(column_body, side=side),
             shape((chips, per, width), dtype),
-            [SMEM] + [VMEM] * 4 + [pl.BlockSpec(memory_space=pl.ANY)],
-            [
-                pltpu.VMEM((chips * per, width), f32),
-                pltpu.VMEM((n_table * more, width), bf16),
-                pltpu.SemaphoreType.DMA,
-            ],
-        )(place, received, codes, more_codes, returned, more_returned)
+            [SMEM] + [VMEM] * 4,
+        )(chip, codes, more_codes, returned, more_returned)
 
     other = lax.ppermute(column(1, bf16), "dp", swap)
     both = call(add_body, shape((chips, per, width), bf16), [VMEM] * 2)(column(0, f32), other)

time: 237 us -> 238 us (level)
  starting transfers between devices: 42.3 us -> 51.1 us
  blocking collectives: 85.3 us -> 80.4 us
    ppermute x1, starting transfers between devices: 6.16 us -> 16.1 us  [on_device(): chip_rows = jnp.concatenate([own_rows, lax.ppermute(own_rows, 'dp', swap)])]
    all_to_all x1, blocking collectives: 35 us -> 27.8 us  [over_table(): lax.all_to_all(parts, 'table', split_axis=0, concat_axis=0, tiled=True)]
    all_to_all x2, waiting for transfers between devices: 79 us -> 73.3 us  [over_table(): lax.all_to_all(parts, 'table', split_axis=0, concat_axis=0, tiled=True)]
    all_to_all x1, starting transfers between devices: 7.64 us -> 3.47 us  [on_device(): lax.all_to_all(jnp.broadcast_to(chip_rows[None], (chips // 2, CORES * per...]
    all_to_all x1, waiting for transfers between devices: 5.14 us -> 9 us  [on_device(): lax.all_to_all(jnp.broadcast_to(chip_rows[None], (chips // 2, CORES * per...]
  transfers between devices with their start and end apart: 7 -> 7, of which waited for: 5 -> 6; matrix products, arithmetic and copies ran while one was open for 0% -> 0% of each run, Pallas kernels for 3% -> 2%
where the time goes in v5:
time: 238 us; the launch traced here: 237 us
  waiting for transfers between devices  84.6 us (36%)
  blocking collectives  80.4 us (34%)
  starting transfers between devices  51.1 us (21%)
  Pallas kernels  15.7 us (7%)
  local copies, waits for them, and re-layouts  2.73 us (1%)
    all_to_all x2, waiting for transfers between devices, over_table(): lax.all_to_all(parts, 'table', split_axis=0, concat_axis=0, tiled=True)  73.3 us
    all_to_all x2, blocking collectives, over_y(): lax.all_to_all(x, 'dp', split_axis=0, concat_axis=0, axis_index_groups=al...  52.6 us
    all_to_all x1, blocking collectives, over_table(): lax.all_to_all(parts, 'table', split_axis=0, concat_axis=0, tiled=True)  27.8 us
    ppermute x1, starting transfers between devices, on_device(): chip_rows = jnp.concatenate([own_rows, lax.ppermute(own_rows, 'dp', swap)])  16.1 us
    all_to_all x2, starting transfers between devices, over_table(): lax.all_to_all(parts, 'table', split_axis=0, concat_axis=0, tiled=True)  15.3 us
    all_to_all x1, waiting for transfers between devices, on_device(): lax.all_to_all(jnp.broadcast_to(chip_rows[None], (chips // 2, CORES * per...  9 us
    ppermute x1, starting transfers between devices, on_device(): far = lax.ppermute(near, 'dp', swap)  8.86 us
    ppermute x1, starting transfers between devices, on_device(): other = lax.ppermute(column(1, bf16), 'dp', swap)  5.52 us
  transfers between devices with their start and end apart: 7, of which 6 were waited for; matrix products, arithmetic and copies ran while one was open for 0% of the time, Pallas kernels for 2%

profile of v5, /device:TPU:1, one launch (start us, length us, event | category | flops | bytes accessed | tf_op | source)
XLA Modules:
  0.0 237.0 jit_solution(15106382607173443847)
XLA Ops:
  0.6 0.9 convert_element_type.10
  1.5 16.1 %collective-permute-start = (bf16[128,256]{1,0:T(8,128)(2,1)S(1)}, bf16[128,256]{1,0:T(8,128)(2,1)S(1)}, u32[]{:S(2)}, u32[]{:S(2)}) collective-permute-start(bf16[128,256]{1,0:T(8,128)(2,1)S(1)} %convert_element_type.10), channel_id=1, source_target_pairs={{0,64},{64,0},{128,192},{192,128},{256,320},{320,256},{384,448},{4... | collective-permute-start | bytes 196616 | tf_op jit(solution)/shard_map/ppermute | solution.py:390
  17.6 0.9 collective-permute-done
  18.5 0.8 broadcast_in_dim.12
  19.4 3.5 %all-to-all-start.2 = ((bf16[4,256,256]{2,1,0:T(8,128)(2,1)}), bf16[4,256,256]{2,1,0:T(8,128)(2,1)S(1)}, u32[]{:S(2)}, u32[]{:S(2)}) async-start(bf16[4,256,256]{2,1,0:T(8,128)(2,1)} %broadcast_in_dim.12), calls=%async_computation.2 | async-start | bytes 1048576 | tf_op jit(solution)/shard_map/all_to_all | solution.py:391
  22.9 0.6 copy-done.4
  23.6 2.2 shard_map.103
  25.8 9.0 %all-to-all-done.2.near_ref = bf16[4,256,256]{2,1,0:T(8,128)(2,1)S(1)} async-done(((bf16[4,256,256]{2,1,0:T(8,128)(2,1)}), bf16[4,256,256]{2,1,0:T(8,128)(2,1)S(1)}, u32[]{:S(2)}, u32[]{:S(2)}) %all-to-all-start.2) | async-done | bytes 524320 | tf_op jit(solution)/shard_map/all_to_all | solution.py:391
  34.8 1.9 collective-permute-start.1
  36.7 27.8 %all_to_all.40 = s32[64,1,40]{2,1,0:T(1,128)S(1)} all-to-all(s32[64,1,40]{2,1,0:T(1,128)S(1)} %bitcast.35), channel_id=1, replica_groups=mesh['dp'=16,'table'=64] {'table'}, dimensions={0} | all-to-all | bytes 20480 | tf_op jit(solution)/shard_map/all_to_all | solution.py:387
  64.5 2.9 %shard_map.104 = (bf16[1536,256]{1,0:T(8,128)(2,1)}, s32[1]{0:T(128)}) custom-call(s32[64,40]{1,0:T(8,128)S(1)} %bitcast.44, bf16[4,256,256]{2,1,0:T(8,128)(2,1)S(1)} %all-to-all-done.2.near_ref, bf16[4,256,256]{2,1,0:T(8,128)(2,1)S(1)} %collective-permute-done.1.next_ref), custom_call_target="tpu_custom_call" | custom-call | tf_op jit(solution)/shard_map/pallas_call | solution.py:416
  67.3 4.8 %all-to-all-start.4 = ((bf16[64,24,256]{2,1,0:T(8,128)(2,1)}), bf16[64,24,256]{2,1,0:T(8,128)(2,1)S(1)}, u32[]{:S(2)}, u32[]{:S(2)}) async-start(bf16[64,24,256]{2,1,0:T(8,128)(2,1)} %bitcast.18), calls=%async_computation.4 | async-start | bytes 1572864 | tf_op jit(solution)/shard_map/all_to_all | solution.py:387
  72.2 0.1 reshape.83.pos_ref
  72.3 0.1 reshape.84.more_pos_ref
  72.4 0.6 copy-done.6
  73.7 33.3 %all-to-all-done.4 = bf16[64,24,256]{2,1,0:T(8,128)(2,1)S(1)} async-done(((bf16[64,24,256]{2,1,0:T(8,128)(2,1)}), bf16[64,24,256]{2,1,0:T(8,128)(2,1)S(1)}, u32[]{:S(2)}, u32[]{:S(2)}) %all-to-all-start.4) | async-done | bytes 786464 | tf_op jit(solution)/shard_map/all_to_all | solution.py:387
  107.0 1.3 shard_map.105
  108.3 32.1 %all_to_all.41.near = bf16[8,256,256]{2,1,0:T(8,128)(2,1)S(1)} all-to-all(bf16[8,256,256]{2,1,0:T(8,128)(2,1)S(1)} %get-tuple-element.49), channel_id=1, replica_groups={{0,128,256,384,512,640,768,896},{64,192,320,448,576,704,832,960},{1,129..., dimensions={0} | all-to-all | bytes 2097152 | tf_op jit(solution)/shard_map/all_to_all | solution.py:381
  140.4 8.9 %collective-permute-start.2 = (bf16[8,256,256]{2,1,0:T(8,128)(2,1)S(1)}, bf16[8,256,256]{2,1,0:T(8,128)(2,1)S(1)}, u32[]{:S(2)}, u32[]{:S(2)}) collective-permute-start(bf16[8,256,256]{2,1,0:T(8,128)(2,1)S(1)} %all_to_all.41.near), channel_id=1, source_target_pairs={{0,64},{64,0},{128,192},{192,128},{256,320},{320,256},{384,448},{4... | collective-permute-start | bytes 3145736 | tf_op jit(solution)/shard_map/ppermute | solution.py:458
  149.2 0.8 shard_map.106
  150.1 1.3 collective-permute-done.2.far
  151.3 5.1 %shard_map.107 = (f32[1,128]{1,0:T(1,128)}, bf16[1536,256]{1,0:T(8,128)(2,1)}, bf16[512,256]{1,0:T(8,128)(2,1)S(1)}) custom-call(s32[1]{0:T(128)} %bitcast.4.y_ref, bf16[8,256,256]{2,1,0:T(8,128)(2,1)S(1)} %all_to_all.41.near, bf16[8,256,256]{2,1,0:T(8,128)(2,1)S(1)} %collective-permute-done.2.far, f32[8,1,128]{2,1,0:T(1,128)S(1)} %get-tuple-element.52.near_sums, ...), custom_call_target="tpu_custom_call" | custom-call | tf_op jit(solution)/shard_map/pallas_call | solution.py:468
  156.5 10.5 %all-to-all-start.6 = ((bf16[64,24,256]{2,1,0:T(8,128)(2,1)}), bf16[64,24,256]{2,1,0:T(8,128)(2,1)S(1)}, u32[]{:S(2)}, u32[]{:S(2)}) async-start(bf16[64,24,256]{2,1,0:T(8,128)(2,1)} %bitcast.23), calls=%async_computation.6 | async-start | bytes 1572864 | tf_op jit(solution)/shard_map/all_to_all | solution.py:387
  167.1 0.1 reshape.81.codes_ref
  167.2 0.1 reshape.82.more_codes_ref
  167.2 40.0 %all-to-all-done.6 = bf16[64,24,256]{2,1,0:T(8,128)(2,1)S(1)} async-done(((bf16[64,24,256]{2,1,0:T(8,128)(2,1)}), bf16[64,24,256]{2,1,0:T(8,128)(2,1)S(1)}, u32[]{:S(2)}, u32[]{:S(2)}) %all-to-all-start.6) | async-done | bytes 786464 | tf_op jit(solution)/shard_map/all_to_all | solution.py:387
  207.2 1.2 shard_map.109
  208.5 5.5 %collective-permute-start.3 = (bf16[8,128,256]{2,1,0:T(8,128)(2,1)S(1)}, bf16[8,128,256]{2,1,0:T(8,128)(2,1)S(1)}, u32[]{:S(2)}, u32[]{:S(2)}) collective-permute-start(bf16[8,128,256]{2,1,0:T(8,128)(2,1)S(1)} %shard_map.109), channel_id=1, source_target_pairs={{0,64},{64,0},{128,192},{192,128},{256,320},{320,256},{384,448},{4... | collective-permute-start | bytes 1572872 | tf_op jit(solution)/shard_map/ppermute | solution.py:490
  214.0 1.3 shard_map.108.a_ref
  215.3 0.2 collective-permute-done.3.b_ref
  215.6 20.5 %all_to_all.42.parts_ref = bf16[8,128,256]{2,1,0:T(8,128)(2,1)S(1)} all-to-all(bf16[8,128,256]{2,1,0:T(8,128)(2,1)S(1)} %shard_map.110), channel_id=1, replica_groups={{0,128,256,384,512,640,768,896},{64,192,320,448,576,704,832,960},{1,129..., dimensions={0} | all-to-all | bytes 1048576 | tf_op jit(solution)/shard_map/all_to_all | solution.py:381
  236.2 0.9 shard_map.111
  (24 shorter events, 0.5 us)
Async XLA Ops:
  1.5 16.9 %collective-permute-start = (bf16[128,256]{1,0:T(8,128)(2,1)S(1)}, bf16[128,256]{1,0:T(8,128)(2,1)S(1)}, u32[]{:S(2)}, u32[]{:S(2)}) collective-permute-start(bf16[128,256]{1,0:T(8,128)(2,1)S(1)} %convert_element_type.10), channel_id=1, source_target_pairs={{0,64},{64,0},{128,192},{192,128},{256,320},{320,256},{384,448},{4... | collective-permute-start | bytes 196616 | tf_op jit(solution)/shard_map/ppermute | solution.py:390
  19.4 15.4 %all-to-all-start.2 = ((bf16[4,256,256]{2,1,0:T(8,128)(2,1)}), bf16[4,256,256]{2,1,0:T(8,128)(2,1)S(1)}, u32[]{:S(2)}, u32[]{:S(2)}) async-start(bf16[4,256,256]{2,1,0:T(8,128)(2,1)} %broadcast_in_dim.12), calls=%async_computation.2 | async-start | bytes 1048576 | tf_op jit(solution)/shard_map/all_to_all | solution.py:391
  22.8 0.7 copy-start.4
  22.9 0.7 copy-start.3
  22.9 0.7 copy-start.2
  22.9 0.7 copy-start.1
  22.9 0.7 copy-start.5
  34.8 29.7 %collective-permute-start.1 = (bf16[4,256,256]{2,1,0:T(8,128)(2,1)S(1)}, bf16[4,256,256]{2,1,0:T(8,128)(2,1)S(1)}, u32[]{:S(2)}, u32[]{:S(2)}) collective-permute-start(bf16[4,256,256]{2,1,0:T(8,128)(2,1)S(1)} %all-to-all-done.2.near_ref), channel_id=1, source_target_pairs={{0,896},{64,192},{128,0},{192,320},{256,128},{320,448},{384,256},{... | collective-permute-start | bytes 1572872 | tf_op jit(solution)/shard_map/ppermute | solution.py:412
  67.3 5.1 %copy-start.7 = (bf16[256,256]{1,0:T(8,128)(2,1)S(1)}, bf16[256,256]{1,0:T(8,128)(2,1)}, u32[]{:S(2)}) copy-start(bf16[256,256]{1,0:T(8,128)(2,1)} %param.14) | copy-start | bytes 393220
  67.3 39.6 %all-to-all-start.4 = ((bf16[64,24,256]{2,1,0:T(8,128)(2,1)}), bf16[64,24,256]{2,1,0:T(8,128)(2,1)S(1)}, u32[]{:S(2)}, u32[]{:S(2)}) async-start(bf16[64,24,256]{2,1,0:T(8,128)(2,1)} %bitcast.18), calls=%async_computation.4 | async-start | bytes 1572864 | tf_op jit(solution)/shard_map/all_to_all | solution.py:387
  72.1 0.9 copy-start.6
  140.4 10.9 %collective-permute-start.2 = (bf16[8,256,256]{2,1,0:T(8,128)(2,1)S(1)}, bf16[8,256,256]{2,1,0:T(8,128)(2,1)S(1)}, u32[]{:S(2)}, u32[]{:S(2)}) collective-permute-start(bf16[8,256,256]{2,1,0:T(8,128)(2,1)S(1)} %all_to_all.41.near), channel_id=1, source_target_pairs={{0,64},{64,0},{128,192},{192,128},{256,320},{320,256},{384,448},{4... | collective-permute-start | bytes 3145736 | tf_op jit(solution)/shard_map/ppermute | solution.py:458
  156.5 50.8 %all-to-all-start.6 = ((bf16[64,24,256]{2,1,0:T(8,128)(2,1)}), bf16[64,24,256]{2,1,0:T(8,128)(2,1)S(1)}, u32[]{:S(2)}, u32[]{:S(2)}) async-start(bf16[64,24,256]{2,1,0:T(8,128)(2,1)} %bitcast.23), calls=%async_computation.6 | async-start | bytes 1572864 | tf_op jit(solution)/shard_map/all_to_all | solution.py:387
  208.5 7.0 %collective-permute-start.3 = (bf16[8,128,256]{2,1,0:T(8,128)(2,1)S(1)}, bf16[8,128,256]{2,1,0:T(8,128)(2,1)S(1)}, u32[]{:S(2)}, u32[]{:S(2)}) collective-permute-start(bf16[8,128,256]{2,1,0:T(8,128)(2,1)S(1)} %shard_map.109), channel_id=1, source_target_pairs={{0,64},{64,0},{128,192},{192,128},{256,320},{320,256},{384,448},{4... | collective-permute-start | bytes 1572872 | tf_op jit(solution)/shard_map/ppermute | solution.py:490
  215.6 20.5 %copy-start = (f32[128,256]{1,0:T(8,128)S(1)}, f32[128,256]{1,0:T(8,128)}, u32[]{:S(2)}) copy-start(f32[128,256]{1,0:T(8,128)} %table_ref.1) | copy-start | bytes 393220

commit v6 on v5

--- a/solution.py
+++ b/solution.py
@@ -98,7 +98,7 @@
         used = jnp.sum(jnp.where(here, spread[depth:], 0.0), axis=0, keepdims=True)
         y = r % rows
         apart = jnp.where(parity == y % 2, 0, rows // 2).astype(jnp.float32)
-        square[r : r + 1, :] = value + ((apart + y // 2) * CORES + side) * LANES
+        square[r : r + 1, :] = value + (side * rows + apart + y // 2) * LANES
         square[2 * entries + r : 2 * entries + r + 1, :] = used
     turned = square[...].T
 
@@ -125,26 +125,39 @@
     req_ref[:, slots:] = jnp.broadcast_to(over, (groups, req_ref.shape[1] - slots))
 
 
-def pick_body(recv_ref, near_ref, next_ref, out_ref, over_ref, square, *, first, count, slots):
-    groups = recv_ref.shape[0]
-    square[...] = jnp.zeros_like(square)
-    square[:groups, : recv_ref.shape[1]] = recv_ref[...].astype(jnp.float32)
-    turned = square[...].T.astype(jnp.int32)
-    over_ref[0] = jnp.max(turned[slots : slots + 1, :groups])
-    rows = jnp.concatenate([ref[...].reshape(-1, ref.shape[-1]) for ref in (near_ref, next_ref)], axis=0)
+def pick_rows(turned_ref, row_refs, out_ref, first, count, begin):
+    groups = out_ref.shape[0] // count
+    rows = jnp.concatenate([ref[...].reshape(-1, ref.shape[-1]) for ref in row_refs], axis=0)
     lane = iota((count, LANES), 1)
     step = 8
     for t in range(0, groups, step):
         hot = []
         for u in range(t, t + step):
-            code = jnp.broadcast_to(turned[first : first + count, u : u + 1], (count, LANES))
+            code = jnp.broadcast_to(turned_ref[first : first + count, u : u + 1], (count, LANES))
             hot.append(
                 jnp.concatenate(
-                    [hits(lane + b * LANES, code) for b in range(rows.shape[0] // LANES)], axis=1
+                    [hits(lane + (begin + b * LANES), code) for b in range(rows.shape[0] // LANES)],
+                    axis=1,
                 )
             )
         hot = jnp.concatenate(hot, axis=0).astype(jnp.bfloat16)
-        out_ref[t * count : (t + step) * count, :] = dot(hot, rows).astype(jnp.bfloat16)
+        yield pl.ds(t * count, step * count), dot(hot, rows)
+
+
+def pick_near_body(recv_ref, near_ref, next_ref, out_ref, turned_ref, over_ref, square, *, first, count, slots):
+    groups = recv_ref.shape[0]
+    square[...] = jnp.zeros_like(square)
+    square[:groups, : recv_ref.shape[1]] = recv_ref[...].astype(jnp.float32)
+    turned_ref[...] = square[...].T.astype(jnp.int32)
+    over_ref[0] = jnp.max(turned_ref[slots : slots + 1, :groups])
+    for span, got in pick_rows(turned_ref, (near_ref, next_ref), out_ref, first, count, 0):
+        out_ref[span, :] = got.astype(jnp.bfloat16)
+
+
+def pick_far_body(turned_ref, far_ref, near_got, out_ref, *, first, count):
+    begin = far_ref.shape[0] * far_ref.shape[1]
+    for span, got in pick_rows(turned_ref, (far_ref,), out_ref, first, count, begin):
+        out_ref[span, :] = (got + near_got[span, :].astype(jnp.float32)).astype(jnp.bfloat16)
 
 
 def project(pool, weight):
@@ -208,13 +221,21 @@
     return jnp.exp2(products * (scale_of(width) * math.log2(math.e)))
 
 
-def near_body(near, hits_ref, more_hits_ref, sums_ref, turned_ref, more_turned_ref):
+def near_body(
+    near, pool_ref, weights_ref, hits_ref, more_hits_ref,
+    sums_ref, normed_ref, factor_ref, turned_ref, more_turned_ref,
+):
     chips, both, width = near.shape
     pairs = both // 2
     step = 256
     for weights, out in ((hits_ref, turned_ref), (more_hits_ref, more_turned_ref)):
         for s in range(0, weights.shape[1], step):
             out[s : s + step, :] = weights[:, s : s + step].T
+    for side in range(2):
+        span = pl.ds(side * pairs, pairs)
+        normed, factor = project(pool_ref[span, :], weights_ref[side])
+        normed_ref[span, :] = normed
+        factor_ref[span, :] = jnp.broadcast_to(factor, (pairs, LANES))
     for y in range(0, chips, 2):
         q = jnp.concatenate([near[y, pairs:, :], near[y + 1, pairs:, :]], axis=0)
         total = jnp.zeros((8, both), jnp.float32)
@@ -228,7 +249,7 @@
 
 
 def loss_body(
-    y_ref, near, far, near_sums, pool_ref, weights_ref, turned_ref, more_turned_ref,
+    y_ref, near, far, near_sums, normed_ref, factor_ref, weights_ref, turned_ref, more_turned_ref,
     loss_ref, grads_ref, more_grads_ref, inverse, own_exp,
 ):
     chips, both, width = near.shape
@@ -296,32 +317,25 @@
     for side, grad in enumerate((grad_item, grad_query)):
         span = pl.ds(side * pairs, pairs)
         grad = grad * scale
-        normed, factor = project(pool_ref[span, :], weights_ref[side])
+        normed, factor = normed_ref[span, :], factor_ref[span, 0:1]
         inner_mean = jnp.mean(grad * normed, axis=1, keepdims=True)
         grad_hidden = (factor * (grad - normed * inner_mean)).astype(jnp.bfloat16)
         backs.append(dot(grad_hidden, weights_ref[side], NT))
-    back = jnp.concatenate(backs, axis=0)
-    high = back.astype(jnp.bfloat16)
-    low = (back - high.astype(jnp.float32)).astype(jnp.bfloat16)
-    split = jnp.concatenate([high, low], axis=1)
-    step = 256
+    back = jnp.concatenate(backs, axis=0).astype(jnp.bfloat16)
     for weights, out in ((turned_ref, grads_ref), (more_turned_ref, more_grads_ref)):
-        for s in range(0, weights.shape[0], step):
-            parts = dot(weights[s : s + step, :], split)
-            out[s : s + step, :] = (parts[:, :width] + parts[:, width:]).astype(jnp.bfloat16)
+        out[...] = dot(weights[...], back).astype(jnp.bfloat16)
 
 
 def column_body(y_ref, codes_ref, more_codes_ref, grads_ref, more_grads_ref, out_ref, *, side):
     chips, per = out_ref.shape[:2]
     parity = y_ref[0] % 2
     for n in range(0, chips, 2):
+        begin = (side * chips + n) * per
         total = None
         for codes, grads in ((codes_ref, grads_ref), (more_codes_ref, more_grads_ref)):
-            hot = [
-                hits(iota((per, codes.shape[1]), 0), codes[...] - ((n + u) * CORES + side) * per)
-                for u in range(2)
-            ]
-            part = dot(jnp.concatenate(hot, axis=0).astype(jnp.bfloat16), grads[...])
+            down = iota((2 * per, codes.shape[1]), 0)
+            hot = hits(down, codes[...] - begin).astype(jnp.bfloat16)
+            part = dot(hot, grads[...])
             total = part if total is None else total + part
         for u in range(2):
             half, k = divmod(n + u, chips // 2)
@@ -386,10 +400,8 @@
         parts = x.reshape(n_table, -1, x.shape[-1])
         return lax.all_to_all(parts, "table", split_axis=0, concat_axis=0, tiled=True).reshape(x.shape)
 
-    own_rows = table.astype(bf16)
-    chip_rows = jnp.concatenate([own_rows, lax.ppermute(own_rows, "dp", swap)])
     near_rows = lax.all_to_all(
-        jnp.broadcast_to(chip_rows[None], (chips // 2, CORES * per, width)),
+        jnp.broadcast_to(table.astype(bf16)[None], (chips // 2, per, width)),
         "dp",
         split_axis=0,
         concat_axis=0,
@@ -411,15 +423,21 @@
     near_rows, requests = lax.optimization_barrier((near_rows, requests))
     next_rows = lax.ppermute(near_rows, "dp", beside)
     received = over_table(requests)
+    received, near_rows, next_rows = lax.optimization_barrier((received, near_rows, next_rows))
+    far_rows = lax.ppermute(jnp.concatenate([near_rows, next_rows]), "dp", swap)
 
     def pick(first, count, received):
-        return call(
-            functools.partial(pick_body, first=first, count=count, slots=slots),
-            (shape((n_table * count, width), bf16), shape((1,), i32)),
+        picked = shape((n_table * count, width), bf16)
+        near_got, turned, over = call(
+            functools.partial(pick_near_body, first=first, count=count, slots=slots),
+            (picked, shape((LANES, LANES), i32), shape((1,), i32)),
             [VMEM] * 3,
             [pltpu.VMEM((LANES, LANES), f32)],
-            out_specs=(VMEM, SMEM),
+            out_specs=(VMEM, VMEM, SMEM),
         )(received, near_rows, next_rows)
+        return call(
+            functools.partial(pick_far_body, first=first, count=count), picked, [VMEM] * 3
+        )(turned, far_rows, near_got), over
 
     picked, over = pick(0, base, received)
     fetched = over_table(picked)
@@ -456,15 +474,17 @@
     )
     near = over_y(spread)
     far = lax.ppermute(near, "dp", swap)
-    near_sums, turned_hits, more_turned_hits = call(
+    near_sums, normed, factor, turned_hits, more_turned_hits = call(
         near_body,
         (
             shape((chips, 1, pairs), f32),
+            shape((2 * pairs, width), f32),
+            shape((2 * pairs, LANES), f32),
             shape((n_table * base, 2 * pairs), bf16),
             shape((n_table * more, 2 * pairs), bf16),
         ),
-        [VMEM] * 3,
-    )(near, pair_hits, more_hits)
+        [VMEM] * 5,
+    )(near, pool, tower_weights, pair_hits, more_hits)
     loss, grads, more_grads = call(
         loss_body,
         (
@@ -472,9 +492,9 @@
             shape((n_table * base, width), bf16),
             shape((n_table * more, width), bf16),
         ),
-        [SMEM] + [VMEM] * 7,
+        [SMEM] + [VMEM] * 8,
         [pltpu.VMEM((chips, 1, 2 * pairs), f32), pltpu.VMEM((chips, pairs, 2 * pairs), f32)],
-    )(chip, near, far, near_sums, pool, tower_weights, turned_hits, more_turned_hits)
+    )(chip, near, far, near_sums, normed, factor, tower_weights, turned_hits, more_turned_hits)
     returned = over_table(grads)
     more_returned = lax.cond(crowded, lambda: over_table(more_grads), lambda: nothing)
     codes = received[:, :base].reshape(1, -1)

time: 238 us -> 236 us (level)
  starting transfers between devices: 51.1 us -> 42.3 us
  blocking collectives: 80.4 us -> 85.3 us
    ppermute x1, starting transfers between devices: 16.1 us -> 6.16 us  [on_device(): far_rows = lax.ppermute(jnp.concatenate([near_rows, next_rows]), 'dp', swap)]
    all_to_all x1, blocking collectives: 27.8 us -> 35 us  [over_table(): lax.all_to_all(parts, 'table', split_axis=0, concat_axis=0, tiled=True)]
    all_to_all x2, waiting for transfers between devices: 73.3 us -> 79 us  [over_table(): lax.all_to_all(parts, 'table', split_axis=0, concat_axis=0, tiled=True)]
    all_to_all x1, starting transfers between devices: 3.47 us -> 7.64 us  [on_device(): lax.all_to_all(jnp.broadcast_to(table.astype(bf16)[None], (chips // 2, pe...]
    all_to_all x1, waiting for transfers between devices: 9 us -> 5.73 us  [on_device(): lax.all_to_all(jnp.broadcast_to(table.astype(bf16)[None], (chips // 2, pe...]
  transfers between devices with their start and end apart: 7 -> 7, of which waited for: 6 -> 5; matrix products, arithmetic and copies ran while one was open for 0% -> 0% of each run, Pallas kernels for 2% -> 2%
where the time goes in v6:
time: 236 us; the launch traced here: 235 us
  waiting for transfers between devices  86.2 us (37%)
  blocking collectives  85.3 us (36%)
  starting transfers between devices  42.3 us (18%)
  Pallas kernels  16.3 us (7%)
  local copies, waits for them, and re-layouts  2.61 us (1%)
    all_to_all x2, waiting for transfers between devices, over_table(): lax.all_to_all(parts, 'table', split_axis=0, concat_axis=0, tiled=True)  79 us
    all_to_all x2, blocking collectives, over_y(): lax.all_to_all(x, 'dp', split_axis=0, concat_axis=0, axis_index_groups=al...  50.3 us
    all_to_all x1, blocking collectives, over_table(): lax.all_to_all(parts, 'table', split_axis=0, concat_axis=0, tiled=True)  35 us
    all_to_all x2, starting transfers between devices, over_table(): lax.all_to_all(parts, 'table', split_axis=0, concat_axis=0, tiled=True)  13.6 us
    all_to_all x1, starting transfers between devices, on_device(): lax.all_to_all(jnp.broadcast_to(table.astype(bf16)[None], (chips // 2, pe...  7.64 us
    ppermute x1, starting transfers between devices, on_device(): far = lax.ppermute(near, 'dp', swap)  7.41 us
    ppermute x1, starting transfers between devices, on_device(): far_rows = lax.ppermute(jnp.concatenate([near_rows, next_rows]), 'dp', swap)  6.16 us
    all_to_all x1, waiting for transfers between devices, on_device(): lax.all_to_all(jnp.broadcast_to(table.astype(bf16)[None], (chips // 2, pe...  5.73 us
  transfers between devices with their start and end apart: 7, of which 5 were waited for; matrix products, arithmetic and copies ran while one was open for 0% of the time, Pallas kernels for 2%

profile of v6, /device:TPU:1, one launch (start us, length us, event | category | flops | bytes accessed | tf_op | source)
XLA Modules:
  0.0 235.1 jit_solution(9782378238131007276)
XLA Ops:
  0.6 0.9 convert_element_type.10
  1.5 0.7 broadcast_in_dim.12
  2.3 7.6 %all-to-all-start.2 = ((bf16[4,128,256]{2,1,0:T(8,128)(2,1)}), bf16[4,128,256]{2,1,0:T(8,128)(2,1)S(1)}, u32[]{:S(2)}, u32[]{:S(2)}) async-start(bf16[4,128,256]{2,1,0:T(8,128)(2,1)} %broadcast_in_dim.12), calls=%async_computation.2 | async-start | bytes 524288 | tf_op jit(solution)/shard_map/all_to_all | solution.py:403
  9.9 0.7 copy-done.4
  10.6 2.2 shard_map.103
  12.8 5.7 %all-to-all-done.2.near_ref = bf16[4,128,256]{2,1,0:T(8,128)(2,1)S(1)} async-done(((bf16[4,128,256]{2,1,0:T(8,128)(2,1)}), bf16[4,128,256]{2,1,0:T(8,128)(2,1)S(1)}, u32[]{:S(2)}, u32[]{:S(2)}) %all-to-all-start.2) | async-done | bytes 262176 | tf_op jit(solution)/shard_map/all_to_all | solution.py:403
  18.5 1.9 collective-permute-start
  20.5 35.0 %all_to_all.40 = s32[64,1,40]{2,1,0:T(1,128)S(1)} all-to-all(s32[64,1,40]{2,1,0:T(1,128)S(1)} %bitcast.35), channel_id=1, replica_groups=mesh['dp'=16,'table'=64] {'table'}, dimensions={0} | all-to-all | bytes 20480 | tf_op jit(solution)/shard_map/all_to_all | solution.py:401
  55.5 6.2 %collective-permute-start.1 = (bf16[8,128,256]{2,1,0:T(8,128)(2,1)S(1)}, bf16[8,128,256]{2,1,0:T(8,128)(2,1)S(1)}, u32[]{:S(2)}, u32[]{:S(2)}) collective-permute-start(bf16[8,128,256]{2,1,0:T(8,128)(2,1)S(1)} %pad_maximum_fusion), channel_id=1, source_target_pairs={{0,64},{64,0},{128,192},{192,128},{256,320},{320,256},{384,448},{4... | collective-permute-start | bytes 1572872 | tf_op jit(solution)/shard_map/ppermute | solution.py:427
  61.6 1.5 shard_map.104
  63.2 2.0 shard_map.105
  65.1 4.8 %all-to-all-start.4 = ((bf16[64,24,256]{2,1,0:T(8,128)(2,1)}), bf16[64,24,256]{2,1,0:T(8,128)(2,1)S(1)}, u32[]{:S(2)}, u32[]{:S(2)}) async-start(bf16[64,24,256]{2,1,0:T(8,128)(2,1)} %bitcast.18), calls=%async_computation.4 | async-start | bytes 1572864 | tf_op jit(solution)/shard_map/all_to_all | solution.py:401
  70.0 0.1 reshape.83.pos_ref
  70.1 0.1 reshape.84.more_pos_ref
  70.2 0.6 copy-done.6
  71.5 39.0 %all-to-all-done.4 = bf16[64,24,256]{2,1,0:T(8,128)(2,1)S(1)} async-done(((bf16[64,24,256]{2,1,0:T(8,128)(2,1)}), bf16[64,24,256]{2,1,0:T(8,128)(2,1)S(1)}, u32[]{:S(2)}, u32[]{:S(2)}) %all-to-all-start.4) | async-done | bytes 786464 | tf_op jit(solution)/shard_map/all_to_all | solution.py:401
  110.6 1.3 shard_map.106
  111.8 29.8 %all_to_all.41.near = bf16[8,256,256]{2,1,0:T(8,128)(2,1)S(1)} all-to-all(bf16[8,256,256]{2,1,0:T(8,128)(2,1)S(1)} %get-tuple-element.63), channel_id=1, replica_groups={{0,128,256,384,512,640,768,896},{64,192,320,448,576,704,832,960},{1,129..., dimensions={0} | all-to-all | bytes 2097152 | tf_op jit(solution)/shard_map/all_to_all | solution.py:395
  141.6 7.4 %collective-permute-start.2 = (bf16[8,256,256]{2,1,0:T(8,128)(2,1)S(1)}, bf16[8,256,256]{2,1,0:T(8,128)(2,1)S(1)}, u32[]{:S(2)}, u32[]{:S(2)}) collective-permute-start(bf16[8,256,256]{2,1,0:T(8,128)(2,1)S(1)} %all_to_all.41.near), channel_id=1, source_target_pairs={{0,64},{64,0},{128,192},{192,128},{256,320},{320,256},{384,448},{4... | collective-permute-start | bytes 3145736 | tf_op jit(solution)/shard_map/ppermute | solution.py:476
  149.1 0.9 shard_map.107
  150.0 1.2 collective-permute-done.2.far
  151.1 5.1 %shard_map.108 = (f32[1,128]{1,0:T(1,128)}, bf16[1536,256]{1,0:T(8,128)(2,1)}, bf16[512,256]{1,0:T(8,128)(2,1)S(1)}) custom-call(s32[1]{0:T(128)} %bitcast.4.y_ref, bf16[8,256,256]{2,1,0:T(8,128)(2,1)S(1)} %all_to_all.41.near, bf16[8,256,256]{2,1,0:T(8,128)(2,1)S(1)} %collective-permute-done.2.far, f32[8,1,128]{2,1,0:T(1,128)S(1)} %get-tuple-element.67.near_sums, ...), custom_call_target="tpu_custom_call" | custom-call | tf_op jit(solution)/shard_map/pallas_call | solution.py:488
  156.2 8.9 %all-to-all-start.6 = ((bf16[64,24,256]{2,1,0:T(8,128)(2,1)}), bf16[64,24,256]{2,1,0:T(8,128)(2,1)S(1)}, u32[]{:S(2)}, u32[]{:S(2)}) async-start(bf16[64,24,256]{2,1,0:T(8,128)(2,1)} %bitcast.23), calls=%async_computation.6 | async-start | bytes 1572864 | tf_op jit(solution)/shard_map/all_to_all | solution.py:401
  165.2 0.1 reshape.81.codes_ref
  165.3 0.1 reshape.82.more_codes_ref
  165.4 40.0 %all-to-all-done.6 = bf16[64,24,256]{2,1,0:T(8,128)(2,1)S(1)} async-done(((bf16[64,24,256]{2,1,0:T(8,128)(2,1)}), bf16[64,24,256]{2,1,0:T(8,128)(2,1)S(1)}, u32[]{:S(2)}, u32[]{:S(2)}) %all-to-all-start.6) | async-done | bytes 786464 | tf_op jit(solution)/shard_map/all_to_all | solution.py:401
  205.4 1.2 shard_map.110
  206.6 5.5 %collective-permute-start.3 = (bf16[8,128,256]{2,1,0:T(8,128)(2,1)S(1)}, bf16[8,128,256]{2,1,0:T(8,128)(2,1)S(1)}, u32[]{:S(2)}, u32[]{:S(2)}) collective-permute-start(bf16[8,128,256]{2,1,0:T(8,128)(2,1)S(1)} %shard_map.110), channel_id=1, source_target_pairs={{0,64},{64,0},{128,192},{192,128},{256,320},{320,256},{384,448},{4... | collective-permute-start | bytes 1572872 | tf_op jit(solution)/shard_map/ppermute | solution.py:510
  212.2 1.3 shard_map.109.a_ref
  213.4 0.2 collective-permute-done.3.b_ref
  213.8 20.5 %all_to_all.42.parts_ref = bf16[8,128,256]{2,1,0:T(8,128)(2,1)S(1)} all-to-all(bf16[8,128,256]{2,1,0:T(8,128)(2,1)S(1)} %shard_map.111), channel_id=1, replica_groups={{0,128,256,384,512,640,768,896},{64,192,320,448,576,704,832,960},{1,129..., dimensions={0} | all-to-all | bytes 1048576 | tf_op jit(solution)/shard_map/all_to_all | solution.py:395
  234.3 0.9 shard_map.112
  (25 shorter events, 0.5 us)
Async XLA Ops:
  2.3 16.3 %all-to-all-start.2 = ((bf16[4,128,256]{2,1,0:T(8,128)(2,1)}), bf16[4,128,256]{2,1,0:T(8,128)(2,1)S(1)}, u32[]{:S(2)}, u32[]{:S(2)}) async-start(bf16[4,128,256]{2,1,0:T(8,128)(2,1)} %broadcast_in_dim.12), calls=%async_computation.2 | async-start | bytes 524288 | tf_op jit(solution)/shard_map/all_to_all | solution.py:403
  9.9 0.7 copy-start.4
  9.9 0.7 copy-start.3
  9.9 0.7 copy-start.2
  9.9 0.7 copy-start.1
  9.9 0.7 copy-start.5
  18.5 36.9 %collective-permute-start = (bf16[4,128,256]{2,1,0:T(8,128)(2,1)S(1)}, bf16[4,128,256]{2,1,0:T(8,128)(2,1)S(1)}, u32[]{:S(2)}, u32[]{:S(2)}) collective-permute-start(bf16[4,128,256]{2,1,0:T(8,128)(2,1)S(1)} %all-to-all-done.2.near_ref), channel_id=1, source_target_pairs={{0,896},{64,192},{128,0},{192,320},{256,128},{320,448},{384,256},{... | collective-permute-start | bytes 786440 | tf_op jit(solution)/shard_map/ppermute | solution.py:424
  55.5 7.7 %collective-permute-start.1 = (bf16[8,128,256]{2,1,0:T(8,128)(2,1)S(1)}, bf16[8,128,256]{2,1,0:T(8,128)(2,1)S(1)}, u32[]{:S(2)}, u32[]{:S(2)}) collective-permute-start(bf16[8,128,256]{2,1,0:T(8,128)(2,1)S(1)} %pad_maximum_fusion), channel_id=1, source_target_pairs={{0,64},{64,0},{128,192},{192,128},{256,320},{320,256},{384,448},{4... | collective-permute-start | bytes 1572872 | tf_op jit(solution)/shard_map/ppermute | solution.py:427
  65.1 5.1 %copy-start.7 = (bf16[256,256]{1,0:T(8,128)(2,1)S(1)}, bf16[256,256]{1,0:T(8,128)(2,1)}, u32[]{:S(2)}) copy-start(bf16[256,256]{1,0:T(8,128)(2,1)} %param.14) | copy-start | bytes 393220
  65.1 45.4 %all-to-all-start.4 = ((bf16[64,24,256]{2,1,0:T(8,128)(2,1)}), bf16[64,24,256]{2,1,0:T(8,128)(2,1)S(1)}, u32[]{:S(2)}, u32[]{:S(2)}) async-start(bf16[64,24,256]{2,1,0:T(8,128)(2,1)} %bitcast.18), calls=%async_computation.4 | async-start | bytes 1572864 | tf_op jit(solution)/shard_map/all_to_all | solution.py:401
  69.9 0.9 copy-start.6
  141.6 9.5 %collective-permute-start.2 = (bf16[8,256,256]{2,1,0:T(8,128)(2,1)S(1)}, bf16[8,256,256]{2,1,0:T(8,128)(2,1)S(1)}, u32[]{:S(2)}, u32[]{:S(2)}) collective-permute-start(bf16[8,256,256]{2,1,0:T(8,128)(2,1)S(1)} %all_to_all.41.near), channel_id=1, source_target_pairs={{0,64},{64,0},{128,192},{192,128},{256,320},{320,256},{384,448},{4... | collective-permute-start | bytes 3145736 | tf_op jit(solution)/shard_map/ppermute | solution.py:476
  156.2 49.1 %all-to-all-start.6 = ((bf16[64,24,256]{2,1,0:T(8,128)(2,1)}), bf16[64,24,256]{2,1,0:T(8,128)(2,1)S(1)}, u32[]{:S(2)}, u32[]{:S(2)}) async-start(bf16[64,24,256]{2,1,0:T(8,128)(2,1)} %bitcast.23), calls=%async_computation.6 | async-start | bytes 1572864 | tf_op jit(solution)/shard_map/all_to_all | solution.py:401
  206.6 7.0 %collective-permute-start.3 = (bf16[8,128,256]{2,1,0:T(8,128)(2,1)S(1)}, bf16[8,128,256]{2,1,0:T(8,128)(2,1)S(1)}, u32[]{:S(2)}, u32[]{:S(2)}) collective-permute-start(bf16[8,128,256]{2,1,0:T(8,128)(2,1)S(1)} %shard_map.110), channel_id=1, source_target_pairs={{0,64},{64,0},{128,192},{192,128},{256,320},{320,256},{384,448},{4... | collective-permute-start | bytes 1572872 | tf_op jit(solution)/shard_map/ppermute | solution.py:510
  213.8 20.5 %copy-start = (f32[128,256]{1,0:T(8,128)S(1)}, f32[128,256]{1,0:T(8,128)}, u32[]{:S(2)}) copy-start(f32[128,256]{1,0:T(8,128)} %table_ref.1) | copy-start | bytes 393220

commit v7 on v6

--- a/solution.py
+++ b/solution.py
@@ -408,7 +408,6 @@
         axis_index_groups=along_parity,
         tiled=True,
     )
-    tower_weights = jnp.stack([item_weight, query_weight])
     items, queries = item_refs[0, 0].T, query_refs[0, 0].T
     requests, places, old_accum = call(
         functools.partial(request_body, base=base),
@@ -426,26 +425,41 @@
     received, near_rows, next_rows = lax.optimization_barrier((received, near_rows, next_rows))
     far_rows = lax.ppermute(jnp.concatenate([near_rows, next_rows]), "dp", swap)
 
-    def pick(first, count, received):
-        picked = shape((n_table * count, width), bf16)
-        near_got, turned, over = call(
+    def pick_near(first, count, received):
+        return call(
             functools.partial(pick_near_body, first=first, count=count, slots=slots),
-            (picked, shape((LANES, LANES), i32), shape((1,), i32)),
+            (shape((n_table * count, width), bf16), shape((LANES, LANES), i32), shape((1,), i32)),
             [VMEM] * 3,
             [pltpu.VMEM((LANES, LANES), f32)],
             out_specs=(VMEM, VMEM, SMEM),
         )(received, near_rows, next_rows)
+
+    def pick_far(first, count, turned, near_got):
         return call(
-            functools.partial(pick_far_body, first=first, count=count), picked, [VMEM] * 3
-        )(turned, far_rows, near_got), over
-
-    picked, over = pick(0, base, received)
-    fetched = over_table(picked)
-    crowded = over[0] > 0
+            functools.partial(pick_far_body, first=first, count=count),
+            shape((n_table * count, width), bf16),
+            [VMEM] * 3,
+        )(turned, far_rows, near_got)
+
+    near_got, turned, over = pick_near(0, base, received)
+    near_got, crowded, base_pos, more_pos, codes, more_codes, tower_weights = lax.optimization_barrier(
+        (
+            near_got,
+            over[0] > 0,
+            places[:, :base].reshape(1, -1),
+            places[:, base:].reshape(1, -1),
+            received[:, :base].reshape(1, -1),
+            received[:, base:slots].reshape(1, -1),
+            jnp.stack([item_weight, query_weight]),
+        )
+    )
+    fetched = over_table(pick_far(0, base, turned, near_got))
     nothing = jnp.zeros((n_table * more, width), bf16)
     late, fetched = lax.optimization_barrier((received, fetched))
     more_fetched = lax.cond(
-        crowded, lambda: over_table(pick(base, more, late)[0]), lambda: nothing
+        crowded,
+        lambda: over_table(pick_far(base, more, turned, pick_near(base, more, late)[0])),
+        lambda: nothing,
     )
     pair_hits, more_hits, pool, spread = call(
         tower_body,
@@ -464,8 +478,8 @@
         ],
     )(
         received,
-        places[:, :base].reshape(1, -1),
-        places[:, base:].reshape(1, -1),
+        base_pos,
+        more_pos,
         items,
         queries,
         fetched,
@@ -497,8 +511,6 @@
     )(chip, near, far, near_sums, normed, factor, tower_weights, turned_hits, more_turned_hits)
     returned = over_table(grads)
     more_returned = lax.cond(crowded, lambda: over_table(more_grads), lambda: nothing)
-    codes = received[:, :base].reshape(1, -1)
-    more_codes = received[:, base:slots].reshape(1, -1)
 
     def column(side, dtype):
         return call(

time: 236 us -> 236 us (level)
  blocking collectives: 85.3 us -> 134 us
  waiting for transfers between devices: 86.2 us -> 48.2 us
  starting transfers between devices: 42.3 us -> 32.8 us
    all_to_all x1 -> x2, blocking collectives: 35 us -> 83.5 us  [over_table(): lax.all_to_all(parts, 'table', split_axis=0, concat_axis=0, tiled=True)]
    all_to_all x2 -> x1, waiting for transfers between devices: 79 us -> 41.1 us  [over_table(): lax.all_to_all(parts, 'table', split_axis=0, concat_axis=0, tiled=True)]
    all_to_all x2 -> x1, starting transfers between devices: 13.6 us -> 4.64 us  [over_table(): lax.all_to_all(parts, 'table', split_axis=0, concat_axis=0, tiled=True)]
  transfers between devices with their start and end apart: 7 -> 6, of which waited for: 5 -> 4; matrix products, arithmetic and copies ran while one was open for 0% -> 0% of each run, Pallas kernels for 2% -> 2%
where the time goes in v7:
time: 236 us; the launch traced here: 235 us
  blocking collectives  134 us (57%)
  waiting for transfers between devices  48.2 us (20%)
  starting transfers between devices  32.8 us (14%)
  Pallas kernels  15.4 us (7%)
    all_to_all x2, blocking collectives, over_table(): lax.all_to_all(parts, 'table', split_axis=0, concat_axis=0, tiled=True)  83.5 us
    all_to_all x2, blocking collectives, over_y(): lax.all_to_all(x, 'dp', split_axis=0, concat_axis=0, axis_index_groups=al...  50.9 us
    all_to_all x1, waiting for transfers between devices, over_table(): lax.all_to_all(parts, 'table', split_axis=0, concat_axis=0, tiled=True)  41.1 us
    all_to_all x1, starting transfers between devices, on_device(): lax.all_to_all(jnp.broadcast_to(table.astype(bf16)[None], (chips // 2, pe...  7.64 us
    ppermute x1, starting transfers between devices, on_device(): far = lax.ppermute(near, 'dp', swap)  6.79 us
    ppermute x1, starting transfers between devices, on_device(): far_rows = lax.ppermute(jnp.concatenate([near_rows, next_rows]), 'dp', swap)  6.29 us
    all_to_all x1, waiting for transfers between devices, on_device(): lax.all_to_all(jnp.broadcast_to(table.astype(bf16)[None], (chips // 2, pe...  5.73 us
    ppermute x1, starting transfers between devices, on_device(): other = lax.ppermute(column(1, bf16), 'dp', swap)  5.52 us
  transfers between devices with their start and end apart: 6, of which 4 were waited for; matrix products, arithmetic and copies ran while one was open for 0% of the time, Pallas kernels for 2%

profile of v7, /device:TPU:1, one launch (start us, length us, event | category | flops | bytes accessed | tf_op | source)
XLA Modules:
  0.0 235.3 jit_solution(17396525023133922553)
XLA Ops:
  0.6 0.9 convert_element_type.7
  1.5 0.7 broadcast_in_dim.12
  2.3 7.6 %all-to-all-start.2 = ((bf16[4,128,256]{2,1,0:T(8,128)(2,1)}), bf16[4,128,256]{2,1,0:T(8,128)(2,1)S(1)}, u32[]{:S(2)}, u32[]{:S(2)}) async-start(bf16[4,128,256]{2,1,0:T(8,128)(2,1)} %broadcast_in_dim.12), calls=%async_computation.2 | async-start | bytes 524288 | tf_op jit(solution)/shard_map/all_to_all | solution.py:403
  9.9 0.7 copy-done.4
  10.6 2.2 shard_map.103
  12.8 5.7 %all-to-all-done.2.near_ref = bf16[4,128,256]{2,1,0:T(8,128)(2,1)S(1)} async-done(((bf16[4,128,256]{2,1,0:T(8,128)(2,1)}), bf16[4,128,256]{2,1,0:T(8,128)(2,1)S(1)}, u32[]{:S(2)}, u32[]{:S(2)}) %all-to-all-start.2) | async-done | bytes 262176 | tf_op jit(solution)/shard_map/all_to_all | solution.py:403
  18.5 1.9 collective-permute-start
  20.5 35.0 %all_to_all.40 = s32[64,1,40]{2,1,0:T(1,128)S(1)} all-to-all(s32[64,1,40]{2,1,0:T(1,128)S(1)} %bitcast.36), channel_id=1, replica_groups=mesh['dp'=16,'table'=64] {'table'}, dimensions={0} | all-to-all | bytes 20480 | tf_op jit(solution)/shard_map/all_to_all | solution.py:401
  55.5 6.3 %collective-permute-start.1 = (bf16[8,128,256]{2,1,0:T(8,128)(2,1)S(1)}, bf16[8,128,256]{2,1,0:T(8,128)(2,1)S(1)}, u32[]{:S(2)}, u32[]{:S(2)}) collective-permute-start(bf16[8,128,256]{2,1,0:T(8,128)(2,1)S(1)} %pad_maximum_fusion), channel_id=1, source_target_pairs={{0,64},{64,0},{128,192},{192,128},{256,320},{320,256},{384,448},{4... | collective-permute-start | bytes 1572872 | tf_op jit(solution)/shard_map/ppermute | solution.py:426
  61.8 0.1 slice.13
  61.9 0.1 reshape.79.pos_ref
  62.0 0.1 reshape.80.more_pos_ref
  62.2 1.5 shard_map.104
  63.7 0.1 reshape.81.codes_ref
  63.8 0.1 reshape.82.more_codes_ref
  64.5 1.9 shard_map.105
  66.5 4.6 %all-to-all-start.4 = ((bf16[64,24,256]{2,1,0:T(8,128)(2,1)}), bf16[64,24,256]{2,1,0:T(8,128)(2,1)S(1)}, u32[]{:S(2)}, u32[]{:S(2)}) async-start(bf16[64,24,256]{2,1,0:T(8,128)(2,1)} %bitcast.21), calls=%async_computation.4 | async-start | bytes 1572864 | tf_op jit(solution)/shard_map/all_to_all | solution.py:401
  71.1 41.1 %all-to-all-done.4 = bf16[64,24,256]{2,1,0:T(8,128)(2,1)S(1)} async-done(((bf16[64,24,256]{2,1,0:T(8,128)(2,1)}), bf16[64,24,256]{2,1,0:T(8,128)(2,1)S(1)}, u32[]{:S(2)}, u32[]{:S(2)}) %all-to-all-start.4) | async-done | bytes 786464 | tf_op jit(solution)/shard_map/all_to_all | solution.py:401
  112.2 1.3 shard_map.106
  113.5 30.4 %all_to_all.41.near = bf16[8,256,256]{2,1,0:T(8,128)(2,1)S(1)} all-to-all(bf16[8,256,256]{2,1,0:T(8,128)(2,1)S(1)} %get-tuple-element.79), channel_id=1, replica_groups={{0,128,256,384,512,640,768,896},{64,192,320,448,576,704,832,960},{1,129..., dimensions={0} | all-to-all | bytes 2097152 | tf_op jit(solution)/shard_map/all_to_all | solution.py:395
  143.9 6.8 %collective-permute-start.2 = (bf16[8,256,256]{2,1,0:T(8,128)(2,1)S(1)}, bf16[8,256,256]{2,1,0:T(8,128)(2,1)S(1)}, u32[]{:S(2)}, u32[]{:S(2)}) collective-permute-start(bf16[8,256,256]{2,1,0:T(8,128)(2,1)S(1)} %all_to_all.41.near), channel_id=1, source_target_pairs={{0,64},{64,0},{128,192},{192,128},{256,320},{320,256},{384,448},{4... | collective-permute-start | bytes 3145736 | tf_op jit(solution)/shard_map/ppermute | solution.py:490
  150.7 0.9 shard_map.107
  151.6 1.2 collective-permute-done.2.far
  152.8 4.2 %shard_map.108 = (f32[1,128]{1,0:T(1,128)}, bf16[1536,256]{1,0:T(8,128)(2,1)S(1)}, bf16[512,256]{1,0:T(8,128)(2,1)S(1)}) custom-call(s32[1]{0:T(128)} %bitcast.4.y_ref, bf16[8,256,256]{2,1,0:T(8,128)(2,1)S(1)} %all_to_all.41.near, bf16[8,256,256]{2,1,0:T(8,128)(2,1)S(1)} %collective-permute-done.2.far, f32[8,1,128]{2,1,0:T(1,128)S(1)} %get-tuple-element.83.near_sums, ...), custom_call_target="tpu_custom_call" | custom-call | tf_op jit(solution)/shard_map/pallas_call | solution.py:502
  157.0 48.6 %all_to_all.42 = bf16[64,24,256]{2,1,0:T(8,128)(2,1)S(1)} all-to-all(bf16[64,24,256]{2,1,0:T(8,128)(2,1)S(1)} %bitcast.34), channel_id=1, replica_groups=mesh['dp'=16,'table'=64] {'table'}, dimensions={0} | all-to-all | bytes 1572864 | tf_op jit(solution)/shard_map/all_to_all | solution.py:401
  205.5 1.2 shard_map.110
  206.8 5.5 %collective-permute-start.3 = (bf16[8,128,256]{2,1,0:T(8,128)(2,1)S(1)}, bf16[8,128,256]{2,1,0:T(8,128)(2,1)S(1)}, u32[]{:S(2)}, u32[]{:S(2)}) collective-permute-start(bf16[8,128,256]{2,1,0:T(8,128)(2,1)S(1)} %shard_map.110), channel_id=1, source_target_pairs={{0,64},{64,0},{128,192},{192,128},{256,320},{320,256},{384,448},{4... | collective-permute-start | bytes 1572872 | tf_op jit(solution)/shard_map/ppermute | solution.py:522
  212.3 1.3 shard_map.109.a_ref
  213.6 0.2 collective-permute-done.3.b_ref
  213.8 0.1 shard_map.111
  213.9 20.5 %all_to_all.43.parts_ref = bf16[8,128,256]{2,1,0:T(8,128)(2,1)S(1)} all-to-all(bf16[8,128,256]{2,1,0:T(8,128)(2,1)S(1)} %shard_map.111), channel_id=1, replica_groups={{0,128,256,384,512,640,768,896},{64,192,320,448,576,704,832,960},{1,129..., dimensions={0} | all-to-all | bytes 1048576 | tf_op jit(solution)/shard_map/all_to_all | solution.py:395
  234.5 0.9 shard_map.112
  (24 shorter events, 0.3 us)
Async XLA Ops:
  2.3 16.3 %all-to-all-start.2 = ((bf16[4,128,256]{2,1,0:T(8,128)(2,1)}), bf16[4,128,256]{2,1,0:T(8,128)(2,1)S(1)}, u32[]{:S(2)}, u32[]{:S(2)}) async-start(bf16[4,128,256]{2,1,0:T(8,128)(2,1)} %broadcast_in_dim.12), calls=%async_computation.2 | async-start | bytes 524288 | tf_op jit(solution)/shard_map/all_to_all | solution.py:403
  9.9 0.7 copy-start.4
  9.9 0.7 copy-start.3
  9.9 0.7 copy-start.2
  9.9 0.7 copy-start.1
  9.9 0.7 copy-start.5
  18.5 36.9 %collective-permute-start = (bf16[4,128,256]{2,1,0:T(8,128)(2,1)S(1)}, bf16[4,128,256]{2,1,0:T(8,128)(2,1)S(1)}, u32[]{:S(2)}, u32[]{:S(2)}) collective-permute-start(bf16[4,128,256]{2,1,0:T(8,128)(2,1)S(1)} %all-to-all-done.2.near_ref), channel_id=1, source_target_pairs={{0,896},{64,192},{128,0},{192,320},{256,128},{320,448},{384,256},{... | collective-permute-start | bytes 786440 | tf_op jit(solution)/shard_map/ppermute | solution.py:423
  55.4 6.6 %copy-start.7 = (bf16[256,256]{1,0:T(8,128)(2,1)S(1)}, bf16[256,256]{1,0:T(8,128)(2,1)}, u32[]{:S(2)}) copy-start(bf16[256,256]{1,0:T(8,128)(2,1)} %param.14) | copy-start | bytes 393220
  55.5 6.6 %copy-start.6 = (bf16[256,256]{1,0:T(8,128)(2,1)S(1)}, bf16[256,256]{1,0:T(8,128)(2,1)}, u32[]{:S(2)}) copy-start(bf16[256,256]{1,0:T(8,128)(2,1)} %param.15) | copy-start | bytes 393220
  55.5 9.0 %collective-permute-start.1 = (bf16[8,128,256]{2,1,0:T(8,128)(2,1)S(1)}, bf16[8,128,256]{2,1,0:T(8,128)(2,1)S(1)}, u32[]{:S(2)}, u32[]{:S(2)}) collective-permute-start(bf16[8,128,256]{2,1,0:T(8,128)(2,1)S(1)} %pad_maximum_fusion), channel_id=1, source_target_pairs={{0,64},{64,0},{128,192},{192,128},{256,320},{320,256},{384,448},{4... | collective-permute-start | bytes 1572872 | tf_op jit(solution)/shard_map/ppermute | solution.py:426
  66.5 45.7 %all-to-all-start.4 = ((bf16[64,24,256]{2,1,0:T(8,128)(2,1)}), bf16[64,24,256]{2,1,0:T(8,128)(2,1)S(1)}, u32[]{:S(2)}, u32[]{:S(2)}) async-start(bf16[64,24,256]{2,1,0:T(8,128)(2,1)} %bitcast.21), calls=%async_computation.4 | async-start | bytes 1572864 | tf_op jit(solution)/shard_map/all_to_all | solution.py:401
  143.9 8.9 %collective-permute-start.2 = (bf16[8,256,256]{2,1,0:T(8,128)(2,1)S(1)}, bf16[8,256,256]{2,1,0:T(8,128)(2,1)S(1)}, u32[]{:S(2)}, u32[]{:S(2)}) collective-permute-start(bf16[8,256,256]{2,1,0:T(8,128)(2,1)S(1)} %all_to_all.41.near), channel_id=1, source_target_pairs={{0,64},{64,0},{128,192},{192,128},{256,320},{320,256},{384,448},{4... | collective-permute-start | bytes 3145736 | tf_op jit(solution)/shard_map/ppermute | solution.py:490
  206.8 7.0 %collective-permute-start.3 = (bf16[8,128,256]{2,1,0:T(8,128)(2,1)S(1)}, bf16[8,128,256]{2,1,0:T(8,128)(2,1)S(1)}, u32[]{:S(2)}, u32[]{:S(2)}) collective-permute-start(bf16[8,128,256]{2,1,0:T(8,128)(2,1)S(1)} %shard_map.110), channel_id=1, source_target_pairs={{0,64},{64,0},{128,192},{192,128},{256,320},{320,256},{384,448},{4... | collective-permute-start | bytes 1572872 | tf_op jit(solution)/shard_map/ppermute | solution.py:522
  213.9 20.5 %copy-start = (f32[128,256]{1,0:T(8,128)S(1)}, f32[128,256]{1,0:T(8,128)}, u32[]{:S(2)}) copy-start(f32[128,256]{1,0:T(8,128)} %table_ref.1) | copy-start | bytes 393220

commit v8 on v7

--- a/solution.py
+++ b/solution.py
@@ -442,17 +442,17 @@
         )(turned, far_rows, near_got)
 
     near_got, turned, over = pick_near(0, base, received)
-    near_got, crowded, base_pos, more_pos, codes, more_codes, tower_weights = lax.optimization_barrier(
+    near_got, codes, more_codes = lax.optimization_barrier(
         (
             near_got,
-            over[0] > 0,
-            places[:, :base].reshape(1, -1),
-            places[:, base:].reshape(1, -1),
             received[:, :base].reshape(1, -1),
             received[:, base:slots].reshape(1, -1),
-            jnp.stack([item_weight, query_weight]),
         )
     )
+    crowded = over[0] > 0
+    base_pos = places[:, :base].reshape(1, -1)
+    more_pos = places[:, base:].reshape(1, -1)
+    tower_weights = jnp.stack([item_weight, query_weight])
     fetched = over_table(pick_far(0, base, turned, near_got))
     nothing = jnp.zeros((n_table * more, width), bf16)
     late, fetched = lax.optimization_barrier((received, fetched))

time: 236 us -> 235 us (level)
  no operation moved by 1% of the time
where the time goes in v8:
time: 235 us; the launch traced here: 234 us
  blocking collectives  135 us (57%)
  waiting for transfers between devices  46.8 us (20%)
  starting transfers between devices  32.3 us (14%)
  Pallas kernels  15.4 us (7%)
  local copies, waits for them, and re-layouts  2.62 us (1%)
    all_to_all x2, blocking collectives, over_table(): lax.all_to_all(parts, 'table', split_axis=0, concat_axis=0, tiled=True)  83.3 us
    all_to_all x2, blocking collectives, over_y(): lax.all_to_all(x, 'dp', split_axis=0, concat_axis=0, axis_index_groups=al...  51.4 us
    all_to_all x1, waiting for transfers between devices, over_table(): lax.all_to_all(parts, 'table', split_axis=0, concat_axis=0, tiled=True)  39.6 us
    all_to_all x1, starting transfers between devices, on_device(): lax.all_to_all(jnp.broadcast_to(table.astype(bf16)[None], (chips // 2, pe...  7.64 us
    ppermute x1, starting transfers between devices, on_device(): far = lax.ppermute(near, 'dp', swap)  6.28 us
    ppermute x1, starting transfers between devices, on_device(): far_rows = lax.ppermute(jnp.concatenate([near_rows, next_rows]), 'dp', swap)  6.16 us
    all_to_all x1, waiting for transfers between devices, on_device(): lax.all_to_all(jnp.broadcast_to(table.astype(bf16)[None], (chips // 2, pe...  5.73 us
    ppermute x1, starting transfers between devices, on_device(): other = lax.ppermute(column(1, bf16), 'dp', swap)  5.52 us
  transfers between devices with their start and end apart: 6, of which 4 were waited for; matrix products, arithmetic and copies ran while one was open for 0% of the time, Pallas kernels for 2%

profile of v8, /device:TPU:1, one launch (start us, length us, event | category | flops | bytes accessed | tf_op | source)
XLA Modules:
  0.0 234.3 jit_solution(16207263014882671702)
XLA Ops:
  0.6 0.9 convert_element_type.10
  1.5 0.7 broadcast_in_dim.12
  2.3 7.6 %all-to-all-start.2 = ((bf16[4,128,256]{2,1,0:T(8,128)(2,1)}), bf16[4,128,256]{2,1,0:T(8,128)(2,1)S(1)}, u32[]{:S(2)}, u32[]{:S(2)}) async-start(bf16[4,128,256]{2,1,0:T(8,128)(2,1)} %broadcast_in_dim.12), calls=%async_computation.2 | async-start | bytes 524288 | tf_op jit(solution)/shard_map/all_to_all | solution.py:403
  9.9 0.7 copy-done.4
  10.6 2.2 shard_map.103
  12.8 5.7 %all-to-all-done.2.near_ref = bf16[4,128,256]{2,1,0:T(8,128)(2,1)S(1)} async-done(((bf16[4,128,256]{2,1,0:T(8,128)(2,1)}), bf16[4,128,256]{2,1,0:T(8,128)(2,1)S(1)}, u32[]{:S(2)}, u32[]{:S(2)}) %all-to-all-start.2) | async-done | bytes 262176 | tf_op jit(solution)/shard_map/all_to_all | solution.py:403
  18.5 1.9 collective-permute-start
  20.5 35.0 %all_to_all.40 = s32[64,1,40]{2,1,0:T(1,128)S(1)} all-to-all(s32[64,1,40]{2,1,0:T(1,128)S(1)} %bitcast.36), channel_id=1, replica_groups=mesh['dp'=16,'table'=64] {'table'}, dimensions={0} | all-to-all | bytes 20480 | tf_op jit(solution)/shard_map/all_to_all | solution.py:401
  55.5 6.2 %collective-permute-start.1 = (bf16[8,128,256]{2,1,0:T(8,128)(2,1)S(1)}, bf16[8,128,256]{2,1,0:T(8,128)(2,1)S(1)}, u32[]{:S(2)}, u32[]{:S(2)}) collective-permute-start(bf16[8,128,256]{2,1,0:T(8,128)(2,1)S(1)} %pad_maximum_fusion), channel_id=1, source_target_pairs={{0,64},{64,0},{128,192},{192,128},{256,320},{320,256},{384,448},{4... | collective-permute-start | bytes 1572872 | tf_op jit(solution)/shard_map/ppermute | solution.py:426
  61.7 1.5 shard_map.104
  63.2 0.1 reshape.81.codes_ref
  63.3 0.1 reshape.82.more_codes_ref
  63.4 1.9 shard_map.105
  65.3 4.8 %all-to-all-start.4 = ((bf16[64,24,256]{2,1,0:T(8,128)(2,1)}), bf16[64,24,256]{2,1,0:T(8,128)(2,1)S(1)}, u32[]{:S(2)}, u32[]{:S(2)}) async-start(bf16[64,24,256]{2,1,0:T(8,128)(2,1)} %bitcast.18), calls=%async_computation.4 | async-start | bytes 1572864 | tf_op jit(solution)/shard_map/all_to_all | solution.py:401
  70.2 0.1 reshape.83.pos_ref
  70.3 0.1 reshape.84.more_pos_ref
  70.4 0.6 copy-done.6
  71.7 39.6 %all-to-all-done.4 = bf16[64,24,256]{2,1,0:T(8,128)(2,1)S(1)} async-done(((bf16[64,24,256]{2,1,0:T(8,128)(2,1)}), bf16[64,24,256]{2,1,0:T(8,128)(2,1)S(1)}, u32[]{:S(2)}, u32[]{:S(2)}) %all-to-all-start.4) | async-done | bytes 786464 | tf_op jit(solution)/shard_map/all_to_all | solution.py:401
  111.4 1.3 shard_map.106
  112.6 30.9 %all_to_all.41.near = bf16[8,256,256]{2,1,0:T(8,128)(2,1)S(1)} all-to-all(bf16[8,256,256]{2,1,0:T(8,128)(2,1)S(1)} %get-tuple-element.71), channel_id=1, replica_groups={{0,128,256,384,512,640,768,896},{64,192,320,448,576,704,832,960},{1,129..., dimensions={0} | all-to-all | bytes 2097152 | tf_op jit(solution)/shard_map/all_to_all | solution.py:395
  143.5 6.3 %collective-permute-start.2 = (bf16[8,256,256]{2,1,0:T(8,128)(2,1)S(1)}, bf16[8,256,256]{2,1,0:T(8,128)(2,1)S(1)}, u32[]{:S(2)}, u32[]{:S(2)}) collective-permute-start(bf16[8,256,256]{2,1,0:T(8,128)(2,1)S(1)} %all_to_all.41.near), channel_id=1, source_target_pairs={{0,64},{64,0},{128,192},{192,128},{256,320},{320,256},{384,448},{4... | collective-permute-start | bytes 3145736 | tf_op jit(solution)/shard_map/ppermute | solution.py:490
  149.8 0.9 shard_map.107
  150.8 1.2 collective-permute-done.2.far
  151.9 4.2 %shard_map.108 = (f32[1,128]{1,0:T(1,128)}, bf16[1536,256]{1,0:T(8,128)(2,1)S(1)}, bf16[512,256]{1,0:T(8,128)(2,1)S(1)}) custom-call(s32[1]{0:T(128)} %bitcast.4.y_ref, bf16[8,256,256]{2,1,0:T(8,128)(2,1)S(1)} %all_to_all.41.near, bf16[8,256,256]{2,1,0:T(8,128)(2,1)S(1)} %collective-permute-done.2.far, f32[8,1,128]{2,1,0:T(1,128)S(1)} %get-tuple-element.75.near_sums, ...), custom_call_target="tpu_custom_call" | custom-call | tf_op jit(solution)/shard_map/pallas_call | solution.py:502
  156.1 48.4 %all_to_all.42 = bf16[64,24,256]{2,1,0:T(8,128)(2,1)S(1)} all-to-all(bf16[64,24,256]{2,1,0:T(8,128)(2,1)S(1)} %bitcast.34), channel_id=1, replica_groups=mesh['dp'=16,'table'=64] {'table'}, dimensions={0} | all-to-all | bytes 1572864 | tf_op jit(solution)/shard_map/all_to_all | solution.py:401
  204.5 1.2 shard_map.110
  205.8 5.5 %collective-permute-start.3 = (bf16[8,128,256]{2,1,0:T(8,128)(2,1)S(1)}, bf16[8,128,256]{2,1,0:T(8,128)(2,1)S(1)}, u32[]{:S(2)}, u32[]{:S(2)}) collective-permute-start(bf16[8,128,256]{2,1,0:T(8,128)(2,1)S(1)} %shard_map.110), channel_id=1, source_target_pairs={{0,64},{64,0},{128,192},{192,128},{256,320},{320,256},{384,448},{4... | collective-permute-start | bytes 1572872 | tf_op jit(solution)/shard_map/ppermute | solution.py:522
  211.3 1.3 shard_map.109.a_ref
  212.6 0.2 collective-permute-done.3.b_ref
  212.8 0.1 shard_map.111
  212.9 20.5 %all_to_all.43.parts_ref = bf16[8,128,256]{2,1,0:T(8,128)(2,1)S(1)} all-to-all(bf16[8,128,256]{2,1,0:T(8,128)(2,1)S(1)} %shard_map.111), channel_id=1, replica_groups={{0,128,256,384,512,640,768,896},{64,192,320,448,576,704,832,960},{1,129..., dimensions={0} | all-to-all | bytes 1048576 | tf_op jit(solution)/shard_map/all_to_all | solution.py:395
  233.4 0.9 shard_map.112
  (24 shorter events, 0.4 us)
Async XLA Ops:
  2.3 16.3 %all-to-all-start.2 = ((bf16[4,128,256]{2,1,0:T(8,128)(2,1)}), bf16[4,128,256]{2,1,0:T(8,128)(2,1)S(1)}, u32[]{:S(2)}, u32[]{:S(2)}) async-start(bf16[4,128,256]{2,1,0:T(8,128)(2,1)} %broadcast_in_dim.12), calls=%async_computation.2 | async-start | bytes 524288 | tf_op jit(solution)/shard_map/all_to_all | solution.py:403
  9.9 0.7 copy-start.4
  9.9 0.7 copy-start.3
  9.9 0.7 copy-start.2
  9.9 0.7 copy-start.1
  9.9 0.7 copy-start.5
  18.5 36.9 %collective-permute-start = (bf16[4,128,256]{2,1,0:T(8,128)(2,1)S(1)}, bf16[4,128,256]{2,1,0:T(8,128)(2,1)S(1)}, u32[]{:S(2)}, u32[]{:S(2)}) collective-permute-start(bf16[4,128,256]{2,1,0:T(8,128)(2,1)S(1)} %all-to-all-done.2.near_ref), channel_id=1, source_target_pairs={{0,896},{64,192},{128,0},{192,320},{256,128},{320,448},{384,256},{... | collective-permute-start | bytes 786440 | tf_op jit(solution)/shard_map/ppermute | solution.py:423
  55.5 7.9 %collective-permute-start.1 = (bf16[8,128,256]{2,1,0:T(8,128)(2,1)S(1)}, bf16[8,128,256]{2,1,0:T(8,128)(2,1)S(1)}, u32[]{:S(2)}, u32[]{:S(2)}) collective-permute-start(bf16[8,128,256]{2,1,0:T(8,128)(2,1)S(1)} %pad_maximum_fusion), channel_id=1, source_target_pairs={{0,64},{64,0},{128,192},{192,128},{256,320},{320,256},{384,448},{4... | collective-permute-start | bytes 1572872 | tf_op jit(solution)/shard_map/ppermute | solution.py:426
  65.3 5.1 %copy-start.7 = (bf16[256,256]{1,0:T(8,128)(2,1)S(1)}, bf16[256,256]{1,0:T(8,128)(2,1)}, u32[]{:S(2)}) copy-start(bf16[256,256]{1,0:T(8,128)(2,1)} %param.14) | copy-start | bytes 393220
  65.3 46.0 %all-to-all-start.4 = ((bf16[64,24,256]{2,1,0:T(8,128)(2,1)}), bf16[64,24,256]{2,1,0:T(8,128)(2,1)S(1)}, u32[]{:S(2)}, u32[]{:S(2)}) async-start(bf16[64,24,256]{2,1,0:T(8,128)(2,1)} %bitcast.18), calls=%async_computation.4 | async-start | bytes 1572864 | tf_op jit(solution)/shard_map/all_to_all | solution.py:401
  70.1 0.9 copy-start.6
  143.5 8.4 %collective-permute-start.2 = (bf16[8,256,256]{2,1,0:T(8,128)(2,1)S(1)}, bf16[8,256,256]{2,1,0:T(8,128)(2,1)S(1)}, u32[]{:S(2)}, u32[]{:S(2)}) collective-permute-start(bf16[8,256,256]{2,1,0:T(8,128)(2,1)S(1)} %all_to_all.41.near), channel_id=1, source_target_pairs={{0,64},{64,0},{128,192},{192,128},{256,320},{320,256},{384,448},{4... | collective-permute-start | bytes 3145736 | tf_op jit(solution)/shard_map/ppermute | solution.py:490
  205.8 7.0 %collective-permute-start.3 = (bf16[8,128,256]{2,1,0:T(8,128)(2,1)S(1)}, bf16[8,128,256]{2,1,0:T(8,128)(2,1)S(1)}, u32[]{:S(2)}, u32[]{:S(2)}) collective-permute-start(bf16[8,128,256]{2,1,0:T(8,128)(2,1)S(1)} %shard_map.110), channel_id=1, source_target_pairs={{0,64},{64,0},{128,192},{192,128},{256,320},{320,256},{384,448},{4... | collective-permute-start | bytes 1572872 | tf_op jit(solution)/shard_map/ppermute | solution.py:522
  212.9 20.5 %copy-start = (f32[128,256]{1,0:T(8,128)S(1)}, f32[128,256]{1,0:T(8,128)}, u32[]{:S(2)}) copy-start(f32[128,256]{1,0:T(8,128)} %table_ref.1) | copy-start | bytes 393220
